TPU v7x, 512 devices: a whole 4x8x8 slice. The times are simulated.
512 devices in a mesh: dp: 32 (over y, z_hi), mp: 16 (over z_lo, x, core).
Axes of the slice: x: 4, y: 8, z: 8 (z_hi: 4, z_lo: 2; z = z_hi * 2 + z_lo), core: 2. Of those that a mesh axis runs over, the one named last changes fastest.
Arguments:
- image_emb: bfloat16 [16384, 1152], P('dp'), may hold values from -6 to 6
- text_emb: bfloat16 [16384, 1152], P(('dp', 'mp')), may hold values from -6 to 6
- image_feat: bfloat16 [16384, 1152], P('dp'), may hold values from -6 to 6
- text_feat: bfloat16 [16384, 1152], P('dp'), may hold values from -6 to 6
- logit_scale: float32 [1], replicated, may hold values from 4 to 16
- logit_bias: float32 [1], replicated, may hold values from -8 to -2
Outputs:
- image_proj_grad: float32 [1152, 1152], P('dp', 'mp')
- text_proj_grad: float32 [1152, 1152], P('dp', 'mp')
All inputs are finite; a program needn't handle non-finite values.
Results may differ from a plain program's by a relative error of at most 0.0055.
Values may be sent and summed in bfloat16 or wider, within the bound.
No kernel may reach another device: no remote copies, remote signals or barrier semaphores. Data moves between devices by JAX's collectives and lax.ppermute only.
A program may use at most 64 MiB of HBM per device.

v0:
```python
import jax
import jax.numpy as jnp
from jax import lax
from jax.sharding import PartitionSpec as P


def shifted(value, axis, steps):
    count = lax.axis_size(axis)
    pairs = [(source, (source + steps) % count) for source in range(count)]
    return lax.ppermute(value, axis, pairs)


def normalize(rows):
    wide = rows.astype(jnp.float32)
    factor = lax.rsqrt(jnp.sum(wide * wide, axis=-1, keepdims=True) + 1e-06)
    return (wide * factor, factor)


def unit_back(direction, unit, factor):
    return (direction - unit * jnp.sum(unit * direction, axis=-1, keepdims=True)) * factor


def run_cycle(step_fn, moved, state, cycle_size):
    state = step_fn(0, state)
    state = step_fn(1, moved(state))

    def one_turn(turn, state):
        state = step_fn(2 + 2 * turn, moved(state))
        return step_fn(3 + 2 * turn, moved(state))

    return lax.fori_loop(0, (cycle_size - 2) // 2, one_turn, state)


def local(image_emb, text_emb, image_feat, text_feat, logit_scale, logit_bias):
    cycle_size = lax.axis_size("dp")
    here = lax.axis_index("dp")
    column = lax.axis_index("mp")
    image_unit, image_norm = normalize(image_emb)
    text_unit, text_norm = normalize(text_emb)
    image_low = image_unit.astype(jnp.bfloat16)
    text_low = text_unit.astype(jnp.bfloat16)
    own_rows = text_low.shape[0]
    block = image_low.shape[0]
    width = image_low.shape[1]
    scale = logit_scale[0]
    offset = logit_bias[0]
    row_ids = column * own_rows + jnp.arange(own_rows, dtype=jnp.int32)[:, None]
    match = row_ids == jnp.arange(block, dtype=jnp.int32)[None, :]

    def tile_weights(text_block, anchor):
        logits = lax.dot_general(
            text_block, image_low, (((1,), (1,)), ((), ())), preferred_element_type=jnp.float32
        )
        sign = jnp.where(match & (anchor == here), 1.0, -1.0).astype(jnp.float32)
        value = scale * logits + offset
        return (-scale * sign * jax.nn.sigmoid(-sign * value)).astype(jnp.bfloat16)

    def advance(text_block):
        return shifted(text_block, "dp", 1)

    def record(step, text_block, tiles, seen):
        anchor = (here - step) % cycle_size
        weights = tile_weights(text_block, anchor)
        tiles = lax.dynamic_update_index_in_dim(tiles, weights, step, 0)
        seen = lax.dynamic_update_index_in_dim(seen, text_block, step, 0)
        return (anchor, weights, tiles, seen)

    tiles_start = jnp.zeros((cycle_size, own_rows, block), jnp.bfloat16)
    seen_start = jnp.zeros((cycle_size, own_rows, width), jnp.bfloat16)

    def carry_partial(partial_value):
        return shifted(partial_value, "dp", 1)

    def step_travel(step, state):
        text_block, partial_value, tiles, seen = state
        anchor, weights, tiles, seen = record(step, text_block, tiles, seen)
        partial_value = partial_value + jnp.dot(
            weights, image_low, preferred_element_type=jnp.float32
        )
        return (text_block, partial_value, tiles, seen)

    def moved_travel(state):
        text_block, partial_value, tiles, seen = state
        return (advance(text_block), carry_partial(partial_value), tiles, seen)

    start_state = (text_low, jnp.zeros((own_rows, width), jnp.float32), tiles_start, seen_start)
    final_state = run_cycle(step_travel, moved_travel, start_state, cycle_size)
    text_dir = carry_partial(final_state[1])
    tiles = final_state[2]
    seen = final_state[3]
    all_tiles = tiles.reshape(cycle_size * own_rows, block)
    all_seen = seen.reshape(cycle_size * own_rows, width)
    image_dir = lax.dot_general(
        all_tiles, all_seen, (((0,), (0,)), ((), ())), preferred_element_type=jnp.float32
    )
    image_part = unit_back(image_dir, image_unit, image_norm)
    image_grad = lax.psum_scatter(image_part, "mp", scatter_dimension=1, tiled=True).astype(
        jnp.bfloat16
    )
    text_grad = unit_back(text_dir, text_unit, text_norm).astype(jnp.bfloat16)
    text_cols = lax.all_to_all(text_grad, "mp", split_axis=1, concat_axis=0, tiled=True)
    image_term = lax.dot_general(
        image_feat, image_grad, (((0,), (0,)), ((), ())), preferred_element_type=jnp.float32
    )
    text_term = lax.dot_general(
        text_feat, text_cols, (((0,), (0,)), ((), ())), preferred_element_type=jnp.float32
    )
    image_proj_grad, text_proj_grad = (
        lax.psum_scatter(image_term, "dp", scatter_dimension=0, tiled=True),
        lax.psum_scatter(text_term, "dp", scatter_dimension=0, tiled=True),
    )
    return (image_proj_grad, text_proj_grad)


def solution(mesh):
    in_specs = (P("dp", None), P(("dp", "mp"), None), P("dp", None), P("dp", None), P(), P())
    out_specs = (P("dp", "mp"), P("dp", "mp"))
    return jax.shard_map(local, mesh=mesh, in_specs=in_specs, out_specs=out_specs, check_vma=False)
```

profile of v0, /device:TPU:6, one launch (start us, length us, event | category | flops | bytes accessed | tf_op | source)
XLA Modules:
  0.0 933.5 jit_solution(409287212543131855)
XLA Ops:
  10.0 6.1 collective-permute-start.4
  22.3 7.3 collective-permute-start.5
  41.2 488.6 %while.22 = (s32[]{:T(128)}, bf16[32,1152]{1,0:T(8,128)(2,1)}, f32[32,1152]{1,0:T(8,128)}, bf16[32,32,512]{2,1,0:T(8,128)(2,1)}, bf16[32,32,1152]{2,1,0:T(8,128)...) while((s32[]{:T(128)}, bf16[32,1152]{1,0:T(8,128)(2,1)}, ...), condition=%wide.region_3.4_spmd.clone, body=%wide.region_2.3_spmd.clone.sunk | while | flops 151494672 | bytes 8015819 | solution.py:31
  43.1 5.5 collective-permute-start.2
  48.6 6.4 collective-permute-done
  78.9 7.1 collective-permute-done
  110.1 7.9 collective-permute-done
  142.6 7.6 collective-permute-done
  166.1 6.0 collective-permute-done.3
  176.7 8.0 collective-permute-done
  210.2 8.8 collective-permute-done
  242.9 8.7 collective-permute-done
  276.7 7.3 collective-permute-done
  309.7 8.0 collective-permute-done
  342.8 7.4 collective-permute-done
  374.0 7.6 collective-permute-done
  405.3 6.9 collective-permute-done
  437.7 7.4 collective-permute-done
  471.8 7.4 collective-permute-done
  503.0 6.9 collective-permute-done
  541.4 9.4 %collective-permute-done.6 = f32[32,1152]{1,0:T(8,128)S(1)} collective-permute-done((f32[32,1152]{1,0:T(8,128)S(1)}, f32[32,1152]{1,0:T(8,128)S(1)}, u32[]{:S(2)}, u32[]{:S(2)}) %collective-permute-start.6) | collective-permute-done | bytes 147488 | tf_op jit(solution)/shard_map/ppermute | solution.py:10
  551.3 14.2 %all_to_all.19 = bf16[32,16,72]{2,0,1:T(8,128)(2,1)S(1)} all-to-all(bf16[32,16,72]{2,0,1:T(8,128)(2,1)S(1)} %copy.13), channel_id=1, replica_groups=mesh['dp'=32,'mp'=16] {'mp'}, dimensions={1} | all-to-all | bytes 147456 | tf_op jit(solution)/shard_map/all_to_all | solution.py:101
  566.6 39.6 %reduce-scatter.6.cloned.1.call-done = f32[72,512]{1,0:T(8,128)} async-done(((f32[1152,512]{1,0:T(8,128)}), f32[72,512]{1,0:T(8,128)}) %reduce-scatter.6.cloned.1.call-update) | async-done | bytes 147472
  610.2 314.1 %all-reduce.7.cloned.1.call-done = (f32[1152,72]{0,1:T(8,128)}, f32[1152,72]{0,1:T(8,128)}) async-done(((f32[1152,72]{0,1:T(8,128)}, f32[1152,72]{0,1:T(8,128)}), (f32[1152,72]{0,1:T(8,128)}, f32[1152,72]{0,1:T(8,128)})) %all-reduce.7.cloned.1.call-update) | async-done | bytes 663568
  (262 shorter events, 400.5 us)
Async XLA Ops:
  7.2 599.0 %reduce-scatter.6.cloned.1.call-start = ((), (), s32[]{:S(2)}) async-start(), calls=%async_computation.2 | async-start | bytes 2506752
  10.0 22.2 %collective-permute-start.4 = (bf16[32,1152]{1,0:T(8,128)(2,1)}, bf16[32,1152]{1,0:T(8,128)(2,1)}, u32[]{:S(2)}, u32[]{:S(2)}) collective-permute-start(bf16[32,1152]{1,0:T(8,128)(2,1)} %fusion.45), channel_id=1, source_target_pairs={{0,16},{16,32},{32,48},{48,64},{64,80},{80,96},{96,112},{112,128},... | collective-permute-start | bytes 221192 | tf_op jit(solution)/shard_map/ppermute | solution.py:10
  22.3 17.0 %collective-permute-start.5 = (f32[32,1152]{1,0:T(8,128)}, f32[32,1152]{1,0:T(8,128)}, u32[]{:S(2)}, u32[]{:S(2)}) collective-permute-start(f32[32,1152]{1,0:T(8,128)} %fusion.55), channel_id=1, source_target_pairs={{0,16},{16,32},{32,48},{48,64},{64,80},{80,96},{96,112},{112,128},... | collective-permute-start | bytes 442376 | tf_op jit(solution)/shard_map/ppermute | solution.py:10
  41.2 13.9 %collective-permute-start = (bf16[32,1152]{1,0:T(8,128)(2,1)}, bf16[32,1152]{1,0:T(8,128)(2,1)}, u32[]{:S(2)}, u32[]{:S(2)}) collective-permute-start(bf16[32,1152]{1,0:T(8,128)(2,1)} %get-tuple-element.418), channel_id=1, source_target_pairs={{0,16},{16,32},{32,48},{48,64},{64,80},{80,96},{96,112},{112,128},... | collective-permute-start | bytes 221192 | tf_op jit(solution)/shard_map/while/body/eval_jaxpr/ppermute | solution.py:10
  43.1 18.7 %collective-permute-start.2 = (f32[32,1152]{1,0:T(8,128)}, f32[32,1152]{1,0:T(8,128)}, u32[]{:S(2)}, u32[]{:S(2)}) collective-permute-start(f32[32,1152]{1,0:T(8,128)} %get-tuple-element.419), channel_id=1, source_target_pairs={{0,16},{16,32},{32,48},{48,64},{64,80},{80,96},{96,112},{112,128},... | collective-permute-start | bytes 442376 | tf_op jit(solution)/shard_map/while/body/eval_jaxpr/ppermute | solution.py:10
  76.9 15.8 %collective-permute-start.2 = (f32[32,1152]{1,0:T(8,128)}, f32[32,1152]{1,0:T(8,128)}, u32[]{:S(2)}, u32[]{:S(2)}) collective-permute-start(f32[32,1152]{1,0:T(8,128)} %get-tuple-element.419), channel_id=1, source_target_pairs={{0,16},{16,32},{32,48},{48,64},{64,80},{80,96},{96,112},{112,128},... | collective-permute-start | bytes 442376 | tf_op jit(solution)/shard_map/while/body/eval_jaxpr/ppermute | solution.py:10
  108.2 16.6 %collective-permute-start.2 = (f32[32,1152]{1,0:T(8,128)}, f32[32,1152]{1,0:T(8,128)}, u32[]{:S(2)}, u32[]{:S(2)}) collective-permute-start(f32[32,1152]{1,0:T(8,128)} %get-tuple-element.419), channel_id=1, source_target_pairs={{0,16},{16,32},{32,48},{48,64},{64,80},{80,96},{96,112},{112,128},... | collective-permute-start | bytes 442376 | tf_op jit(solution)/shard_map/while/body/eval_jaxpr/ppermute | solution.py:10
  140.7 16.3 %collective-permute-start.2 = (f32[32,1152]{1,0:T(8,128)}, f32[32,1152]{1,0:T(8,128)}, u32[]{:S(2)}, u32[]{:S(2)}) collective-permute-start(f32[32,1152]{1,0:T(8,128)} %get-tuple-element.419), channel_id=1, source_target_pairs={{0,16},{16,32},{32,48},{48,64},{64,80},{80,96},{96,112},{112,128},... | collective-permute-start | bytes 442376 | tf_op jit(solution)/shard_map/while/body/eval_jaxpr/ppermute | solution.py:10
  158.2 14.0 %collective-permute-start.3 = (f32[32,1152]{1,0:T(8,128)S(1)}, f32[32,1152]{1,0:T(8,128)S(1)}, u32[]{:S(2)}, u32[]{:S(2)}) collective-permute-start(f32[32,1152]{1,0:T(8,128)S(1)} %convolution_add_fusion.3), channel_id=1, source_target_pairs={{0,16},{16,32},{32,48},{48,64},{64,80},{80,96},{96,112},{112,128},... | collective-permute-start | bytes 442376 | tf_op jit(solution)/shard_map/while/body/eval_jaxpr/ppermute | solution.py:10
  174.8 16.7 %collective-permute-start.2 = (f32[32,1152]{1,0:T(8,128)}, f32[32,1152]{1,0:T(8,128)}, u32[]{:S(2)}, u32[]{:S(2)}) collective-permute-start(f32[32,1152]{1,0:T(8,128)} %get-tuple-element.419), channel_id=1, source_target_pairs={{0,16},{16,32},{32,48},{48,64},{64,80},{80,96},{96,112},{112,128},... | collective-permute-start | bytes 442376 | tf_op jit(solution)/shard_map/while/body/eval_jaxpr/ppermute | solution.py:10
  208.2 17.5 %collective-permute-start.2 = (f32[32,1152]{1,0:T(8,128)}, f32[32,1152]{1,0:T(8,128)}, u32[]{:S(2)}, u32[]{:S(2)}) collective-permute-start(f32[32,1152]{1,0:T(8,128)} %get-tuple-element.419), channel_id=1, source_target_pairs={{0,16},{16,32},{32,48},{48,64},{64,80},{80,96},{96,112},{112,128},... | collective-permute-start | bytes 442376 | tf_op jit(solution)/shard_map/while/body/eval_jaxpr/ppermute | solution.py:10
  240.9 17.5 %collective-permute-start.2 = (f32[32,1152]{1,0:T(8,128)}, f32[32,1152]{1,0:T(8,128)}, u32[]{:S(2)}, u32[]{:S(2)}) collective-permute-start(f32[32,1152]{1,0:T(8,128)} %get-tuple-element.419), channel_id=1, source_target_pairs={{0,16},{16,32},{32,48},{48,64},{64,80},{80,96},{96,112},{112,128},... | collective-permute-start | bytes 442376 | tf_op jit(solution)/shard_map/while/body/eval_jaxpr/ppermute | solution.py:10
  274.7 16.0 %collective-permute-start.2 = (f32[32,1152]{1,0:T(8,128)}, f32[32,1152]{1,0:T(8,128)}, u32[]{:S(2)}, u32[]{:S(2)}) collective-permute-start(f32[32,1152]{1,0:T(8,128)} %get-tuple-element.419), channel_id=1, source_target_pairs={{0,16},{16,32},{32,48},{48,64},{64,80},{80,96},{96,112},{112,128},... | collective-permute-start | bytes 442376 | tf_op jit(solution)/shard_map/while/body/eval_jaxpr/ppermute | solution.py:10
  291.9 13.3 %collective-permute-start.3 = (f32[32,1152]{1,0:T(8,128)S(1)}, f32[32,1152]{1,0:T(8,128)S(1)}, u32[]{:S(2)}, u32[]{:S(2)}) collective-permute-start(f32[32,1152]{1,0:T(8,128)S(1)} %convolution_add_fusion.3), channel_id=1, source_target_pairs={{0,16},{16,32},{32,48},{48,64},{64,80},{80,96},{96,112},{112,128},... | collective-permute-start | bytes 442376 | tf_op jit(solution)/shard_map/while/body/eval_jaxpr/ppermute | solution.py:10
  307.8 16.7 %collective-permute-start.2 = (f32[32,1152]{1,0:T(8,128)}, f32[32,1152]{1,0:T(8,128)}, u32[]{:S(2)}, u32[]{:S(2)}) collective-permute-start(f32[32,1152]{1,0:T(8,128)} %get-tuple-element.419), channel_id=1, source_target_pairs={{0,16},{16,32},{32,48},{48,64},{64,80},{80,96},{96,112},{112,128},... | collective-permute-start | bytes 442376 | tf_op jit(solution)/shard_map/while/body/eval_jaxpr/ppermute | solution.py:10
  340.8 16.1 %collective-permute-start.2 = (f32[32,1152]{1,0:T(8,128)}, f32[32,1152]{1,0:T(8,128)}, u32[]{:S(2)}, u32[]{:S(2)}) collective-permute-start(f32[32,1152]{1,0:T(8,128)} %get-tuple-element.419), channel_id=1, source_target_pairs={{0,16},{16,32},{32,48},{48,64},{64,80},{80,96},{96,112},{112,128},... | collective-permute-start | bytes 442376 | tf_op jit(solution)/shard_map/while/body/eval_jaxpr/ppermute | solution.py:10
  372.0 16.3 %collective-permute-start.2 = (f32[32,1152]{1,0:T(8,128)}, f32[32,1152]{1,0:T(8,128)}, u32[]{:S(2)}, u32[]{:S(2)}) collective-permute-start(f32[32,1152]{1,0:T(8,128)} %get-tuple-element.419), channel_id=1, source_target_pairs={{0,16},{16,32},{32,48},{48,64},{64,80},{80,96},{96,112},{112,128},... | collective-permute-start | bytes 442376 | tf_op jit(solution)/shard_map/while/body/eval_jaxpr/ppermute | solution.py:10
  403.3 16.7 %collective-permute-start.2 = (f32[32,1152]{1,0:T(8,128)}, f32[32,1152]{1,0:T(8,128)}, u32[]{:S(2)}, u32[]{:S(2)}) collective-permute-start(f32[32,1152]{1,0:T(8,128)} %get-tuple-element.419), channel_id=1, source_target_pairs={{0,16},{16,32},{32,48},{48,64},{64,80},{80,96},{96,112},{112,128},... | collective-permute-start | bytes 442376 | tf_op jit(solution)/shard_map/while/body/eval_jaxpr/ppermute | solution.py:10
  435.8 16.2 %collective-permute-start.2 = (f32[32,1152]{1,0:T(8,128)}, f32[32,1152]{1,0:T(8,128)}, u32[]{:S(2)}, u32[]{:S(2)}) collective-permute-start(f32[32,1152]{1,0:T(8,128)} %get-tuple-element.419), channel_id=1, source_target_pairs={{0,16},{16,32},{32,48},{48,64},{64,80},{80,96},{96,112},{112,128},... | collective-permute-start | bytes 442376 | tf_op jit(solution)/shard_map/while/body/eval_jaxpr/ppermute | solution.py:10
  445.2 13.1 %collective-permute-start.1 = (bf16[32,1152]{1,0:T(8,128)(2,1)}, bf16[32,1152]{1,0:T(8,128)(2,1)}, u32[]{:S(2)}, u32[]{:S(2)}) collective-permute-start(bf16[32,1152]{1,0:T(8,128)(2,1)} %collective-permute-done), channel_id=1, source_target_pairs={{0,16},{16,32},{32,48},{48,64},{64,80},{80,96},{96,112},{112,128},... | collective-permute-start | bytes 221192 | tf_op jit(solution)/shard_map/while/body/eval_jaxpr/ppermute | solution.py:10
  453.1 14.1 %collective-permute-start.3 = (f32[32,1152]{1,0:T(8,128)S(1)}, f32[32,1152]{1,0:T(8,128)S(1)}, u32[]{:S(2)}, u32[]{:S(2)}) collective-permute-start(f32[32,1152]{1,0:T(8,128)S(1)} %convolution_add_fusion.3), channel_id=1, source_target_pairs={{0,16},{16,32},{32,48},{48,64},{64,80},{80,96},{96,112},{112,128},... | collective-permute-start | bytes 442376 | tf_op jit(solution)/shard_map/while/body/eval_jaxpr/ppermute | solution.py:10
  469.8 16.1 %collective-permute-start.2 = (f32[32,1152]{1,0:T(8,128)}, f32[32,1152]{1,0:T(8,128)}, u32[]{:S(2)}, u32[]{:S(2)}) collective-permute-start(f32[32,1152]{1,0:T(8,128)} %get-tuple-element.419), channel_id=1, source_target_pairs={{0,16},{16,32},{32,48},{48,64},{64,80},{80,96},{96,112},{112,128},... | collective-permute-start | bytes 442376 | tf_op jit(solution)/shard_map/while/body/eval_jaxpr/ppermute | solution.py:10
  501.0 15.6 %collective-permute-start.2 = (f32[32,1152]{1,0:T(8,128)}, f32[32,1152]{1,0:T(8,128)}, u32[]{:S(2)}, u32[]{:S(2)}) collective-permute-start(f32[32,1152]{1,0:T(8,128)} %get-tuple-element.419), channel_id=1, source_target_pairs={{0,16},{16,32},{32,48},{48,64},{64,80},{80,96},{96,112},{112,128},... | collective-permute-start | bytes 442376 | tf_op jit(solution)/shard_map/while/body/eval_jaxpr/ppermute | solution.py:10
  538.6 385.7 %all-reduce.7.cloned.1.call-start = ((), (), s32[]{:S(2)}) async-start(), calls=%async_computation.3 | async-start | bytes 1327104
  (50 other events, 1137.2 us)
Sparse Core Ops, SparseCore 0:
  538.7 67.4 reduce-scatter.5
  609.1 315.0 all-reduce.6
where the time goes:
time: 939 us; the launch traced here: 933 us
  waiting for transfers between devices  558 us (59%)
  starting transfers between devices  135 us (14%)
  matrix products  133 us (14%)
  local copies, waits for them, and re-layouts  58 us (6%)
  other arithmetic  17.8 us (2%)
  between operations  16.2 us (2%)
  blocking collectives  14.2 us (2%)
    unnamed x4, waiting for transfers between devices  354 us
    ppermute x63, waiting for transfers between devices, shifted(): return lax.ppermute(value, axis, pairs)  205 us
    ppermute x63, starting transfers between devices, shifted(): return lax.ppermute(value, axis, pairs)  135 us
    dot_general x32, matrix products, tile_weights(): lax.dot_general(text_block, image_low, (((1,), (1,)), ((), ())), preferre...  101 us
    dynamic_update_slice x32, local copies, waits for them, and re-layouts, record(): seen = lax.dynamic_update_index_in_dim(seen, text_block, step, 0)  47.6 us
    dot_general x32, matrix products, step_travel(): jnp.dot(weights, image_low, preferred_element_type=jnp.float32)  25.9 us
  transfers between devices with their start and end apart: 65, of which 48 were waited for; matrix products, arithmetic and copies ran while one was open for 19% of the time, Pallas kernels for 0%

commit v1 on v0

v1 whole, which is shorter than its diff:
```python
import jax
import jax.numpy as jnp
from jax import lax
from jax.sharding import Mesh, PartitionSpec as P

SIZES = (8, 4, 2, 4, 2)
NAMES = ("y", "zh", "zl", "x", "c")
DP = ("y", "zh")
MP = ("zl", "x", "c")


def shifted(value, axis, steps):
    count = lax.axis_size(axis)
    return lax.ppermute(value, axis, [(s, (s + steps) % count) for s in range(count)])


def normalize(rows):
    wide = rows.astype(jnp.float32)
    factor = lax.rsqrt(jnp.sum(wide * wide, axis=-1, keepdims=True) + 1e-06)
    return (wide * factor, factor)


def unit_back(direction, unit, factor):
    return (direction - unit * jnp.sum(unit * direction, axis=-1, keepdims=True)) * factor


def gather(own, up_last):
    near = [own] + [shifted(own, "zh", k) for k in (1, 2, 3)]
    chunk = jnp.concatenate(near, axis=0)
    chunks = [chunk]
    up = down = chunk
    for _ in range(3):
        up, down = shifted(up, "y", 1), shifted(down, "y", -1)
        chunks += [up, down]
    chunks.append(shifted(up, "y", 1) if up_last else shifted(down, "y", -1))
    return jnp.concatenate(chunks, axis=0)


def sum_over_mp(parts):
    slabs = parts.reshape((8, 2) + parts.shape[1:])
    core = lax.axis_index("c")
    keep = lax.dynamic_index_in_dim(slabs, core, 1, keepdims=False)
    give = lax.dynamic_index_in_dim(slabs, 1 - core, 1, keepdims=False).astype(jnp.bfloat16)
    half = keep + shifted(give, "c", 1).astype(jnp.float32)
    got = lax.all_to_all(half.astype(jnp.bfloat16), ("zl", "x"), 0, 0, tiled=True)
    return jnp.sum(got.astype(jnp.float32), axis=0)


def sum_over_dp(parts):
    slabs = parts.reshape((8, 4) + parts.shape[1:]).astype(jnp.bfloat16)
    got = lax.all_to_all(slabs, "y", 0, 0, tiled=True)
    near = jnp.sum(got.astype(jnp.float32), axis=0)
    return jnp.sum(lax.all_to_all(near, "zh", 0, 0, tiled=True), axis=0)


def local(image_emb, text_emb, image_feat, text_feat, logit_scale, logit_bias):
    column = lax.axis_index(MP)
    own_rows, width = text_emb.shape
    block = image_emb.shape[0]
    depth = image_feat.shape[1]
    scale = logit_scale[0]
    offset = logit_bias[0]
    own_feat = lax.dynamic_slice_in_dim(text_feat, column * own_rows, own_rows, 0)
    all_emb = gather(text_emb, True)
    all_feat = gather(own_feat, False)

    image_unit, image_norm = normalize(image_emb)
    text_unit, text_norm = normalize(all_emb)
    image_low = image_unit.astype(jnp.bfloat16)
    text_low = text_unit.astype(jnp.bfloat16)
    rows = text_low.shape[0]
    logits = lax.dot_general(text_low, image_low, (((1,), (1,)), ((), ())), preferred_element_type=jnp.float32)
    row_ids = jnp.arange(rows, dtype=jnp.int32)[:, None]
    match = (row_ids < own_rows) & (column * own_rows + row_ids == jnp.arange(block, dtype=jnp.int32)[None, :])
    sign = jnp.where(match, 1.0, -1.0).astype(jnp.float32)
    value = scale * logits + offset
    weights = (-scale * sign * jax.nn.sigmoid(-sign * value)).astype(jnp.bfloat16)

    image_dir = lax.dot_general(weights, text_low, (((0,), (0,)), ((), ())), preferred_element_type=jnp.float32)
    image_part = unit_back(image_dir, image_unit, image_norm)
    image_cols = sum_over_mp(image_part.T.reshape(16, width // 16, block)).astype(jnp.bfloat16)
    image_term = jnp.dot(image_cols, image_feat, preferred_element_type=jnp.float32)

    text_dir = jnp.dot(weights, image_low, preferred_element_type=jnp.float32)
    text_part = unit_back(text_dir, text_unit, text_norm).astype(jnp.bfloat16)
    text_all = lax.dot_general(text_part, all_feat, (((0,), (0,)), ((), ())), preferred_element_type=jnp.float32)
    text_term = sum_over_mp(text_all.reshape(16, width // 16, depth))

    def home(term):
        own = sum_over_dp(term.T.reshape(32, depth // 32, width // 16))
        return own

    return (home(image_term), home(text_term))


def solution(mesh):
    split = Mesh(mesh.devices.reshape(SIZES), NAMES)
    in_specs = (P(DP, None), P(DP + MP, None), P(DP, None), P(DP, None), P(), P())
    out_specs = (P(DP, MP), P(DP, MP))
    return jax.shard_map(local, mesh=split, in_specs=in_specs, out_specs=out_specs, check_vma=False)
```

time: 939 us -> 234 us (0.25)
  waiting for transfers between devices: 558 us -> 61.7 us
  matrix products: 133 us -> 12.4 us
  local copies, waits for them, and re-layouts: 58 us -> 31.9 us
  starting transfers between devices: 135 us -> 112 us
  blocking collectives: 14.2 us -> 0 us
  between operations: 16.2 us -> 2.45 us
    unnamed x4 -> x0, waiting for transfers between devices: 354 us -> none
    ppermute x63 -> x22, waiting for transfers between devices: 205 us -> 9.72 us  [shifted(): lax.ppermute(value, axis, [(s, (s + steps) % count) for s in range(count)])]
    dot_general x67 -> x5, matrix products: 133 us -> 12.4 us  [the longest x1 4.27 us: local(): text_dir = jnp.dot(weights, image_low, preferred_element_type=jnp.float32)]
    all_to_all x0 -> x6, waiting for transfers between devices: none -> 52 us  [the longest x2 18.4 us: sum_over_dp(): got = lax.all_to_all(slabs, 'y', 0, 0, tiled=True)]
    ppermute x63 -> x22, starting transfers between devices: 135 us -> 84.7 us  [shifted(): lax.ppermute(value, axis, [(s, (s + steps) % count) for s in range(count)])]
    dynamic_update_slice x33 -> x0, local copies, waits for them, and re-layouts: 48.5 us -> none  [the longest x32 47.6 us: record(): seen = lax.dynamic_update_index_in_dim(seen, text_block, step, 0)]
    all_to_all x0 -> x6, starting transfers between devices: none -> 27.2 us  [the longest x2 11.1 us: sum_over_mp(): lax.all_to_all(half.astype(jnp.bfloat16), ('zl', 'x'), 0, 0, tiled=True)]
    all_to_all x1 -> x0, blocking collectives: 14.2 us -> none  [local(): lax.all_to_all(text_grad, 'mp', split_axis=1, concat_axis=0, tiled=True)]
  transfers between devices with their start and end apart: 65 -> 28, of which waited for: 48 -> 9; matrix products, arithmetic and copies ran while one was open for 19% -> 20% of each run, Pallas kernels for 0% -> 0%
where the time goes in v1:
time: 234 us; the launch traced here: 231 us
  starting transfers between devices  112 us (48%)
  waiting for transfers between devices  61.7 us (26%)
  local copies, waits for them, and re-layouts  31.9 us (14%)
  matrix products  12.4 us (5%)
  other arithmetic  11 us (5%)
  between operations  2.45 us (1%)
    ppermute x22, starting transfers between devices, shifted(): lax.ppermute(value, axis, [(s, (s + steps) % count) for s in range(count)])  84.7 us
    unnamed x35, local copies, waits for them, and re-layouts  19 us
    all_to_all x2, waiting for transfers between devices, sum_over_dp(): got = lax.all_to_all(slabs, 'y', 0, 0, tiled=True)  18.4 us
    all_to_all x2, waiting for transfers between devices, sum_over_mp(): lax.all_to_all(half.astype(jnp.bfloat16), ('zl', 'x'), 0, 0, tiled=True)  18.3 us
    all_to_all x2, waiting for transfers between devices, sum_over_dp(): return jnp.sum(lax.all_to_all(near, 'zh', 0, 0, tiled=True), axis=0)  15.2 us
    all_to_all x2, starting transfers between devices, sum_over_mp(): lax.all_to_all(half.astype(jnp.bfloat16), ('zl', 'x'), 0, 0, tiled=True)  11.1 us
    ppermute x22, waiting for transfers between devices, shifted(): lax.ppermute(value, axis, [(s, (s + steps) % count) for s in range(count)])  9.72 us
    all_to_all x2, starting transfers between devices, sum_over_dp(): return jnp.sum(lax.all_to_all(near, 'zh', 0, 0, tiled=True), axis=0)  8.67 us
  transfers between devices with their start and end apart: 28, of which 9 were waited for; matrix products, arithmetic and copies ran while one was open for 20% of the time, Pallas kernels for 0%

profile of v1, /device:TPU:6, one launch (start us, length us, event | category | flops | bytes accessed | tf_op | source)
XLA Modules:
  0.0 231.4 jit_solution(4052765931113157133)
XLA Ops:
  0.6 11.1 %collective-permute-start.1 = (bf16[32,1152]{1,0:T(8,128)(2,1)}, bf16[32,1152]{1,0:T(8,128)(2,1)}, u32[]{:S(2)}, u32[]{:S(2)}) collective-permute-start(bf16[32,1152]{1,0:T(8,128)(2,1)} %param.7), channel_id=1, source_target_pairs={{0,32},{16,48},{32,0},{48,16},{1,33},{17,49},{33,1},{49,17},{2,34}... | collective-permute-start | bytes 221192 | tf_op jit(solution)/shard_map/ppermute | solution.py:14
  11.7 4.3 %collective-permute-start = (bf16[32,1152]{1,0:T(8,128)(2,1)}, bf16[32,1152]{1,0:T(8,128)(2,1)}, u32[]{:S(2)}, u32[]{:S(2)}) collective-permute-start(bf16[32,1152]{1,0:T(8,128)(2,1)} %param.7), channel_id=1, source_target_pairs={{0,16},{16,32},{32,48},{48,0},{1,17},{17,33},{33,49},{49,1},{2,18}... | collective-permute-start | bytes 221192 | tf_op jit(solution)/shard_map/ppermute | solution.py:14
  17.6 3.6 %collective-permute-start.13 = (bf16[32,1152]{1,0:T(8,128)(2,1)}, bf16[32,1152]{1,0:T(8,128)(2,1)}, u32[]{:S(2)}, u32[]{:S(2)}) collective-permute-start(bf16[32,1152]{1,0:T(8,128)(2,1)} %get-tuple-element.3), channel_id=1, source_target_pairs={{0,48},{16,0},{32,16},{48,32},{1,49},{17,1},{33,17},{49,33},{2,50}... | collective-permute-start | bytes 221192 | tf_op jit(solution)/shard_map/ppermute | solution.py:14
  21.2 3.7 %collective-permute-start.12 = (bf16[32,1152]{1,0:T(8,128)(2,1)}, bf16[32,1152]{1,0:T(8,128)(2,1)}, u32[]{:S(2)}, u32[]{:S(2)}) collective-permute-start(bf16[32,1152]{1,0:T(8,128)(2,1)} %get-tuple-element.3), channel_id=1, source_target_pairs={{0,32},{16,48},{32,0},{48,16},{1,33},{17,49},{33,1},{49,17},{2,34}... | collective-permute-start | bytes 221192 | tf_op jit(solution)/shard_map/ppermute | solution.py:14
  31.9 5.5 %collective-permute-start.2 = (bf16[32,1152]{1,0:T(8,128)(2,1)}, bf16[32,1152]{1,0:T(8,128)(2,1)S(1)}, u32[]{:S(2)}, u32[]{:S(2)}) collective-permute-start(bf16[32,1152]{1,0:T(8,128)(2,1)} %param.7), channel_id=1, source_target_pairs={{0,48},{16,0},{32,16},{48,32},{1,49},{17,1},{33,17},{49,33},{2,50}... | collective-permute-start | bytes 221192 | tf_op jit(solution)/shard_map/ppermute | solution.py:14
  38.4 5.4 %collective-permute-start.15 = (bf16[128,1152]{1,0:T(8,128)(2,1)S(1)}, bf16[128,1152]{1,0:T(8,128)(2,1)S(1)}, u32[]{:S(2)}, u32[]{:S(2)}) collective-permute-start(bf16[128,1152]{1,0:T(8,128)(2,1)S(1)} %pad_maximum_fusion), channel_id=1, source_target_pairs={{0,448},{64,0},{128,64},{192,128},{256,192},{320,256},{384,320},{4... | collective-permute-start | bytes 884744 | tf_op jit(solution)/shard_map/ppermute | solution.py:14
  49.5 5.1 %collective-permute-start.4 = (bf16[128,1152]{1,0:T(8,128)(2,1)}, bf16[128,1152]{1,0:T(8,128)(2,1)S(1)}, u32[]{:S(2)}, u32[]{:S(2)}) collective-permute-start(bf16[128,1152]{1,0:T(8,128)(2,1)} %get-tuple-element.4), channel_id=1, source_target_pairs={{0,448},{64,0},{128,64},{192,128},{256,192},{320,256},{384,320},{4... | collective-permute-start | bytes 884744 | tf_op jit(solution)/shard_map/ppermute | solution.py:14
  61.1 5.1 %collective-permute-start.17 = (bf16[128,1152]{1,0:T(8,128)(2,1)S(1)}, bf16[128,1152]{1,0:T(8,128)(2,1)S(1)}, u32[]{:S(2)}, u32[]{:S(2)}) collective-permute-start(bf16[128,1152]{1,0:T(8,128)(2,1)S(1)} %collective-permute-done.15), channel_id=1, source_target_pairs={{0,448},{64,0},{128,64},{192,128},{256,192},{320,256},{384,320},{4... | collective-permute-start | bytes 884744 | tf_op jit(solution)/shard_map/ppermute | solution.py:14
  68.9 5.1 %collective-permute-start.6 = (bf16[128,1152]{1,0:T(8,128)(2,1)S(1)}, bf16[128,1152]{1,0:T(8,128)(2,1)S(1)}, u32[]{:S(2)}, u32[]{:S(2)}) collective-permute-start(bf16[128,1152]{1,0:T(8,128)(2,1)S(1)} %collective-permute-done.4), channel_id=1, source_target_pairs={{0,448},{64,0},{128,64},{192,128},{256,192},{320,256},{384,320},{4... | collective-permute-start | bytes 884744 | tf_op jit(solution)/shard_map/ppermute | solution.py:14
  76.7 5.1 %collective-permute-start.19 = (bf16[128,1152]{1,0:T(8,128)(2,1)S(1)}, bf16[128,1152]{1,0:T(8,128)(2,1)}, u32[]{:S(2)}, u32[]{:S(2)}) collective-permute-start(bf16[128,1152]{1,0:T(8,128)(2,1)S(1)} %collective-permute-done.17), channel_id=1, source_target_pairs={{0,448},{64,0},{128,64},{192,128},{256,192},{320,256},{384,320},{4... | collective-permute-start | bytes 884744 | tf_op jit(solution)/shard_map/ppermute | solution.py:14
  84.6 5.1 %collective-permute-start.8 = (bf16[128,1152]{1,0:T(8,128)(2,1)S(1)}, bf16[128,1152]{1,0:T(8,128)(2,1)S(1)}, u32[]{:S(2)}, u32[]{:S(2)}) collective-permute-start(bf16[128,1152]{1,0:T(8,128)(2,1)S(1)} %collective-permute-done.6), channel_id=1, source_target_pairs={{0,448},{64,0},{128,64},{192,128},{256,192},{320,256},{384,320},{4... | collective-permute-start | bytes 884744 | tf_op jit(solution)/shard_map/ppermute | solution.py:14
  92.4 5.1 %collective-permute-start.20 = (bf16[128,1152]{1,0:T(8,128)(2,1)}, bf16[128,1152]{1,0:T(8,128)(2,1)}, u32[]{:S(2)}, u32[]{:S(2)}) collective-permute-start(bf16[128,1152]{1,0:T(8,128)(2,1)} %collective-permute-done.19), channel_id=1, source_target_pairs={{0,448},{64,0},{128,64},{192,128},{256,192},{320,256},{384,320},{4... | collective-permute-start | bytes 884744 | tf_op jit(solution)/shard_map/ppermute | solution.py:14
  102.4 7.6 %collective-permute-done.9 = bf16[128,1152]{1,0:T(8,128)(2,1)S(1)} collective-permute-done((bf16[128,1152]{1,0:T(8,128)(2,1)S(1)}, bf16[128,1152]{1,0:T(8,128)(2,1)S(1)}, u32[]{:S(2)}, u32[]{:S(2)}) %collective-permute-start.9) | collective-permute-done | bytes 294944 | tf_op jit(solution)/shard_map/ppermute | solution.py:14
  117.5 4.3 %fusion.3 = (f32[1024]{0:T(1024)S(1)}, f32[1024,1152]{1,0:T(8,128)S(1)}) fusion(bf16[1024,1152]{1,0:T(8,128)(2,1)} %copy-done.4, f32[1024]{0:T(1024)S(1)} %add_rsqrt_fusion, bf16[1024,512]{1,0:T(8,128)(2,1)} %copy-done.7, bf16[512,1152]{1,0:T(8,128)(2,1)} %param.6, f32[512]{0:T(512)S(1)} %add_rsqrt_fusion.1), kind=kOutput, calls=%fused_computation.5 | convolution fusion | flops 1214446592 | bytes 9316352 | tf_op jit(solution)/shard_map/dot_general | solution.py:84
  139.3 5.7 %all-to-all-start = ((bf16[8,72,512]{2,1,0:T(8,128)(2,1)}), bf16[8,72,512]{2,1,0:T(8,128)(2,1)S(1)}, u32[]{:S(2)}, u32[]{:S(2)}) async-start(bf16[8,72,512]{2,1,0:T(8,128)(2,1)} %fusion.31), calls=%async_computation | async-start | bytes 1179648 | tf_op jit(solution)/shard_map/all_to_all | solution.py:45
  148.5 5.2 %all-to-all-done = bf16[8,72,512]{2,1,0:T(8,128)(2,1)S(1)} async-done(((bf16[8,72,512]{2,1,0:T(8,128)(2,1)}), bf16[8,72,512]{2,1,0:T(8,128)(2,1)S(1)}, u32[]{:S(2)}, u32[]{:S(2)}) %all-to-all-start) | async-done | bytes 589856 | tf_op jit(solution)/shard_map/all_to_all | solution.py:45
  153.7 5.4 %all-to-all-start.3 = ((bf16[8,72,1152]{2,1,0:T(8,128)(2,1)}), bf16[8,72,1152]{2,1,0:T(8,128)(2,1)S(1)}, u32[]{:S(2)}, u32[]{:S(2)}) async-start(bf16[8,72,1152]{2,1,0:T(8,128)(2,1)} %fusion.11), calls=%async_computation.3 | async-start | bytes 2654208 | tf_op jit(solution)/shard_map/all_to_all | solution.py:45
  162.5 13.1 %all-to-all-done.3 = bf16[8,72,1152]{2,1,0:T(8,128)(2,1)S(1)} async-done(((bf16[8,72,1152]{2,1,0:T(8,128)(2,1)}), bf16[8,72,1152]{2,1,0:T(8,128)(2,1)S(1)}, u32[]{:S(2)}, u32[]{:S(2)}) %all-to-all-start.3) | async-done | bytes 1327136 | tf_op jit(solution)/shard_map/all_to_all | solution.py:45
  175.6 4.1 %all-to-all-start.1 = ((bf16[8,4,36,72]{3,1,2,0:T(4,128)(2,1)}), bf16[8,4,36,72]{3,1,2,0:T(4,128)(2,1)S(1)}, u32[]{:S(2)}, u32[]{:S(2)}) async-start(bf16[8,4,36,72]{3,1,2,0:T(4,128)(2,1)} %copy.24), calls=%async_computation.1 | async-start | bytes 589824 | tf_op jit(solution)/shard_map/all_to_all | solution.py:51
  182.8 8.5 %all-to-all-done.1 = bf16[8,4,36,72]{3,1,2,0:T(4,128)(2,1)S(1)} async-done(((bf16[8,4,36,72]{3,1,2,0:T(4,128)(2,1)}), bf16[8,4,36,72]{3,1,2,0:T(4,128)(2,1)S(1)}, u32[]{:S(2)}, u32[]{:S(2)}) %all-to-all-start.1) | async-done | bytes 165920 | tf_op jit(solution)/shard_map/all_to_all | solution.py:51
  195.5 9.9 %all-to-all-done.4 = bf16[8,4,36,72]{3,1,2,0:T(4,128)(2,1)S(1)} async-done(((bf16[8,4,36,72]{3,1,2,0:T(4,128)(2,1)}), bf16[8,4,36,72]{3,1,2,0:T(4,128)(2,1)S(1)}, u32[]{:S(2)}, u32[]{:S(2)}) %all-to-all-start.4) | async-done | bytes 165920 | tf_op jit(solution)/shard_map/all_to_all | solution.py:51
  205.5 5.4 %all-to-all-start.2 = ((f32[4,36,72]{2,1,0:T(8,128)}), f32[4,36,72]{2,1,0:T(8,128)S(1)}, u32[]{:S(2)}, u32[]{:S(2)}) async-start(f32[4,36,72]{2,1,0:T(8,128)} %copy.25), calls=%async_computation.2 | async-start | bytes 163840 | tf_op jit(solution)/shard_map/all_to_all | solution.py:53
  211.6 7.5 %all-to-all-done.2 = f32[4,36,72]{2,1,0:T(8,128)S(1)} async-done(((f32[4,36,72]{2,1,0:T(8,128)}), f32[4,36,72]{2,1,0:T(8,128)S(1)}, u32[]{:S(2)}, u32[]{:S(2)}) %all-to-all-start.2) | async-done | bytes 41504 | tf_op jit(solution)/shard_map/all_to_all | solution.py:53
  223.1 7.7 %all-to-all-done.5 = f32[4,36,72]{2,1,0:T(8,128)S(1)} async-done(((f32[4,36,72]{2,1,0:T(8,128)}), f32[4,36,72]{2,1,0:T(8,128)S(1)}, u32[]{:S(2)}, u32[]{:S(2)}) %all-to-all-start.5) | async-done | bytes 41504 | tf_op jit(solution)/shard_map/all_to_all | solution.py:53
  (100 shorter events, 80.2 us)
Async XLA Ops:
  0.6 46.7 %collective-permute-start.1 = (bf16[32,1152]{1,0:T(8,128)(2,1)}, bf16[32,1152]{1,0:T(8,128)(2,1)}, u32[]{:S(2)}, u32[]{:S(2)}) collective-permute-start(bf16[32,1152]{1,0:T(8,128)(2,1)} %param.7), channel_id=1, source_target_pairs={{0,32},{16,48},{32,0},{48,16},{1,33},{17,49},{33,1},{49,17},{2,34}... | collective-permute-start | bytes 221192 | tf_op jit(solution)/shard_map/ppermute | solution.py:14
  11.7 34.1 %collective-permute-start = (bf16[32,1152]{1,0:T(8,128)(2,1)}, bf16[32,1152]{1,0:T(8,128)(2,1)}, u32[]{:S(2)}, u32[]{:S(2)}) collective-permute-start(bf16[32,1152]{1,0:T(8,128)(2,1)} %param.7), channel_id=1, source_target_pairs={{0,16},{16,32},{32,48},{48,0},{1,17},{17,33},{33,49},{49,1},{2,18}... | collective-permute-start | bytes 221192 | tf_op jit(solution)/shard_map/ppermute | solution.py:14
  17.6 14.3 %collective-permute-start.13 = (bf16[32,1152]{1,0:T(8,128)(2,1)}, bf16[32,1152]{1,0:T(8,128)(2,1)}, u32[]{:S(2)}, u32[]{:S(2)}) collective-permute-start(bf16[32,1152]{1,0:T(8,128)(2,1)} %get-tuple-element.3), channel_id=1, source_target_pairs={{0,48},{16,0},{32,16},{48,32},{1,49},{17,1},{33,17},{49,33},{2,50}... | collective-permute-start | bytes 221192 | tf_op jit(solution)/shard_map/ppermute | solution.py:14
  21.2 16.2 %collective-permute-start.12 = (bf16[32,1152]{1,0:T(8,128)(2,1)}, bf16[32,1152]{1,0:T(8,128)(2,1)}, u32[]{:S(2)}, u32[]{:S(2)}) collective-permute-start(bf16[32,1152]{1,0:T(8,128)(2,1)} %get-tuple-element.3), channel_id=1, source_target_pairs={{0,32},{16,48},{32,0},{48,16},{1,33},{17,49},{33,1},{49,17},{2,34}... | collective-permute-start | bytes 221192 | tf_op jit(solution)/shard_map/ppermute | solution.py:14
  25.0 12.4 %collective-permute-start.11 = (bf16[32,1152]{1,0:T(8,128)(2,1)}, bf16[32,1152]{1,0:T(8,128)(2,1)}, u32[]{:S(2)}, u32[]{:S(2)}) collective-permute-start(bf16[32,1152]{1,0:T(8,128)(2,1)} %get-tuple-element.3), channel_id=1, source_target_pairs={{0,16},{16,32},{32,48},{48,0},{1,17},{17,33},{33,49},{49,1},{2,18}... | collective-permute-start | bytes 221192 | tf_op jit(solution)/shard_map/ppermute | solution.py:14
  31.9 16.9 %collective-permute-start.2 = (bf16[32,1152]{1,0:T(8,128)(2,1)}, bf16[32,1152]{1,0:T(8,128)(2,1)S(1)}, u32[]{:S(2)}, u32[]{:S(2)}) collective-permute-start(bf16[32,1152]{1,0:T(8,128)(2,1)} %param.7), channel_id=1, source_target_pairs={{0,48},{16,0},{32,16},{48,32},{1,49},{17,1},{33,17},{49,33},{2,50}... | collective-permute-start | bytes 221192 | tf_op jit(solution)/shard_map/ppermute | solution.py:14
  38.4 22.6 %collective-permute-start.15 = (bf16[128,1152]{1,0:T(8,128)(2,1)S(1)}, bf16[128,1152]{1,0:T(8,128)(2,1)S(1)}, u32[]{:S(2)}, u32[]{:S(2)}) collective-permute-start(bf16[128,1152]{1,0:T(8,128)(2,1)S(1)} %pad_maximum_fusion), channel_id=1, source_target_pairs={{0,448},{64,0},{128,64},{192,128},{256,192},{320,256},{384,320},{4... | collective-permute-start | bytes 884744 | tf_op jit(solution)/shard_map/ppermute | solution.py:14
  43.8 22.4 %collective-permute-start.14 = (bf16[128,1152]{1,0:T(8,128)(2,1)S(1)}, bf16[128,1152]{1,0:T(8,128)(2,1)S(1)}, u32[]{:S(2)}, u32[]{:S(2)}) collective-permute-start(bf16[128,1152]{1,0:T(8,128)(2,1)S(1)} %pad_maximum_fusion), channel_id=1, source_target_pairs={{0,64},{64,128},{128,192},{192,256},{256,320},{320,384},{384,448},... | collective-permute-start | bytes 884744 | tf_op jit(solution)/shard_map/ppermute | solution.py:14
  49.5 19.4 %collective-permute-start.4 = (bf16[128,1152]{1,0:T(8,128)(2,1)}, bf16[128,1152]{1,0:T(8,128)(2,1)S(1)}, u32[]{:S(2)}, u32[]{:S(2)}) collective-permute-start(bf16[128,1152]{1,0:T(8,128)(2,1)} %get-tuple-element.4), channel_id=1, source_target_pairs={{0,448},{64,0},{128,64},{192,128},{256,192},{320,256},{384,320},{4... | collective-permute-start | bytes 884744 | tf_op jit(solution)/shard_map/ppermute | solution.py:14
  54.6 20.1 %collective-permute-start.3 = (bf16[128,1152]{1,0:T(8,128)(2,1)}, bf16[128,1152]{1,0:T(8,128)(2,1)S(1)}, u32[]{:S(2)}, u32[]{:S(2)}) collective-permute-start(bf16[128,1152]{1,0:T(8,128)(2,1)} %get-tuple-element.4), channel_id=1, source_target_pairs={{0,64},{64,128},{128,192},{192,256},{256,320},{320,384},{384,448},... | collective-permute-start | bytes 884744 | tf_op jit(solution)/shard_map/ppermute | solution.py:14
  61.1 15.7 %collective-permute-start.17 = (bf16[128,1152]{1,0:T(8,128)(2,1)S(1)}, bf16[128,1152]{1,0:T(8,128)(2,1)S(1)}, u32[]{:S(2)}, u32[]{:S(2)}) collective-permute-start(bf16[128,1152]{1,0:T(8,128)(2,1)S(1)} %collective-permute-done.15), channel_id=1, source_target_pairs={{0,448},{64,0},{128,64},{192,128},{256,192},{320,256},{384,320},{4... | collective-permute-start | bytes 884744 | tf_op jit(solution)/shard_map/ppermute | solution.py:14
  66.2 15.7 %collective-permute-start.16 = (bf16[128,1152]{1,0:T(8,128)(2,1)S(1)}, bf16[128,1152]{1,0:T(8,128)(2,1)S(1)}, u32[]{:S(2)}, u32[]{:S(2)}) collective-permute-start(bf16[128,1152]{1,0:T(8,128)(2,1)S(1)} %collective-permute-done.14), channel_id=1, source_target_pairs={{0,64},{64,128},{128,192},{192,256},{256,320},{320,384},{384,448},... | collective-permute-start | bytes 884744 | tf_op jit(solution)/shard_map/ppermute | solution.py:14
  68.9 15.7 %collective-permute-start.6 = (bf16[128,1152]{1,0:T(8,128)(2,1)S(1)}, bf16[128,1152]{1,0:T(8,128)(2,1)S(1)}, u32[]{:S(2)}, u32[]{:S(2)}) collective-permute-start(bf16[128,1152]{1,0:T(8,128)(2,1)S(1)} %collective-permute-done.4), channel_id=1, source_target_pairs={{0,448},{64,0},{128,64},{192,128},{256,192},{320,256},{384,320},{4... | collective-permute-start | bytes 884744 | tf_op jit(solution)/shard_map/ppermute | solution.py:14
  74.7 15.7 %collective-permute-start.5 = (bf16[128,1152]{1,0:T(8,128)(2,1)S(1)}, bf16[128,1152]{1,0:T(8,128)(2,1)S(1)}, u32[]{:S(2)}, u32[]{:S(2)}) collective-permute-start(bf16[128,1152]{1,0:T(8,128)(2,1)S(1)} %collective-permute-done.3), channel_id=1, source_target_pairs={{0,64},{64,128},{128,192},{192,256},{256,320},{320,384},{384,448},... | collective-permute-start | bytes 884744 | tf_op jit(solution)/shard_map/ppermute | solution.py:14
  76.7 15.7 %collective-permute-start.19 = (bf16[128,1152]{1,0:T(8,128)(2,1)S(1)}, bf16[128,1152]{1,0:T(8,128)(2,1)}, u32[]{:S(2)}, u32[]{:S(2)}) collective-permute-start(bf16[128,1152]{1,0:T(8,128)(2,1)S(1)} %collective-permute-done.17), channel_id=1, source_target_pairs={{0,448},{64,0},{128,64},{192,128},{256,192},{320,256},{384,320},{4... | collective-permute-start | bytes 884744 | tf_op jit(solution)/shard_map/ppermute | solution.py:14
  81.9 15.7 %collective-permute-start.18 = (bf16[128,1152]{1,0:T(8,128)(2,1)S(1)}, bf16[128,1152]{1,0:T(8,128)(2,1)S(1)}, u32[]{:S(2)}, u32[]{:S(2)}) collective-permute-start(bf16[128,1152]{1,0:T(8,128)(2,1)S(1)} %collective-permute-done.16), channel_id=1, source_target_pairs={{0,64},{64,128},{128,192},{192,256},{256,320},{320,384},{384,448},... | collective-permute-start | bytes 884744 | tf_op jit(solution)/shard_map/ppermute | solution.py:14
  84.6 17.8 %collective-permute-start.8 = (bf16[128,1152]{1,0:T(8,128)(2,1)S(1)}, bf16[128,1152]{1,0:T(8,128)(2,1)S(1)}, u32[]{:S(2)}, u32[]{:S(2)}) collective-permute-start(bf16[128,1152]{1,0:T(8,128)(2,1)S(1)} %collective-permute-done.6), channel_id=1, source_target_pairs={{0,448},{64,0},{128,64},{192,128},{256,192},{320,256},{384,320},{4... | collective-permute-start | bytes 884744 | tf_op jit(solution)/shard_map/ppermute | solution.py:14
  92.4 29.3 %collective-permute-start.20 = (bf16[128,1152]{1,0:T(8,128)(2,1)}, bf16[128,1152]{1,0:T(8,128)(2,1)}, u32[]{:S(2)}, u32[]{:S(2)}) collective-permute-start(bf16[128,1152]{1,0:T(8,128)(2,1)} %collective-permute-done.19), channel_id=1, source_target_pairs={{0,448},{64,0},{128,64},{192,128},{256,192},{320,256},{384,320},{4... | collective-permute-start | bytes 884744 | tf_op jit(solution)/shard_map/ppermute | solution.py:14
  130.1 15.0 %collective-permute-start.21 = (bf16[8,72,1152]{2,1,0:T(8,128)(2,1)}, bf16[8,72,1152]{2,1,0:T(8,128)(2,1)}, u32[]{:S(2)}, u32[]{:S(2)}) collective-permute-start(bf16[8,72,1152]{2,1,0:T(8,128)(2,1)} %fusion.30), channel_id=1, source_target_pairs={{0,1},{1,0},{2,3},{3,2},{4,5},{5,4},{6,7},{7,6},{8,9},{9,8},{10,11... | collective-permute-start | bytes 3981320 | tf_op jit(solution)/shard_map/ppermute | solution.py:14
  139.3 14.4 %all-to-all-start = ((bf16[8,72,512]{2,1,0:T(8,128)(2,1)}), bf16[8,72,512]{2,1,0:T(8,128)(2,1)S(1)}, u32[]{:S(2)}, u32[]{:S(2)}) async-start(bf16[8,72,512]{2,1,0:T(8,128)(2,1)} %fusion.31), calls=%async_computation | async-start | bytes 1179648 | tf_op jit(solution)/shard_map/all_to_all | solution.py:45
  153.7 21.9 %all-to-all-start.3 = ((bf16[8,72,1152]{2,1,0:T(8,128)(2,1)}), bf16[8,72,1152]{2,1,0:T(8,128)(2,1)S(1)}, u32[]{:S(2)}, u32[]{:S(2)}) async-start(bf16[8,72,1152]{2,1,0:T(8,128)(2,1)} %fusion.11), calls=%async_computation.3 | async-start | bytes 2654208 | tf_op jit(solution)/shard_map/all_to_all | solution.py:45
  175.6 15.7 %all-to-all-start.1 = ((bf16[8,4,36,72]{3,1,2,0:T(4,128)(2,1)}), bf16[8,4,36,72]{3,1,2,0:T(4,128)(2,1)S(1)}, u32[]{:S(2)}, u32[]{:S(2)}) async-start(bf16[8,4,36,72]{3,1,2,0:T(4,128)(2,1)} %copy.24), calls=%async_computation.1 | async-start | bytes 589824 | tf_op jit(solution)/shard_map/all_to_all | solution.py:51
  191.3 14.2 %all-to-all-start.4 = ((bf16[8,4,36,72]{3,1,2,0:T(4,128)(2,1)}), bf16[8,4,36,72]{3,1,2,0:T(4,128)(2,1)S(1)}, u32[]{:S(2)}, u32[]{:S(2)}) async-start(bf16[8,4,36,72]{3,1,2,0:T(4,128)(2,1)} %copy.28), calls=%async_computation.4 | async-start | bytes 589824 | tf_op jit(solution)/shard_map/all_to_all | solution.py:51
  205.5 13.7 %all-to-all-start.2 = ((f32[4,36,72]{2,1,0:T(8,128)}), f32[4,36,72]{2,1,0:T(8,128)S(1)}, u32[]{:S(2)}, u32[]{:S(2)}) async-start(f32[4,36,72]{2,1,0:T(8,128)} %copy.25), calls=%async_computation.2 | async-start | bytes 163840 | tf_op jit(solution)/shard_map/all_to_all | solution.py:53
  (12 other events, 229.2 us)

commit v2 on v1

v2 whole, which is shorter than its diff:
```python
import jax
import jax.numpy as jnp
from jax import lax
from jax.sharding import Mesh, PartitionSpec as P

SIZES = (8, 2, 2, 2, 4, 2)
NAMES = ("y", "a", "b", "zl", "x", "c")
DP = ("y", "a", "b")
MP = ("zl", "x", "c")
ROW = ("zl", "x")


def shifted(value, axis, steps):
    count = lax.axis_size(axis)
    return lax.ppermute(value, axis, [(s, (s + steps) % count) for s in range(count)])


def normalize(rows, axis=-1):
    wide = rows.astype(jnp.float32)
    factor = lax.rsqrt(jnp.sum(wide * wide, axis=axis, keepdims=True) + 1e-06)
    return (wide * factor, factor)


def unit_back(direction, unit, factor, axis=-1):
    return (direction - unit * jnp.sum(unit * direction, axis=axis, keepdims=True)) * factor


def gather(text, feat):
    rows = text.shape[0]
    far = shifted(jnp.concatenate([text, feat], axis=0), "a", 1)
    chunk = jnp.concatenate([text, far[:rows], feat, far[rows:]], axis=0)
    chunks = [chunk]
    up = down = chunk
    for _ in range(3):
        up, down = shifted(up, "y", 1), shifted(down, "y", -1)
        chunks += [up, down]
    half = chunk.shape[0] // 2
    last_text, last_feat = shifted(up[:half], "y", 1), shifted(down[half:], "y", -1)
    texts = jnp.concatenate([piece[:half] for piece in chunks] + [last_text], axis=0)
    feats = jnp.concatenate([piece[half:] for piece in chunks] + [last_feat], axis=0)
    return texts, shifted(texts, "c", 1), feats, shifted(feats, "c", 1)


def sum_over_row(slabs):
    got = lax.all_to_all(slabs, ROW, 0, 0, tiled=True)
    return jnp.sum(got.astype(jnp.float32), axis=0)


def sum_over_dp(parts):
    rows, cols = parts.shape
    got = lax.all_to_all(parts.astype(jnp.bfloat16).reshape(8, rows // 8, cols), "y", 0, 0, tiled=True)
    near = jnp.sum(got.astype(jnp.float32), axis=0)
    return jnp.sum(lax.all_to_all(near.reshape(4, rows // 32, cols), ("a", "b"), 0, 0, tiled=True), axis=0)


def local(image_emb, text_emb, image_feat, text_feat, logit_scale, logit_bias):
    column = lax.axis_index(MP)
    core = lax.axis_index("c")
    low = lax.axis_index("b")
    own_rows, width = text_emb.shape
    block = image_emb.shape[0]
    depth = image_feat.shape[1]
    cols = width // 16
    scale = logit_scale[0]
    offset = logit_bias[0]

    images = lax.ppermute(image_emb, ("b", "c"), [(0, 0), (1, 2), (2, 1), (3, 3)])
    own_feat = lax.dynamic_slice_in_dim(text_feat, column * own_rows, own_rows, 0)
    text_here, text_there, feat_here, feat_there = gather(text_emb, own_feat)

    image_unit, image_norm = normalize(images)
    image_low = image_unit.astype(jnp.bfloat16)
    texts = jnp.concatenate([text_here, text_there], axis=0)
    feats = jnp.concatenate([feat_here, feat_there], axis=0)
    text_unit, text_norm = normalize(texts)
    text_low = text_unit.astype(jnp.bfloat16)
    rows = text_low.shape[0]
    logits = lax.dot_general(text_low, image_low, (((1,), (1,)), ((), ())), preferred_element_type=jnp.float32)
    row_ids = jnp.arange(rows, dtype=jnp.int32)[:, None]
    image_ids = jnp.arange(block, dtype=jnp.int32)[None, :]
    other = column + 1 - 2 * core
    match = (row_ids < own_rows) & (image_ids == column * own_rows + row_ids)
    match |= (row_ids >= rows // 2) & (row_ids < rows // 2 + own_rows) & (
        image_ids == other * own_rows + row_ids - rows // 2
    )
    sign = jnp.where(match & (low == core), 1.0, -1.0).astype(jnp.float32)
    value = scale * logits + offset
    weights = (-scale * sign * jax.nn.sigmoid(-sign * value)).astype(jnp.bfloat16)

    image_dir = lax.dot_general(text_low, weights, (((0,), (0,)), ((), ())), preferred_element_type=jnp.float32)
    image_part = unit_back(image_dir, image_unit.T, image_norm.T, 0).astype(jnp.bfloat16)
    image_two = sum_over_row(image_part.reshape(8, 2 * cols, block)).reshape(2, cols, block)
    same = lax.dynamic_index_in_dim(image_two, low, 0, keepdims=False)
    cross = lax.dynamic_index_in_dim(image_two, 1 - low, 0, keepdims=False)
    same = lax.ppermute(same, ("b", "c"), [(0, 0), (1, 2), (2, 1), (3, 3)])
    cross = lax.ppermute(cross, ("b", "c"), [(0, 1), (1, 3), (2, 0), (3, 2)])
    image_cols = (same + cross).astype(jnp.bfloat16)
    image_term = jnp.dot(image_cols, image_feat, preferred_element_type=jnp.float32)

    text_dir = jnp.dot(weights, image_low, preferred_element_type=jnp.float32)
    text_part = unit_back(text_dir, text_unit, text_norm).astype(jnp.bfloat16)
    text_all = lax.dot_general(text_part, feats, (((0,), (0,)), ((), ())), preferred_element_type=jnp.float32)
    slabs = text_all.astype(jnp.bfloat16).reshape(8, 2, cols, depth)
    keep = lax.dynamic_index_in_dim(slabs, core, 1, keepdims=False).astype(jnp.float32)
    give = lax.dynamic_index_in_dim(slabs, 1 - core, 1, keepdims=False)
    text_term = sum_over_row((keep + shifted(give, "c", 1).astype(jnp.float32)).astype(jnp.bfloat16))

    own = sum_over_dp(jnp.concatenate([image_term, text_term], axis=0).T)
    return (own[:, :cols], own[:, cols:])


def solution(mesh):
    split = Mesh(mesh.devices.reshape(SIZES), NAMES)
    in_specs = (P(DP, None), P(DP + MP, None), P(DP, None), P(DP, None), P(), P())
    out_specs = (P(DP, MP), P(DP, MP))
    return jax.shard_map(local, mesh=split, in_specs=in_specs, out_specs=out_specs, check_vma=False)
```

time: 234 us -> 193 us (0.82)
  starting transfers between devices: 112 us -> 63.6 us
  blocking collectives: 0 us -> 43.1 us
  waiting for transfers between devices: 61.7 us -> 32 us
  local copies, waits for them, and re-layouts: 31.9 us -> 21.1 us
  matrix products: 12.4 us -> 18.5 us
    all_to_all x6 -> x2, waiting for transfers between devices: 52 us -> 7.21 us  [sum_over_row(): got = lax.all_to_all(slabs, ROW, 0, 0, tiled=True)]
    all_to_all x0 -> x2, blocking collectives: none -> 43.1 us  [the longest x1 24.4 us: sum_over_dp(): lax.all_to_all(parts.astype(jnp.bfloat16).reshape(8, rows // 8, cols), 'y...]
    ppermute x22 -> x12, starting transfers between devices: 84.7 us -> 42.7 us  [shifted(): lax.ppermute(value, axis, [(s, (s + steps) % count) for s in range(count)])]
    all_to_all x6 -> x2, starting transfers between devices: 27.2 us -> 12.6 us  [sum_over_row(): got = lax.all_to_all(slabs, ROW, 0, 0, tiled=True)]
    ppermute x22 -> x12, waiting for transfers between devices: 9.72 us -> 21.8 us  [shifted(): lax.ppermute(value, axis, [(s, (s + steps) % count) for s in range(count)])]
    ppermute x0 -> x3, starting transfers between devices: none -> 8.31 us  [the longest x1 6.9 us: local(): cross = lax.ppermute(cross, ('b', 'c'), [(0, 1), (1, 3), (2, 0), (3, 2)])]
    convert_element_type x6 -> x0, local copies, waits for them, and re-layouts: 7.96 us -> none  [the longest x4 5.86 us: sum_over_dp(): slabs = parts.reshape((8, 4) + parts.shape[1:]).astype(jnp.bfloat16)]
    unnamed x35 -> x16, local copies, waits for them, and re-layouts: 19 us -> 11.7 us
  transfers between devices with their start and end apart: 28 -> 17, of which waited for: 9 -> 8; matrix products, arithmetic and copies ran while one was open for 20% -> 23% of each run, Pallas kernels for 0% -> 0%
where the time goes in v2:
time: 193 us; the launch traced here: 192 us
  starting transfers between devices  63.6 us (33%)
  blocking collectives  43.1 us (22%)
  waiting for transfers between devices  32 us (17%)
  local copies, waits for them, and re-layouts  21.1 us (11%)
  matrix products  18.5 us (10%)
  other arithmetic  11.5 us (6%)
  between operations  2.28 us (1%)
    ppermute x12, starting transfers between devices, shifted(): lax.ppermute(value, axis, [(s, (s + steps) % count) for s in range(count)])  42.7 us
    all_to_all x1, blocking collectives, sum_over_dp(): lax.all_to_all(parts.astype(jnp.bfloat16).reshape(8, rows // 8, cols), 'y...  24.4 us
    ppermute x12, waiting for transfers between devices, shifted(): lax.ppermute(value, axis, [(s, (s + steps) % count) for s in range(count)])  21.8 us
    all_to_all x1, blocking collectives, sum_over_dp(): lax.all_to_all(near.reshape(4, rows // 32, cols), ('a', 'b'), 0, 0, tiled...  18.7 us
    all_to_all x2, starting transfers between devices, sum_over_row(): got = lax.all_to_all(slabs, ROW, 0, 0, tiled=True)  12.6 us
    unnamed x16, local copies, waits for them, and re-layouts  11.7 us
    all_to_all x2, waiting for transfers between devices, sum_over_row(): got = lax.all_to_all(slabs, ROW, 0, 0, tiled=True)  7.21 us
    dot_general x1, matrix products, local(): lax.dot_general(text_part, feats, (((0,), (0,)), ((), ())), preferred_ele...  7 us
  transfers between devices with their start and end apart: 17, of which 8 were waited for; matrix products, arithmetic and copies ran while one was open for 23% of the time, Pallas kernels for 0%

profile of v2, /device:TPU:6, one launch (start us, length us, event | category | flops | bytes accessed | tf_op | source)
XLA Modules:
  0.0 191.9 jit_solution(3196212016280991532)
XLA Ops:
  3.2 10.9 %collective-permute-start = (bf16[64,1152]{1,0:T(8,128)(2,1)S(1)}, bf16[64,1152]{1,0:T(8,128)(2,1)S(1)}, u32[]{:S(2)}, u32[]{:S(2)}) collective-permute-start(bf16[64,1152]{1,0:T(8,128)(2,1)S(1)} %pad_maximum_fusion.1), channel_id=1, source_target_pairs={{0,32},{32,0},{1,33},{33,1},{2,34},{34,2},{3,35},{35,3},{4,36},{36... | collective-permute-start | bytes 442376 | tf_op jit(solution)/shard_map/ppermute | solution.py:15
  15.8 2.3 %collective-permute-done = bf16[64,1152]{1,0:T(8,128)(2,1)S(1)} collective-permute-done((bf16[64,1152]{1,0:T(8,128)(2,1)S(1)}, bf16[64,1152]{1,0:T(8,128)(2,1)S(1)}, u32[]{:S(2)}, u32[]{:S(2)}) %collective-permute-start) | collective-permute-done | bytes 147488 | tf_op jit(solution)/shard_map/ppermute | solution.py:15
  20.4 3.5 %collective-permute-start.1 = (bf16[128,1152]{1,0:T(8,128)(2,1)}, bf16[128,1152]{1,0:T(8,128)(2,1)}, u32[]{:S(2)}, u32[]{:S(2)}) collective-permute-start(bf16[128,1152]{1,0:T(8,128)(2,1)} %pad_maximum_fusion), channel_id=1, source_target_pairs={{0,64},{64,128},{128,192},{192,256},{256,320},{320,384},{384,448},... | collective-permute-start | bytes 884744 | tf_op jit(solution)/shard_map/ppermute | solution.py:15
  23.9 3.8 %collective-permute-start.2 = (bf16[128,1152]{1,0:T(8,128)(2,1)}, bf16[128,1152]{1,0:T(8,128)(2,1)}, u32[]{:S(2)}, u32[]{:S(2)}) collective-permute-start(bf16[128,1152]{1,0:T(8,128)(2,1)} %pad_maximum_fusion), channel_id=1, source_target_pairs={{0,448},{64,0},{128,64},{192,128},{256,192},{320,256},{384,320},{4... | collective-permute-start | bytes 884744 | tf_op jit(solution)/shard_map/ppermute | solution.py:15
  29.1 3.3 %collective-permute-done.1 = bf16[128,1152]{1,0:T(8,128)(2,1)} collective-permute-done((bf16[128,1152]{1,0:T(8,128)(2,1)}, bf16[128,1152]{1,0:T(8,128)(2,1)}, u32[]{:S(2)}, u32[]{:S(2)}) %collective-permute-start.1) | collective-permute-done | bytes 294944 | tf_op jit(solution)/shard_map/ppermute | solution.py:15
  34.4 5.1 %collective-permute-start.4 = (bf16[128,1152]{1,0:T(8,128)(2,1)}, bf16[128,1152]{1,0:T(8,128)(2,1)S(1)}, u32[]{:S(2)}, u32[]{:S(2)}) collective-permute-start(bf16[128,1152]{1,0:T(8,128)(2,1)} %collective-permute-done.2), channel_id=1, source_target_pairs={{0,448},{64,0},{128,64},{192,128},{256,192},{320,256},{384,320},{4... | collective-permute-start | bytes 884744 | tf_op jit(solution)/shard_map/ppermute | solution.py:15
  45.1 5.3 %collective-permute-start.6 = (bf16[128,1152]{1,0:T(8,128)(2,1)S(1)}, bf16[128,1152]{1,0:T(8,128)(2,1)S(1)}, u32[]{:S(2)}, u32[]{:S(2)}) collective-permute-start(bf16[128,1152]{1,0:T(8,128)(2,1)S(1)} %collective-permute-done.4), channel_id=1, source_target_pairs={{0,448},{64,0},{128,64},{192,128},{256,192},{320,256},{384,320},{4... | collective-permute-start | bytes 884744 | tf_op jit(solution)/shard_map/ppermute | solution.py:15
  57.8 6.1 %collective-permute-done.7 = bf16[64,1152]{1,0:T(8,128)(2,1)S(1)} collective-permute-done((bf16[64,1152]{1,0:T(8,128)(2,1)S(1)}, bf16[64,1152]{1,0:T(8,128)(2,1)S(1)}, u32[]{:S(2)}, u32[]{:S(2)}) %collective-permute-start.7) | collective-permute-done | bytes 147488 | tf_op jit(solution)/shard_map/ppermute | solution.py:15
  64.7 2.6 %collective-permute-start.8 = (bf16[512,1152]{1,0:T(8,128)(2,1)}, bf16[512,1152]{1,0:T(8,128)(2,1)}, u32[]{:S(2)}, u32[]{:S(2)}) collective-permute-start(bf16[512,1152]{1,0:T(8,128)(2,1)} %get-tuple-element.32), channel_id=1, source_target_pairs={{0,1},{1,0},{2,3},{3,2},{4,5},{5,4},{6,7},{7,6},{8,9},{9,8},{10,11... | collective-permute-start | bytes 3538952 | tf_op jit(solution)/shard_map/ppermute | solution.py:15
  70.6 4.7 %collective-permute-done.12 = bf16[64,1152]{1,0:T(8,128)(2,1)} collective-permute-done((bf16[64,1152]{1,0:T(8,128)(2,1)}, bf16[64,1152]{1,0:T(8,128)(2,1)}, u32[]{:S(2)}, u32[]{:S(2)}) %collective-permute-start.12) | collective-permute-done | bytes 147488 | tf_op jit(solution)/shard_map/ppermute | solution.py:15
  79.2 2.4 %constant_dynamic-update-slice_fusion.4 = bf16[1024,1152]{1,0:T(8,128)(2,1)} fusion(bf16[1024,1152]{1,0:T(8,128)(2,1)} %get-tuple-element.33, bf16[512,1152]{1,0:T(8,128)(2,1)} %collective-permute-done.8), kind=kLoop, calls=%fused_computation.77 | loop fusion | bytes 2359296 | tf_op jit(solution)/shard_map/concatenate | solution.py:73
  83.8 4.4 %fusion.22 = bf16[1024,512]{1,0:T(8,128)(2,1)S(1)} fusion(f32[]{:T(128)} %bitcast.38, f32[]{:T(128)} %bitcast.37, s32[1024]{0:T(1024)S(1)} %get-tuple-element.51, s32[1024]{0:T(1024)S(1)} %get-tuple-element.52, f32[]{:T(128)S(6)} %neg.9, pred[1024]{0:T(1024)(128)(4,1)S(1)} %get-tuple-element.54, pred[1024]{0:T(1024)(128)(4,1)S(1)} %get-tuple-element.53, ...), kind=kOutput, calls=%fused_computation.31 | convolution fusion | flops 1222180864 | bytes 4603917 | tf_op jit(solution)/shard_map/dot_general | solution.py:78
  88.1 3.2 %fusion.13 = (f32[512]{0:T(512)S(1)}, f32[1152,512]{1,0:T(8,128)S(1)}) fusion(bf16[512,1152]{0,1:T(8,128)(2,1)S(1)} %collective-permute-done.9, f32[512]{0:T(512)S(1)} %add_rsqrt_fusion.1, bf16[1024,512]{1,0:T(8,128)(2,1)S(1)} %fusion.22, bf16[1024,1152]{1,0:T(8,128)(2,1)} %constant_dynamic-update-slice_fusion.4, f32[1024]{0:T(1024)S(1)} %add_rsqrt_fusion), kind=kOutput, calls=%fused_computation.21 | convolution fusion | flops 1213857280 | bytes 6955008 | tf_op jit(solution)/shard_map/dot_general | solution.py:90
  92.9 6.9 %all-to-all-start = ((bf16[8,144,512]{2,1,0:T(8,128)(2,1)}), bf16[8,144,512]{2,1,0:T(8,128)(2,1)}, u32[]{:S(2)}, u32[]{:S(2)}) async-start(bf16[8,144,512]{2,1,0:T(8,128)(2,1)} %bitcast.3), calls=%async_computation | async-start | bytes 2359296 | tf_op jit(solution)/shard_map/all_to_all | solution.py:45
  99.8 3.5 %fusion.3 = (f32[1024]{0:T(1024)S(1)}, f32[1024,1152]{1,0:T(8,128)S(1)}) fusion(bf16[1024,1152]{1,0:T(8,128)(2,1)} %constant_dynamic-update-slice_fusion.4, f32[1024]{0:T(1024)S(1)} %add_rsqrt_fusion, bf16[1024,512]{1,0:T(8,128)(2,1)S(1)} %fusion.22, bf16[512,1152]{0,1:T(8,128)(2,1)S(1)} %collective-permute-done.9, f32[512]{0:T(512)S(1)} %add_rsqrt_fusion.1), kind=kOutput, calls=%fused_computation.6 | convolution fusion | flops 1214446592 | bytes 9316352 | tf_op jit(solution)/shard_map/dot_general | solution.py:100
  104.8 7.0 %convolution_convert_fusion = bf16[1152,1152]{1,0:T(8,128)(2,1)} fusion(bf16[1024,1152]{1,0:T(8,128)(2,1)S(1)} %constant_dynamic-update-slice_fusion.13, f32[1024,1152]{1,0:T(8,128)S(1)} %get-tuple-element.47, bf16[1024,1152]{1,0:T(8,128)(2,1)} %constant_dynamic-update-slice_fusion.4, f32[1024]{0:T(1024)S(1)} %get-tuple-element.46, f32[1024]{0:T(1024)S(1)} %add_rsqrt_fusion), kind=kOutput, calls=%fused_computation | convolution fusion | flops 2726313984 | bytes 12099584 | tf_op jit(solution)/shard_map/dot_general | solution.py:102
  115.2 3.2 %collective-permute-done.14 = bf16[8,72,1152]{2,1,0:T(8,128)(2,1)} collective-permute-done((bf16[8,72,1152]{2,1,0:T(8,128)(2,1)S(1)}, bf16[8,72,1152]{2,1,0:T(8,128)(2,1)}, u32[]{:S(2)}, u32[]{:S(2)}) %collective-permute-start.14) | collective-permute-done | bytes 1327136 | tf_op jit(solution)/shard_map/ppermute | solution.py:15
  118.3 3.1 %fusion.12 = bf16[8,72,1152]{2,1,0:T(8,128)(2,1)} fusion(bf16[8,72,1152]{2,1,0:T(8,128)(2,1)} %collective-permute-done.14, bf16[8,2,72,1152]{3,2,1,0:T(8,128)(2,1)} %bitcast.7, s32[]{:T(128)S(6)} %select_n.25), kind=kLoop, calls=%fused_computation.20 | loop fusion | flops 2654208 | bytes 3981316 | tf_op jit(solution)/shard_map/convert_element_type | solution.py:106
  121.4 5.7 %all-to-all-start.1 = ((bf16[8,72,1152]{2,1,0:T(8,128)(2,1)}), bf16[8,72,1152]{2,1,0:T(8,128)(2,1)S(1)}, u32[]{:S(2)}, u32[]{:S(2)}) async-start(bf16[8,72,1152]{2,1,0:T(8,128)(2,1)} %fusion.12), calls=%async_computation.1 | async-start | bytes 2654208 | tf_op jit(solution)/shard_map/all_to_all | solution.py:45
  129.3 6.9 %collective-permute-start.11 = (f32[72,512]{1,0:T(8,128)S(1)}, f32[72,512]{1,0:T(8,128)S(1)}, u32[]{:S(2)}, u32[]{:S(2)}) collective-permute-start(f32[72,512]{1,0:T(8,128)S(1)} %get-tuple-element.4), channel_id=1, source_target_pairs={{0,1},{1,17},{16,0},{17,16},{2,3},{3,19},{18,2},{19,18},{4,5},{5,2... | collective-permute-start | bytes 442376 | tf_op jit(solution)/shard_map/ppermute | solution.py:96
  136.2 3.0 %collective-permute-done.11 = f32[72,512]{1,0:T(8,128)S(1)} collective-permute-done((f32[72,512]{1,0:T(8,128)S(1)}, f32[72,512]{1,0:T(8,128)S(1)}, u32[]{:S(2)}, u32[]{:S(2)}) %collective-permute-start.11) | collective-permute-done | bytes 147488 | tf_op jit(solution)/shard_map/ppermute | solution.py:96
  139.6 7.2 %all-to-all-done.1 = bf16[8,72,1152]{2,1,0:T(8,128)(2,1)S(1)} async-done(((bf16[8,72,1152]{2,1,0:T(8,128)(2,1)}), bf16[8,72,1152]{2,1,0:T(8,128)(2,1)S(1)}, u32[]{:S(2)}, u32[]{:S(2)}) %all-to-all-start.1) | async-done | bytes 1327136 | tf_op jit(solution)/shard_map/all_to_all | solution.py:45
  147.9 24.4 %all_to_all.20 = bf16[8,144,144]{1,2,0:T(8,128)(2,1)S(1)} all-to-all(bf16[8,144,144]{1,2,0:T(8,128)(2,1)S(1)} %copy.11), channel_id=1, replica_groups=mesh['y'=8,'a'=2,'b'=2,'zl'=2,'x'=4,'c'=2] {'y'}, dimensions={0} | all-to-all | bytes 663552 | tf_op jit(solution)/shard_map/all_to_all | solution.py:51
  172.5 18.7 %all_to_all.21 = f32[4,36,144]{2,1,0:T(8,128)S(1)} all-to-all(f32[4,36,144]{2,1,0:T(8,128)S(1)} %reshape.71), channel_id=1, replica_groups=mesh['y'=8,'a'=2,'b'=2,'zl'=2,'x'=4,'c'=2] {'a','b'}, dimensions={0} | all-to-all | bytes 165888 | tf_op jit(solution)/shard_map/all_to_all | solution.py:53
  (59 shorter events, 42.3 us)
Async XLA Ops:
  0.6 138.6 %copy-start = (bf16[512,1152]{1,0:T(8,128)(2,1)S(1)}, bf16[512,1152]{1,0:T(8,128)(2,1)}, u32[]{:S(2)}) copy-start(bf16[512,1152]{1,0:T(8,128)(2,1)} %param.8) | copy-start | bytes 3538948
  0.6 27.1 %copy-start.1 = (bf16[512,1152]{1,0:T(8,128)(2,1)S(1)}, bf16[512,1152]{1,0:T(8,128)(2,1)}, u32[]{:S(2)}) copy-start(bf16[512,1152]{1,0:T(8,128)(2,1)} %param.6) | copy-start | bytes 3538948
  3.2 14.9 %collective-permute-start = (bf16[64,1152]{1,0:T(8,128)(2,1)S(1)}, bf16[64,1152]{1,0:T(8,128)(2,1)S(1)}, u32[]{:S(2)}, u32[]{:S(2)}) collective-permute-start(bf16[64,1152]{1,0:T(8,128)(2,1)S(1)} %pad_maximum_fusion.1), channel_id=1, source_target_pairs={{0,32},{32,0},{1,33},{33,1},{2,34},{34,2},{3,35},{35,3},{4,36},{36... | collective-permute-start | bytes 442376 | tf_op jit(solution)/shard_map/ppermute | solution.py:15
  20.4 12.0 %collective-permute-start.1 = (bf16[128,1152]{1,0:T(8,128)(2,1)}, bf16[128,1152]{1,0:T(8,128)(2,1)}, u32[]{:S(2)}, u32[]{:S(2)}) collective-permute-start(bf16[128,1152]{1,0:T(8,128)(2,1)} %pad_maximum_fusion), channel_id=1, source_target_pairs={{0,64},{64,128},{128,192},{192,256},{256,320},{320,384},{384,448},... | collective-permute-start | bytes 884744 | tf_op jit(solution)/shard_map/ppermute | solution.py:15
  23.9 10.5 %collective-permute-start.2 = (bf16[128,1152]{1,0:T(8,128)(2,1)}, bf16[128,1152]{1,0:T(8,128)(2,1)}, u32[]{:S(2)}, u32[]{:S(2)}) collective-permute-start(bf16[128,1152]{1,0:T(8,128)(2,1)} %pad_maximum_fusion), channel_id=1, source_target_pairs={{0,448},{64,0},{128,64},{192,128},{256,192},{320,256},{384,320},{4... | collective-permute-start | bytes 884744 | tf_op jit(solution)/shard_map/ppermute | solution.py:15
  28.4 50.5 %collective-permute-start.9 = (bf16[512,1152]{0,1:T(8,128)(2,1)S(1)}, bf16[512,1152]{0,1:T(8,128)(2,1)S(1)}, u32[]{:S(2)}, u32[]{:S(2)}) collective-permute-start(bf16[512,1152]{0,1:T(8,128)(2,1)S(1)} %copy.10), channel_id=1, source_target_pairs={{0,0},{1,16},{16,1},{17,17},{2,2},{3,18},{18,3},{19,19},{4,4},{5,2... | collective-permute-start | bytes 3538952 | tf_op jit(solution)/shard_map/ppermute | solution.py:67
  32.5 10.7 %collective-permute-start.3 = (bf16[128,1152]{1,0:T(8,128)(2,1)}, bf16[128,1152]{1,0:T(8,128)(2,1)S(1)}, u32[]{:S(2)}, u32[]{:S(2)}) collective-permute-start(bf16[128,1152]{1,0:T(8,128)(2,1)} %collective-permute-done.1), channel_id=1, source_target_pairs={{0,64},{64,128},{128,192},{192,256},{256,320},{320,384},{384,448},... | collective-permute-start | bytes 884744 | tf_op jit(solution)/shard_map/ppermute | solution.py:15
  34.4 10.7 %collective-permute-start.4 = (bf16[128,1152]{1,0:T(8,128)(2,1)}, bf16[128,1152]{1,0:T(8,128)(2,1)S(1)}, u32[]{:S(2)}, u32[]{:S(2)}) collective-permute-start(bf16[128,1152]{1,0:T(8,128)(2,1)} %collective-permute-done.2), channel_id=1, source_target_pairs={{0,448},{64,0},{128,64},{192,128},{256,192},{320,256},{384,320},{4... | collective-permute-start | bytes 884744 | tf_op jit(solution)/shard_map/ppermute | solution.py:15
  43.2 11.0 %collective-permute-start.5 = (bf16[128,1152]{1,0:T(8,128)(2,1)S(1)}, bf16[128,1152]{1,0:T(8,128)(2,1)S(1)}, u32[]{:S(2)}, u32[]{:S(2)}) collective-permute-start(bf16[128,1152]{1,0:T(8,128)(2,1)S(1)} %collective-permute-done.3), channel_id=1, source_target_pairs={{0,64},{64,128},{128,192},{192,256},{256,320},{320,384},{384,448},... | collective-permute-start | bytes 884744 | tf_op jit(solution)/shard_map/ppermute | solution.py:15
  45.1 11.8 %collective-permute-start.6 = (bf16[128,1152]{1,0:T(8,128)(2,1)S(1)}, bf16[128,1152]{1,0:T(8,128)(2,1)S(1)}, u32[]{:S(2)}, u32[]{:S(2)}) collective-permute-start(bf16[128,1152]{1,0:T(8,128)(2,1)S(1)} %collective-permute-done.4), channel_id=1, source_target_pairs={{0,448},{64,0},{128,64},{192,128},{256,192},{320,256},{384,320},{4... | collective-permute-start | bytes 884744 | tf_op jit(solution)/shard_map/ppermute | solution.py:15
  55.0 9.0 %collective-permute-start.7 = (bf16[64,1152]{1,0:T(8,128)(2,1)S(1)}, bf16[64,1152]{1,0:T(8,128)(2,1)S(1)}, u32[]{:S(2)}, u32[]{:S(2)}) collective-permute-start(bf16[64,1152]{1,0:T(8,128)(2,1)S(1)} %get-tuple-element.15), channel_id=1, source_target_pairs={{0,64},{64,128},{128,192},{192,256},{256,320},{320,384},{384,448},... | collective-permute-start | bytes 442376 | tf_op jit(solution)/shard_map/ppermute | solution.py:15
  64.7 14.4 %collective-permute-start.8 = (bf16[512,1152]{1,0:T(8,128)(2,1)}, bf16[512,1152]{1,0:T(8,128)(2,1)}, u32[]{:S(2)}, u32[]{:S(2)}) collective-permute-start(bf16[512,1152]{1,0:T(8,128)(2,1)} %get-tuple-element.32), channel_id=1, source_target_pairs={{0,1},{1,0},{2,3},{3,2},{4,5},{5,4},{6,7},{7,6},{8,9},{9,8},{10,11... | collective-permute-start | bytes 3538952 | tf_op jit(solution)/shard_map/ppermute | solution.py:15
  67.3 8.0 %collective-permute-start.12 = (bf16[64,1152]{1,0:T(8,128)(2,1)}, bf16[64,1152]{1,0:T(8,128)(2,1)}, u32[]{:S(2)}, u32[]{:S(2)}) collective-permute-start(bf16[64,1152]{1,0:T(8,128)(2,1)} %get-tuple-element.10), channel_id=1, source_target_pairs={{0,448},{64,0},{128,64},{192,128},{256,192},{320,256},{384,320},{4... | collective-permute-start | bytes 442376 | tf_op jit(solution)/shard_map/ppermute | solution.py:15
  76.9 26.4 %collective-permute-start.13 = (bf16[512,1152]{1,0:T(8,128)(2,1)}, bf16[512,1152]{1,0:T(8,128)(2,1)}, u32[]{:S(2)}, u32[]{:S(2)}) collective-permute-start(bf16[512,1152]{1,0:T(8,128)(2,1)} %get-tuple-element.40), channel_id=1, source_target_pairs={{0,1},{1,0},{2,3},{3,2},{4,5},{5,4},{6,7},{7,6},{8,9},{9,8},{10,11... | collective-permute-start | bytes 3538952 | tf_op jit(solution)/shard_map/ppermute | solution.py:15
  92.9 28.6 %all-to-all-start = ((bf16[8,144,512]{2,1,0:T(8,128)(2,1)}), bf16[8,144,512]{2,1,0:T(8,128)(2,1)}, u32[]{:S(2)}, u32[]{:S(2)}) async-start(bf16[8,144,512]{2,1,0:T(8,128)(2,1)} %bitcast.3), calls=%async_computation | async-start | bytes 2359296 | tf_op jit(solution)/shard_map/all_to_all | solution.py:45
  99.8 3.6 %copy-start.2 = (bf16[1024,1152]{1,0:T(8,128)(2,1)S(1)}, bf16[1024,1152]{1,0:T(8,128)(2,1)}, u32[]{:S(2)}) copy-start(bf16[1024,1152]{1,0:T(8,128)(2,1)} %get-tuple-element.41) | copy-start | bytes 7077892
  113.3 5.1 %collective-permute-start.14 = (bf16[8,72,1152]{2,1,0:T(8,128)(2,1)S(1)}, bf16[8,72,1152]{2,1,0:T(8,128)(2,1)}, u32[]{:S(2)}, u32[]{:S(2)}) collective-permute-start(bf16[8,72,1152]{2,1,0:T(8,128)(2,1)S(1)} %dynamic-slice_bitcast_fusion), channel_id=1, source_target_pairs={{0,1},{1,0},{2,3},{3,2},{4,5},{5,4},{6,7},{7,6},{8,9},{9,8},{10,11... | collective-permute-start | bytes 3981320 | tf_op jit(solution)/shard_map/ppermute | solution.py:15
  121.4 25.3 %all-to-all-start.1 = ((bf16[8,72,1152]{2,1,0:T(8,128)(2,1)}), bf16[8,72,1152]{2,1,0:T(8,128)(2,1)S(1)}, u32[]{:S(2)}, u32[]{:S(2)}) async-start(bf16[8,72,1152]{2,1,0:T(8,128)(2,1)} %fusion.12), calls=%async_computation.1 | async-start | bytes 2654208 | tf_op jit(solution)/shard_map/all_to_all | solution.py:45
  128.6 7.6 %collective-permute-start.10 = (f32[72,512]{1,0:T(8,128)S(1)}, f32[72,512]{1,0:T(8,128)S(1)}, u32[]{:S(2)}, u32[]{:S(2)}) collective-permute-start(f32[72,512]{1,0:T(8,128)S(1)} %get-tuple-element.5), channel_id=1, source_target_pairs={{0,0},{1,16},{16,1},{17,17},{2,2},{3,18},{18,3},{19,19},{4,4},{5,2... | collective-permute-start | bytes 442376 | tf_op jit(solution)/shard_map/ppermute | solution.py:95
  129.3 9.9 %collective-permute-start.11 = (f32[72,512]{1,0:T(8,128)S(1)}, f32[72,512]{1,0:T(8,128)S(1)}, u32[]{:S(2)}, u32[]{:S(2)}) collective-permute-start(f32[72,512]{1,0:T(8,128)S(1)} %get-tuple-element.4), channel_id=1, source_target_pairs={{0,1},{1,17},{16,0},{17,16},{2,3},{3,19},{18,2},{19,18},{4,5},{5,2... | collective-permute-start | bytes 442376 | tf_op jit(solution)/shard_map/ppermute | solution.py:96

commit v3 on v2

v3 whole, which is shorter than its diff:
```python
import jax
import jax.numpy as jnp
from jax import lax
from jax.sharding import Mesh, PartitionSpec as P

SIZES = (8, 2, 2, 2, 4, 2)
NAMES = ("y", "a", "b", "zl", "x", "c")
DP = ("y", "a", "b")
MP = ("zl", "x", "c")
ROW = ("zl", "x")


def shifted(value, axis, steps):
    count = lax.axis_size(axis)
    return lax.ppermute(value, axis, [(s, (s + steps) % count) for s in range(count)])


def normalize(rows, axis=-1):
    wide = rows.astype(jnp.float32)
    factor = lax.rsqrt(jnp.sum(wide * wide, axis=axis, keepdims=True) + 1e-06)
    return (wide * factor, factor)


def unit_back(direction, unit, factor, axis=-1):
    return (direction - unit * jnp.sum(unit * direction, axis=axis, keepdims=True)) * factor


def gather(text, feat):
    chunk = jnp.concatenate([text, shifted(text, "a", 1), feat, shifted(feat, "a", 1)], axis=0)
    chunks = [chunk]
    up = down = chunk
    for _ in range(3):
        up, down = shifted(up, "y", 1), shifted(down, "y", -1)
        chunks += [up, down]
    half = chunk.shape[0] // 2
    last_text, last_feat = shifted(up[:half], "y", 1), shifted(down[half:], "y", -1)
    texts = jnp.concatenate([piece[:half] for piece in chunks] + [last_text], axis=0)
    feats = jnp.concatenate([piece[half:] for piece in chunks] + [last_feat], axis=0)
    return chunk, texts, feats


def other_block(image_emb, after):
    core = lax.axis_index("c")
    half = image_emb.shape[0] // 2
    piece = lax.dynamic_slice_in_dim(image_emb, core * half, half, 0)
    piece, _ = lax.optimization_barrier((piece, after))
    mine = shifted(piece, "b", 1)
    theirs = shifted(mine, "c", 1)
    return [jnp.where(core == 0, mine, theirs), jnp.where(core == 0, theirs, mine)]


def sum_over_mp_row(full):
    core = lax.axis_index("c")
    slabs = full.reshape(8, 2, full.shape[0] // 16, full.shape[1])
    keep = lax.dynamic_index_in_dim(slabs, core, 1, keepdims=False).astype(jnp.float32)
    give = lax.dynamic_index_in_dim(slabs, 1 - core, 1, keepdims=False)
    both = (keep + shifted(give, "c", 1).astype(jnp.float32)).astype(jnp.bfloat16)
    got = lax.all_to_all(both, ROW, 0, 0, tiled=True)
    return jnp.sum(got.astype(jnp.float32), axis=0)


def sum_over_dp(parts):
    rows, cols = parts.shape
    own = rows // 32
    parts = parts.astype(jnp.bfloat16)
    main = parts[:, :128].reshape(32, own, 128)
    rest = parts[:, 128:].reshape(32, own * (cols - 128))
    rest = jnp.pad(rest, ((0, 0), (0, -rest.shape[1] % 128))).reshape(32, -1, 128)
    got = lax.all_to_all(jnp.concatenate([main, rest], axis=1), DP, 0, 0, tiled=True)
    total = jnp.sum(got.astype(jnp.float32), axis=0)
    tail = total[own:].reshape(-1)[: own * (cols - 128)].reshape(own, cols - 128)
    return jnp.concatenate([total[:own], tail], axis=1)


def local(image_emb, text_emb, image_feat, text_feat, logit_scale, logit_bias):
    column = lax.axis_index(MP)
    own_rows, width = text_emb.shape
    block = image_emb.shape[0]
    cols = width // 16
    scale = logit_scale[0]
    offset = logit_bias[0]

    own_feat = lax.dynamic_slice_in_dim(text_feat, column * own_rows, own_rows, 0)
    chunk, texts, feats = gather(text_emb, own_feat)
    images = jnp.concatenate([image_emb] + other_block(image_emb, chunk), axis=0)
    images_t = lax.optimization_barrier(images.T)

    image_unit, image_norm = normalize(images)
    image_low = image_unit.astype(jnp.bfloat16)
    image_unit_t, image_norm_t = normalize(images_t, 0)
    text_unit, text_norm = normalize(texts)
    text_low = text_unit.astype(jnp.bfloat16)
    rows = text_low.shape[0]
    logits = lax.dot_general(text_low, image_low, (((1,), (1,)), ((), ())), preferred_element_type=jnp.float32)
    row_ids = jnp.arange(rows, dtype=jnp.int32)[:, None]
    image_ids = jnp.arange(2 * block, dtype=jnp.int32)[None, :]
    match = (row_ids < own_rows) & (image_ids == column * own_rows + row_ids)
    sign = jnp.where(match, 1.0, -1.0).astype(jnp.float32)
    value = scale * logits + offset
    weights = (-scale * sign * jax.nn.sigmoid(-sign * value)).astype(jnp.bfloat16)

    image_dir = lax.dot_general(text_low, weights, (((0,), (0,)), ((), ())), preferred_element_type=jnp.float32)
    image_part = unit_back(image_dir, image_unit_t, image_norm_t, 0).astype(jnp.bfloat16)
    image_two = sum_over_mp_row(image_part)
    image_cols = image_two[:, :block] + shifted(image_two[:, block:], "b", 1)
    image_term = jnp.dot(image_cols.astype(jnp.bfloat16), image_feat, preferred_element_type=jnp.float32)

    text_dir = jnp.dot(weights, image_low, preferred_element_type=jnp.float32)
    text_part = unit_back(text_dir, text_unit, text_norm).astype(jnp.bfloat16)
    text_all = lax.dot_general(text_part, feats, (((0,), (0,)), ((), ())), preferred_element_type=jnp.float32)
    text_term = sum_over_mp_row(text_all.astype(jnp.bfloat16))

    own = sum_over_dp(jnp.concatenate([image_term, text_term], axis=0).T)
    return (own[:, :cols], own[:, cols:])


def solution(mesh):
    split = Mesh(mesh.devices.reshape(SIZES), NAMES)
    in_specs = (P(DP, None), P(DP + MP, None), P(DP, None), P(DP, None), P(), P())
    out_specs = (P(DP, MP), P(DP, MP))
    return jax.shard_map(local, mesh=split, in_specs=in_specs, out_specs=out_specs, check_vma=False)
```

time: 193 us -> 167 us (0.87)
  blocking collectives: 43.1 us -> 24 us
  matrix products: 18.5 us -> 9.64 us
  local copies, waits for them, and re-layouts: 21.1 us -> 15.8 us
  waiting for transfers between devices: 32 us -> 36.7 us
  starting transfers between devices: 63.6 us -> 66.3 us
  other arithmetic: 11.5 us -> 9.33 us
    all_to_all x2 -> x1, blocking collectives: 43.1 us -> 24 us  [sum_over_dp(): lax.all_to_all(jnp.concatenate([main, rest], axis=1), DP, 0, 0, tiled=True)]
    ppermute x12 -> x15, starting transfers between devices: 42.7 us -> 56.5 us  [shifted(): lax.ppermute(value, axis, [(s, (s + steps) % count) for s in range(count)])]
    ppermute x3 -> x0, starting transfers between devices: 8.31 us -> none  [the longest x1 6.9 us: local(): cross = lax.ppermute(cross, ('b', 'c'), [(0, 1), (1, 3), (2, 0), (3, 2)])]
    ppermute x12 -> x15, waiting for transfers between devices: 21.8 us -> 27.6 us  [shifted(): lax.ppermute(value, axis, [(s, (s + steps) % count) for s in range(count)])]
    concatenate x2 -> x0, local copies, waits for them, and re-layouts: 3.82 us -> none  [the longest x1 2.38 us: local(): texts = jnp.concatenate([text_here, text_there], axis=0)]
    dot_general x1, matrix products: 7 us -> 3.53 us  [local(): lax.dot_general(text_part, feats, (((0,), (0,)), ((), ())), preferred_ele...]
    ppermute x3 -> x0, waiting for transfers between devices: 3 us -> none  [the longest x1 3 us: local(): cross = lax.ppermute(cross, ('b', 'c'), [(0, 1), (1, 3), (2, 0), (3, 2)])]
    all_to_all x2, starting transfers between devices: 12.6 us -> 9.75 us  [sum_over_mp_row(): got = lax.all_to_all(both, ROW, 0, 0, tiled=True)]
  transfers between devices with their start and end apart: 17 -> 17, of which waited for: 8 -> 8; matrix products, arithmetic and copies ran while one was open for 23% -> 16% of each run, Pallas kernels for 0% -> 0%
where the time goes in v3:
time: 167 us; the launch traced here: 164 us
  starting transfers between devices  66.3 us (40%)
  waiting for transfers between devices  36.7 us (22%)
  blocking collectives  24 us (14%)
  local copies, waits for them, and re-layouts  15.8 us (9%)
  matrix products  9.64 us (6%)
  other arithmetic  9.33 us (6%)
  between operations  2.3 us (1%)
    ppermute x15, starting transfers between devices, shifted(): lax.ppermute(value, axis, [(s, (s + steps) % count) for s in range(count)])  56.5 us
    ppermute x15, waiting for transfers between devices, shifted(): lax.ppermute(value, axis, [(s, (s + steps) % count) for s in range(count)])  27.6 us
    all_to_all x1, blocking collectives, sum_over_dp(): lax.all_to_all(jnp.concatenate([main, rest], axis=1), DP, 0, 0, tiled=True)  24 us
    unnamed x18, local copies, waits for them, and re-layouts  11 us
    all_to_all x2, starting transfers between devices, sum_over_mp_row(): got = lax.all_to_all(both, ROW, 0, 0, tiled=True)  9.75 us
    all_to_all x2, waiting for transfers between devices, sum_over_mp_row(): got = lax.all_to_all(both, ROW, 0, 0, tiled=True)  9.1 us
    dot_general x1, matrix products, local(): lax.dot_general(text_part, feats, (((0,), (0,)), ((), ())), preferred_ele...  3.53 us
  transfers between devices with their start and end apart: 17, of which 8 were waited for; matrix products, arithmetic and copies ran while one was open for 16% of the time, Pallas kernels for 0%

profile of v3, /device:TPU:6, one launch (start us, length us, event | category | flops | bytes accessed | tf_op | source)
XLA Modules:
  0.0 164.1 jit_solution(2474363820361371762)
XLA Ops:
  2.3 10.9 %collective-permute-start.1 = (bf16[32,1152]{1,0:T(8,128)(2,1)}, bf16[32,1152]{1,0:T(8,128)(2,1)}, u32[]{:S(2)}, u32[]{:S(2)}) collective-permute-start(bf16[32,1152]{1,0:T(8,128)(2,1)} %get-tuple-element.5), channel_id=1, source_target_pairs={{0,32},{32,0},{1,33},{33,1},{2,34},{34,2},{3,35},{35,3},{4,36},{36... | collective-permute-start | bytes 221192 | tf_op jit(solution)/shard_map/ppermute | solution.py:15
  13.2 1.9 %collective-permute-start = (bf16[32,1152]{1,0:T(8,128)(2,1)}, bf16[32,1152]{1,0:T(8,128)(2,1)}, u32[]{:S(2)}, u32[]{:S(2)}) collective-permute-start(bf16[32,1152]{1,0:T(8,128)(2,1)} %param.7), channel_id=1, source_target_pairs={{0,32},{32,0},{1,33},{33,1},{2,34},{34,2},{3,35},{35,3},{4,36},{36... | collective-permute-start | bytes 221192 | tf_op jit(solution)/shard_map/ppermute | solution.py:15
  19.8 4.2 %collective-permute-done = bf16[32,1152]{1,0:T(8,128)(2,1)} collective-permute-done((bf16[32,1152]{1,0:T(8,128)(2,1)}, bf16[32,1152]{1,0:T(8,128)(2,1)}, u32[]{:S(2)}, u32[]{:S(2)}) %collective-permute-start) | collective-permute-done | bytes 73760 | tf_op jit(solution)/shard_map/ppermute | solution.py:15
  25.1 3.5 %collective-permute-start.2 = (bf16[128,1152]{1,0:T(8,128)(2,1)S(1)}, bf16[128,1152]{1,0:T(8,128)(2,1)S(1)}, u32[]{:S(2)}, u32[]{:S(2)}) collective-permute-start(bf16[128,1152]{1,0:T(8,128)(2,1)S(1)} %pad_maximum_fusion.2), channel_id=1, source_target_pairs={{0,64},{64,128},{128,192},{192,256},{256,320},{320,384},{384,448},... | collective-permute-start | bytes 884744 | tf_op jit(solution)/shard_map/ppermute | solution.py:15
  28.6 3.8 %collective-permute-start.3 = (bf16[128,1152]{1,0:T(8,128)(2,1)S(1)}, bf16[128,1152]{1,0:T(8,128)(2,1)S(1)}, u32[]{:S(2)}, u32[]{:S(2)}) collective-permute-start(bf16[128,1152]{1,0:T(8,128)(2,1)S(1)} %pad_maximum_fusion.2), channel_id=1, source_target_pairs={{0,448},{64,0},{128,64},{192,128},{256,192},{320,256},{384,320},{4... | collective-permute-start | bytes 884744 | tf_op jit(solution)/shard_map/ppermute | solution.py:15
  32.4 5.0 %collective-permute-start.9 = (bf16[256,1152]{0,1:T(8,128)(2,1)}, bf16[256,1152]{0,1:T(8,128)(2,1)S(1)}, u32[]{:S(2)}, u32[]{:S(2)}) collective-permute-start(bf16[256,1152]{0,1:T(8,128)(2,1)} %constant_dynamic-slice_fusion), channel_id=1, source_target_pairs={{0,16},{16,0},{1,17},{17,1},{2,18},{18,2},{3,19},{19,3},{4,20},{20... | collective-permute-start | bytes 1769480 | tf_op jit(solution)/shard_map/ppermute | solution.py:15
  39.8 2.0 %collective-permute-start.4 = (bf16[128,1152]{1,0:T(8,128)(2,1)S(1)}, bf16[128,1152]{1,0:T(8,128)(2,1)S(1)}, u32[]{:S(2)}, u32[]{:S(2)}) collective-permute-start(bf16[128,1152]{1,0:T(8,128)(2,1)S(1)} %collective-permute-done.2), channel_id=1, source_target_pairs={{0,64},{64,128},{128,192},{192,256},{256,320},{320,384},{384,448},... | collective-permute-start | bytes 884744 | tf_op jit(solution)/shard_map/ppermute | solution.py:15
  41.8 5.0 %collective-permute-start.5 = (bf16[128,1152]{1,0:T(8,128)(2,1)S(1)}, bf16[128,1152]{1,0:T(8,128)(2,1)S(1)}, u32[]{:S(2)}, u32[]{:S(2)}) collective-permute-start(bf16[128,1152]{1,0:T(8,128)(2,1)S(1)} %collective-permute-done.3), channel_id=1, source_target_pairs={{0,448},{64,0},{128,64},{192,128},{256,192},{320,256},{384,320},{4... | collective-permute-start | bytes 884744 | tf_op jit(solution)/shard_map/ppermute | solution.py:15
  49.6 1.9 %collective-permute-start.6 = (bf16[128,1152]{1,0:T(8,128)(2,1)S(1)}, bf16[128,1152]{1,0:T(8,128)(2,1)S(1)}, u32[]{:S(2)}, u32[]{:S(2)}) collective-permute-start(bf16[128,1152]{1,0:T(8,128)(2,1)S(1)} %collective-permute-done.4), channel_id=1, source_target_pairs={{0,64},{64,128},{128,192},{192,256},{256,320},{320,384},{384,448},... | collective-permute-start | bytes 884744 | tf_op jit(solution)/shard_map/ppermute | solution.py:15
  51.5 5.1 %collective-permute-start.7 = (bf16[128,1152]{1,0:T(8,128)(2,1)S(1)}, bf16[128,1152]{1,0:T(8,128)(2,1)S(1)}, u32[]{:S(2)}, u32[]{:S(2)}) collective-permute-start(bf16[128,1152]{1,0:T(8,128)(2,1)S(1)} %collective-permute-done.5), channel_id=1, source_target_pairs={{0,448},{64,0},{128,64},{192,128},{256,192},{320,256},{384,320},{4... | collective-permute-start | bytes 884744 | tf_op jit(solution)/shard_map/ppermute | solution.py:15
  56.7 5.4 %collective-permute-done.9 = bf16[256,1152]{0,1:T(8,128)(2,1)S(1)} collective-permute-done((bf16[256,1152]{0,1:T(8,128)(2,1)}, bf16[256,1152]{0,1:T(8,128)(2,1)S(1)}, u32[]{:S(2)}, u32[]{:S(2)}) %collective-permute-start.9) | collective-permute-done | bytes 589856 | tf_op jit(solution)/shard_map/ppermute | solution.py:15
  62.0 1.9 %collective-permute-start.10 = (bf16[256,1152]{0,1:T(8,128)(2,1)S(1)}, bf16[256,1152]{0,1:T(8,128)(2,1)S(1)}, u32[]{:S(2)}, u32[]{:S(2)}) collective-permute-start(bf16[256,1152]{0,1:T(8,128)(2,1)S(1)} %collective-permute-done.9), channel_id=1, source_target_pairs={{0,1},{1,0},{2,3},{3,2},{4,5},{5,4},{6,7},{7,6},{8,9},{9,8},{10,11... | collective-permute-start | bytes 1769480 | tf_op jit(solution)/shard_map/ppermute | solution.py:15
  68.7 5.1 %collective-permute-start.13 = (bf16[64,1152]{1,0:T(8,128)(2,1)S(1)}, bf16[64,1152]{1,0:T(8,128)(2,1)S(1)}, u32[]{:S(2)}, u32[]{:S(2)}) collective-permute-start(bf16[64,1152]{1,0:T(8,128)(2,1)S(1)} %get-tuple-element.13), channel_id=1, source_target_pairs={{0,448},{64,0},{128,64},{192,128},{256,192},{320,256},{384,320},{4... | collective-permute-start | bytes 442376 | tf_op jit(solution)/shard_map/ppermute | solution.py:15
  77.2 2.4 %fusion.20 = bf16[512,1024]{1,0:T(8,128)(2,1)S(1)} fusion(f32[1024]{0:T(1024)S(1)} %add_rsqrt_fusion.1, f32[]{:T(128)} %bitcast.25, f32[]{:T(128)} %bitcast.24, s32[512]{0:T(512)S(1)} %iota_add_fusion, f32[]{:T(128)S(6)} %neg.9, pred[512]{0:T(512)(128)(4,1)S(1)} %iota_compare_fusion.1, bf16[512,1152]{1,0:T(8,128)(2,1)S(1)} %constant_dynamic-update-slice_fusion, ...), kind=kOutput, calls=%fused_computation.34 | convolution fusion | flops 1225981952 | bytes 4596236 | tf_op jit(solution)/shard_map/dot_general | solution.py:94
  82.5 2.2 %collective-permute-start.11 = (bf16[8,72,1024]{2,1,0:T(8,128)(2,1)S(1)}, bf16[8,72,1024]{2,1,0:T(8,128)(2,1)S(1)}, u32[]{:S(2)}, u32[]{:S(2)}) collective-permute-start(bf16[8,72,1024]{2,1,0:T(8,128)(2,1)S(1)} %dynamic-slice_bitcast_fusion.1), channel_id=1, source_target_pairs={{0,1},{1,0},{2,3},{3,2},{4,5},{5,4},{6,7},{7,6},{8,9},{9,8},{10,11... | collective-permute-start | bytes 3538952 | tf_op jit(solution)/shard_map/ppermute | solution.py:15
  86.5 3.5 %convolution_convert_fusion = bf16[1152,1152]{1,0:T(8,128)(2,1)} fusion(bf16[512,1152]{1,0:T(8,128)(2,1)S(1)} %constant_dynamic-update-slice_fusion.4, f32[512,1152]{1,0:T(8,128)S(1)} %get-tuple-element.23, bf16[512,1152]{1,0:T(8,128)(2,1)S(1)} %constant_dynamic-update-slice_fusion, f32[512]{0:T(512)S(1)} %get-tuple-element.22, f32[512]{0:T(512)S(1)} %add_rsqrt_fusion.2), kind=kOutput, calls=%fused_computation | convolution fusion | flops 1363820544 | bytes 7376896 | tf_op jit(solution)/shard_map/dot_general | solution.py:110
  91.5 4.8 %all-to-all-start = ((bf16[8,72,1024]{2,1,0:T(8,128)(2,1)}), bf16[8,72,1024]{2,1,0:T(8,128)(2,1)S(1)}, u32[]{:S(2)}, u32[]{:S(2)}) async-start(bf16[8,72,1024]{2,1,0:T(8,128)(2,1)} %fusion.18), calls=%async_computation | async-start | bytes 2359296 | tf_op jit(solution)/shard_map/all_to_all | solution.py:58
  97.9 1.9 %collective-permute-start.14 = (bf16[8,72,1152]{2,1,0:T(8,128)(2,1)S(1)}, bf16[8,72,1152]{2,1,0:T(8,128)(2,1)S(1)}, u32[]{:S(2)}, u32[]{:S(2)}) collective-permute-start(bf16[8,72,1152]{2,1,0:T(8,128)(2,1)S(1)} %dynamic-slice_bitcast_fusion), channel_id=1, source_target_pairs={{0,1},{1,0},{2,3},{3,2},{4,5},{5,4},{6,7},{7,6},{8,9},{9,8},{10,11... | collective-permute-start | bytes 3981320 | tf_op jit(solution)/shard_map/ppermute | solution.py:15
  99.8 3.0 %collective-permute-done.14 = bf16[8,72,1152]{2,1,0:T(8,128)(2,1)S(1)} collective-permute-done((bf16[8,72,1152]{2,1,0:T(8,128)(2,1)S(1)}, bf16[8,72,1152]{2,1,0:T(8,128)(2,1)S(1)}, u32[]{:S(2)}, u32[]{:S(2)}) %collective-permute-start.14) | collective-permute-done | bytes 1327136 | tf_op jit(solution)/shard_map/ppermute | solution.py:15
  104.3 7.6 %all-to-all-done = bf16[8,72,1024]{2,1,0:T(8,128)(2,1)S(1)} async-done(((bf16[8,72,1024]{2,1,0:T(8,128)(2,1)}), bf16[8,72,1024]{2,1,0:T(8,128)(2,1)S(1)}, u32[]{:S(2)}, u32[]{:S(2)}) %all-to-all-start) | async-done | bytes 1179680 | tf_op jit(solution)/shard_map/all_to_all | solution.py:58
  112.8 5.0 %all-to-all-start.1 = ((bf16[8,72,1152]{2,1,0:T(8,128)(2,1)}), bf16[8,72,1152]{2,1,0:T(8,128)(2,1)S(1)}, u32[]{:S(2)}, u32[]{:S(2)}) async-start(bf16[8,72,1152]{2,1,0:T(8,128)(2,1)} %fusion.12), calls=%async_computation.1 | async-start | bytes 2654208 | tf_op jit(solution)/shard_map/all_to_all | solution.py:58
  119.3 4.3 %collective-permute-start.12 = (f32[72,512]{1,0:T(8,128)S(1)}, f32[72,512]{1,0:T(8,128)S(1)}, u32[]{:S(2)}, u32[]{:S(2)}) collective-permute-start(f32[72,512]{1,0:T(8,128)S(1)} %slice.102), channel_id=1, source_target_pairs={{0,16},{16,0},{1,17},{17,1},{2,18},{18,2},{3,19},{19,3},{4,20},{20... | collective-permute-start | bytes 442376 | tf_op jit(solution)/shard_map/ppermute | solution.py:15
  123.6 12.0 %collective-permute-done.12 = f32[72,512]{1,0:T(8,128)S(1)} collective-permute-done((f32[72,512]{1,0:T(8,128)S(1)}, f32[72,512]{1,0:T(8,128)S(1)}, u32[]{:S(2)}, u32[]{:S(2)}) %collective-permute-start.12) | collective-permute-done | bytes 147488 | tf_op jit(solution)/shard_map/ppermute | solution.py:15
  138.6 24.0 %all_to_all.15 = bf16[32,41,128]{2,1,0:T(8,128)(2,1)S(1)} all-to-all(bf16[32,41,128]{2,1,0:T(8,128)(2,1)S(1)} %pad_maximum_fusion.1), channel_id=1, replica_groups=mesh['y'=8,'a'=2,'b'=2,'zl'=2,'x'=4,'c'=2] {'y','a','b'}, dimensions={0} | all-to-all | bytes 671744 | tf_op jit(solution)/shard_map/all_to_all | solution.py:69
  (73 shorter events, 35.3 us)
Async XLA Ops:
  0.6 135.0 %copy-start = (bf16[512,1152]{1,0:T(8,128)(2,1)S(1)}, bf16[512,1152]{1,0:T(8,128)(2,1)}, u32[]{:S(2)}) copy-start(bf16[512,1152]{1,0:T(8,128)(2,1)} %param.8) | copy-start | bytes 3538948
  2.3 17.5 %collective-permute-start.1 = (bf16[32,1152]{1,0:T(8,128)(2,1)}, bf16[32,1152]{1,0:T(8,128)(2,1)}, u32[]{:S(2)}, u32[]{:S(2)}) collective-permute-start(bf16[32,1152]{1,0:T(8,128)(2,1)} %get-tuple-element.5), channel_id=1, source_target_pairs={{0,32},{32,0},{1,33},{33,1},{2,34},{34,2},{3,35},{35,3},{4,36},{36... | collective-permute-start | bytes 221192 | tf_op jit(solution)/shard_map/ppermute | solution.py:15
  13.2 10.8 %collective-permute-start = (bf16[32,1152]{1,0:T(8,128)(2,1)}, bf16[32,1152]{1,0:T(8,128)(2,1)}, u32[]{:S(2)}, u32[]{:S(2)}) collective-permute-start(bf16[32,1152]{1,0:T(8,128)(2,1)} %param.7), channel_id=1, source_target_pairs={{0,32},{32,0},{1,33},{33,1},{2,34},{34,2},{3,35},{35,3},{4,36},{36... | collective-permute-start | bytes 221192 | tf_op jit(solution)/shard_map/ppermute | solution.py:15
  25.1 14.7 %collective-permute-start.2 = (bf16[128,1152]{1,0:T(8,128)(2,1)S(1)}, bf16[128,1152]{1,0:T(8,128)(2,1)S(1)}, u32[]{:S(2)}, u32[]{:S(2)}) collective-permute-start(bf16[128,1152]{1,0:T(8,128)(2,1)S(1)} %pad_maximum_fusion.2), channel_id=1, source_target_pairs={{0,64},{64,128},{128,192},{192,256},{256,320},{320,384},{384,448},... | collective-permute-start | bytes 884744 | tf_op jit(solution)/shard_map/ppermute | solution.py:15
  28.6 13.2 %collective-permute-start.3 = (bf16[128,1152]{1,0:T(8,128)(2,1)S(1)}, bf16[128,1152]{1,0:T(8,128)(2,1)S(1)}, u32[]{:S(2)}, u32[]{:S(2)}) collective-permute-start(bf16[128,1152]{1,0:T(8,128)(2,1)S(1)} %pad_maximum_fusion.2), channel_id=1, source_target_pairs={{0,448},{64,0},{128,64},{192,128},{256,192},{320,256},{384,320},{4... | collective-permute-start | bytes 884744 | tf_op jit(solution)/shard_map/ppermute | solution.py:15
  32.4 29.6 %collective-permute-start.9 = (bf16[256,1152]{0,1:T(8,128)(2,1)}, bf16[256,1152]{0,1:T(8,128)(2,1)S(1)}, u32[]{:S(2)}, u32[]{:S(2)}) collective-permute-start(bf16[256,1152]{0,1:T(8,128)(2,1)} %constant_dynamic-slice_fusion), channel_id=1, source_target_pairs={{0,16},{16,0},{1,17},{17,1},{2,18},{18,2},{3,19},{19,3},{4,20},{20... | collective-permute-start | bytes 1769480 | tf_op jit(solution)/shard_map/ppermute | solution.py:15
  39.8 9.8 %collective-permute-start.4 = (bf16[128,1152]{1,0:T(8,128)(2,1)S(1)}, bf16[128,1152]{1,0:T(8,128)(2,1)S(1)}, u32[]{:S(2)}, u32[]{:S(2)}) collective-permute-start(bf16[128,1152]{1,0:T(8,128)(2,1)S(1)} %collective-permute-done.2), channel_id=1, source_target_pairs={{0,64},{64,128},{128,192},{192,256},{256,320},{320,384},{384,448},... | collective-permute-start | bytes 884744 | tf_op jit(solution)/shard_map/ppermute | solution.py:15
  41.8 9.7 %collective-permute-start.5 = (bf16[128,1152]{1,0:T(8,128)(2,1)S(1)}, bf16[128,1152]{1,0:T(8,128)(2,1)S(1)}, u32[]{:S(2)}, u32[]{:S(2)}) collective-permute-start(bf16[128,1152]{1,0:T(8,128)(2,1)S(1)} %collective-permute-done.3), channel_id=1, source_target_pairs={{0,448},{64,0},{128,64},{192,128},{256,192},{320,256},{384,320},{4... | collective-permute-start | bytes 884744 | tf_op jit(solution)/shard_map/ppermute | solution.py:15
  49.6 15.7 %collective-permute-start.6 = (bf16[128,1152]{1,0:T(8,128)(2,1)S(1)}, bf16[128,1152]{1,0:T(8,128)(2,1)S(1)}, u32[]{:S(2)}, u32[]{:S(2)}) collective-permute-start(bf16[128,1152]{1,0:T(8,128)(2,1)S(1)} %collective-permute-done.4), channel_id=1, source_target_pairs={{0,64},{64,128},{128,192},{192,256},{256,320},{320,384},{384,448},... | collective-permute-start | bytes 884744 | tf_op jit(solution)/shard_map/ppermute | solution.py:15
  51.5 16.4 %collective-permute-start.7 = (bf16[128,1152]{1,0:T(8,128)(2,1)S(1)}, bf16[128,1152]{1,0:T(8,128)(2,1)S(1)}, u32[]{:S(2)}, u32[]{:S(2)}) collective-permute-start(bf16[128,1152]{1,0:T(8,128)(2,1)S(1)} %collective-permute-done.5), channel_id=1, source_target_pairs={{0,448},{64,0},{128,64},{192,128},{256,192},{320,256},{384,320},{4... | collective-permute-start | bytes 884744 | tf_op jit(solution)/shard_map/ppermute | solution.py:15
  62.0 13.7 %collective-permute-start.10 = (bf16[256,1152]{0,1:T(8,128)(2,1)S(1)}, bf16[256,1152]{0,1:T(8,128)(2,1)S(1)}, u32[]{:S(2)}, u32[]{:S(2)}) collective-permute-start(bf16[256,1152]{0,1:T(8,128)(2,1)S(1)} %collective-permute-done.9), channel_id=1, source_target_pairs={{0,1},{1,0},{2,3},{3,2},{4,5},{5,4},{6,7},{7,6},{8,9},{9,8},{10,11... | collective-permute-start | bytes 1769480 | tf_op jit(solution)/shard_map/ppermute | solution.py:15
  66.0 9.3 %collective-permute-start.8 = (bf16[64,1152]{1,0:T(8,128)(2,1)S(1)}, bf16[64,1152]{1,0:T(8,128)(2,1)S(1)}, u32[]{:S(2)}, u32[]{:S(2)}) collective-permute-start(bf16[64,1152]{1,0:T(8,128)(2,1)S(1)} %get-tuple-element.8), channel_id=1, source_target_pairs={{0,64},{64,128},{128,192},{192,256},{256,320},{320,384},{384,448},... | collective-permute-start | bytes 442376 | tf_op jit(solution)/shard_map/ppermute | solution.py:15
  68.7 16.1 %collective-permute-start.13 = (bf16[64,1152]{1,0:T(8,128)(2,1)S(1)}, bf16[64,1152]{1,0:T(8,128)(2,1)S(1)}, u32[]{:S(2)}, u32[]{:S(2)}) collective-permute-start(bf16[64,1152]{1,0:T(8,128)(2,1)S(1)} %get-tuple-element.13), channel_id=1, source_target_pairs={{0,448},{64,0},{128,64},{192,128},{256,192},{320,256},{384,320},{4... | collective-permute-start | bytes 442376 | tf_op jit(solution)/shard_map/ppermute | solution.py:15
  82.3 2.4 %copy-start.3 = (bf16[512,1152]{1,0:T(8,128)(2,1)S(1)}, bf16[512,1152]{1,0:T(8,128)(2,1)}, u32[]{:S(2)}) copy-start(bf16[512,1152]{1,0:T(8,128)(2,1)} %get-tuple-element.12) | copy-start | bytes 3538948
  82.5 7.6 %collective-permute-start.11 = (bf16[8,72,1024]{2,1,0:T(8,128)(2,1)S(1)}, bf16[8,72,1024]{2,1,0:T(8,128)(2,1)S(1)}, u32[]{:S(2)}, u32[]{:S(2)}) collective-permute-start(bf16[8,72,1024]{2,1,0:T(8,128)(2,1)S(1)} %dynamic-slice_bitcast_fusion.1), channel_id=1, source_target_pairs={{0,1},{1,0},{2,3},{3,2},{4,5},{5,4},{6,7},{7,6},{8,9},{9,8},{10,11... | collective-permute-start | bytes 3538952 | tf_op jit(solution)/shard_map/ppermute | solution.py:15
  91.5 20.3 %all-to-all-start = ((bf16[8,72,1024]{2,1,0:T(8,128)(2,1)}), bf16[8,72,1024]{2,1,0:T(8,128)(2,1)S(1)}, u32[]{:S(2)}, u32[]{:S(2)}) async-start(bf16[8,72,1024]{2,1,0:T(8,128)(2,1)} %fusion.18), calls=%async_computation | async-start | bytes 2359296 | tf_op jit(solution)/shard_map/all_to_all | solution.py:58
  96.3 6.5 %copy-start.2 = (bf16[1152,1152]{1,0:T(8,128)(2,1)S(1)}, bf16[1152,1152]{1,0:T(8,128)(2,1)}, u32[]{:S(2)}) copy-start(bf16[1152,1152]{1,0:T(8,128)(2,1)} %convolution_convert_fusion) | copy-start | bytes 7962628
  97.9 5.0 %collective-permute-start.14 = (bf16[8,72,1152]{2,1,0:T(8,128)(2,1)S(1)}, bf16[8,72,1152]{2,1,0:T(8,128)(2,1)S(1)}, u32[]{:S(2)}, u32[]{:S(2)}) collective-permute-start(bf16[8,72,1152]{2,1,0:T(8,128)(2,1)S(1)} %dynamic-slice_bitcast_fusion), channel_id=1, source_target_pairs={{0,1},{1,0},{2,3},{3,2},{4,5},{5,4},{6,7},{7,6},{8,9},{9,8},{10,11... | collective-permute-start | bytes 3981320 | tf_op jit(solution)/shard_map/ppermute | solution.py:15
  111.8 1.0 copy-start.1
  112.8 24.6 %all-to-all-start.1 = ((bf16[8,72,1152]{2,1,0:T(8,128)(2,1)}), bf16[8,72,1152]{2,1,0:T(8,128)(2,1)S(1)}, u32[]{:S(2)}, u32[]{:S(2)}) async-start(bf16[8,72,1152]{2,1,0:T(8,128)(2,1)} %fusion.12), calls=%async_computation.1 | async-start | bytes 2654208 | tf_op jit(solution)/shard_map/all_to_all | solution.py:58
  119.3 16.3 %collective-permute-start.12 = (f32[72,512]{1,0:T(8,128)S(1)}, f32[72,512]{1,0:T(8,128)S(1)}, u32[]{:S(2)}, u32[]{:S(2)}) collective-permute-start(f32[72,512]{1,0:T(8,128)S(1)} %slice.102), channel_id=1, source_target_pairs={{0,16},{16,0},{1,17},{17,1},{2,18},{18,2},{3,19},{19,3},{4,20},{20... | collective-permute-start | bytes 442376 | tf_op jit(solution)/shard_map/ppermute | solution.py:15

commit v4 on v3

v4 whole, which is shorter than its diff:
```python
import jax
import jax.numpy as jnp
from jax import lax
from jax.sharding import Mesh, PartitionSpec as P

SIZES = (8, 2, 2, 2, 4, 2)
NAMES = ("y", "a", "b", "zl", "x", "c")
DP = ("y", "a", "b")
MP = ("zl", "x", "c")
ROW = ("zl", "x")


def shifted(value, axis, steps):
    count = lax.axis_size(axis)
    return lax.ppermute(value, axis, [(s, (s + steps) % count) for s in range(count)])


def after(value, other):
    return lax.optimization_barrier((value, other))[0]


def normalize(rows, axis=-1):
    wide = rows.astype(jnp.float32)
    factor = lax.rsqrt(jnp.sum(wide * wide, axis=axis, keepdims=True) + 1e-06)
    return (wide * factor, factor)


def unit_back(direction, unit, factor, axis=-1):
    return (direction - unit * jnp.sum(unit * direction, axis=axis, keepdims=True)) * factor


def ring_step(value, way):
    count = lax.axis_size("y")
    pairs = [(2 * s + c, 2 * ((s + way * (1 - 2 * c)) % count) + c) for s in range(count) for c in range(2)]
    return lax.ppermute(value, ("y", "c"), pairs)


def gather(text, feat, image_emb):
    rows = text.shape[0]
    own = jnp.concatenate([text, feat], axis=0)
    far = lax.ppermute(own, ("a", "b", "zl"), [(s, 7 - s) for s in range(8)])
    chunk = jnp.concatenate([text, far[:rows], feat, far[rows:]], axis=0)
    chunks = [chunk]
    core = lax.axis_index("c")
    part = image_emb.shape[0] // 2
    piece = lax.dynamic_slice_in_dim(image_emb, core * part, part, 0)
    mine = shifted(after(piece, chunk), "b", 1)
    up = down = chunk
    for _ in range(3):
        up, down = ring_step(up, 1), ring_step(down, -1)
        chunks += [up, down]
    theirs = shifted(mine, "c", 1)
    other = [jnp.where(core == 0, mine, theirs), jnp.where(core == 0, theirs, mine)]
    last = ring_step(up, 1)
    half = chunk.shape[0] // 2
    texts = jnp.concatenate([piece[:half] for piece in chunks], axis=0)
    feats = jnp.concatenate([piece[half:] for piece in chunks + [last]], axis=0)
    return texts, last[:half], feats, jnp.concatenate([image_emb] + other, axis=0)


def core_sum(full):
    core = lax.axis_index("c")
    slabs = full.reshape(8, 2, full.shape[0] // 16, full.shape[1])
    keep = lax.dynamic_index_in_dim(slabs, core, 1, keepdims=False).astype(jnp.float32)
    give = lax.dynamic_index_in_dim(slabs, 1 - core, 1, keepdims=False)
    return (keep + shifted(give, "c", 1).astype(jnp.float32)).astype(jnp.bfloat16)


def row_sum(slabs):
    got = lax.all_to_all(slabs, ROW, 0, 0, tiled=True)
    return jnp.sum(got.astype(jnp.float32), axis=0)


def sum_over_dp(parts):
    rows, cols = parts.shape
    own = rows // 32
    parts = parts.astype(jnp.bfloat16)
    main = parts[:, :128].reshape(32, own, 128)
    rest = parts[:, 128:].reshape(32, own * (cols - 128))
    rest = jnp.pad(rest, ((0, 0), (0, -rest.shape[1] % 128))).reshape(32, -1, 128)
    got = lax.all_to_all(jnp.concatenate([main, rest], axis=1), DP, 0, 0, tiled=True)
    total = jnp.sum(got.astype(jnp.float32), axis=0)
    tail = total[own:].reshape(-1)[: own * (cols - 128)].reshape(own, cols - 128)
    return jnp.concatenate([total[:own], tail], axis=1)


def local(image_emb, text_emb, image_feat, text_feat, logit_scale, logit_bias):
    column = lax.axis_index(MP)
    own_rows, width = text_emb.shape
    block = image_emb.shape[0]
    cols = width // 16
    scale = logit_scale[0]
    offset = logit_bias[0]

    own_feat = lax.dynamic_slice_in_dim(text_feat, column * own_rows, own_rows, 0)
    texts, last_text, feats, images = gather(text_emb, own_feat, image_emb)
    images_t = lax.optimization_barrier(images.T)

    image_unit, image_norm = normalize(images)
    image_low = image_unit.astype(jnp.bfloat16)
    image_unit_t, image_norm_t = normalize(images_t, 0)
    image_ids = jnp.arange(2 * block, dtype=jnp.int32)[None, :]

    def pair_weights(low, has_own):
        logits = lax.dot_general(low, image_low, (((1,), (1,)), ((), ())), preferred_element_type=jnp.float32)
        value = scale * logits + offset
        if not has_own:
            return (scale * jax.nn.sigmoid(value)).astype(jnp.bfloat16)
        row_ids = jnp.arange(low.shape[0], dtype=jnp.int32)[:, None]
        match = (row_ids < own_rows) & (image_ids == column * own_rows + row_ids)
        sign = jnp.where(match, 1.0, -1.0).astype(jnp.float32)
        return (-scale * sign * jax.nn.sigmoid(-sign * value)).astype(jnp.bfloat16)

    def image_direction(low, weights):
        return lax.dot_general(low, weights, (((0,), (0,)), ((), ())), preferred_element_type=jnp.float32)

    def text_gradient(unit, norm, weights):
        direction = jnp.dot(weights, image_low, preferred_element_type=jnp.float32)
        return unit_back(direction, unit, norm).astype(jnp.bfloat16)

    text_unit, text_norm = normalize(texts)
    text_low = text_unit.astype(jnp.bfloat16)
    weights = pair_weights(text_low, True)
    image_dir = image_direction(text_low, weights)

    last_text = after(last_text, image_dir)
    last_unit, last_norm = normalize(last_text)
    last_low = last_unit.astype(jnp.bfloat16)
    last_weights = pair_weights(last_low, False)
    image_dir = image_dir + image_direction(last_low, last_weights)
    image_part = unit_back(image_dir, image_unit_t, image_norm_t, 0).astype(jnp.bfloat16)
    image_slabs = core_sum(image_part)
    image_two = row_sum(image_slabs)
    image_cols = image_two[:, :block] + shifted(image_two[:, block:], "b", 1)
    image_term = jnp.dot(image_cols.astype(jnp.bfloat16), image_feat, preferred_element_type=jnp.float32)

    last_weights = after(last_weights, image_part)
    text_part = jnp.concatenate(
        [text_gradient(text_unit, text_norm, weights), text_gradient(last_unit, last_norm, last_weights)], axis=0
    )
    text_part = after(text_part, image_slabs)
    text_all = lax.dot_general(text_part, feats, (((0,), (0,)), ((), ())), preferred_element_type=jnp.float32)
    text_term = row_sum(core_sum(text_all.astype(jnp.bfloat16)))

    own = sum_over_dp(jnp.concatenate([image_term, text_term], axis=0).T)
    return (own[:, :cols], own[:, cols:])


def solution(mesh):
    split = Mesh(mesh.devices.reshape(SIZES), NAMES)
    in_specs = (P(DP, None), P(DP + MP, None), P(DP, None), P(DP, None), P(), P())
    out_specs = (P(DP, MP), P(DP, MP))
    return jax.shard_map(local, mesh=split, in_specs=in_specs, out_specs=out_specs, check_vma=False)
```

time: 167 us -> 162 us (0.970)
  starting transfers between devices: 66.3 us -> 59.4 us
  other arithmetic: 9.33 us -> 12.6 us
  waiting for transfers between devices: 36.7 us -> 34.6 us
  matrix products: 9.64 us -> 11.7 us
    ppermute x15 -> x5, starting transfers between devices: 56.5 us -> 14.3 us  [shifted(): lax.ppermute(value, axis, [(s, (s + steps) % count) for s in range(count)])]
    ppermute x0 -> x8, starting transfers between devices: none -> 35 us  [the longest x7 24 us: ring_step(): return lax.ppermute(value, ('y', 'c'), pairs)]
    ppermute x0 -> x8, waiting for transfers between devices: none -> 8.44 us  [the longest x1 6.08 us: gather(): far = lax.ppermute(own, ('a', 'b', 'zl'), [(s, 7 - s) for s in range(8)])]
    ppermute x15 -> x5, waiting for transfers between devices: 27.6 us -> 19.8 us  [shifted(): lax.ppermute(value, axis, [(s, (s + steps) % count) for s in range(count)])]
    all_to_all x2, waiting for transfers between devices: 9.1 us -> 6.37 us  [row_sum(): got = lax.all_to_all(slabs, ROW, 0, 0, tiled=True)]
    concatenate x1 -> x3, other arithmetic: 1.02 us -> 3.63 us  [the longest x1 1.63 us: gather(): chunk = jnp.concatenate([text, far[:rows], feat, far[rows:]], axis=0)]
    dot_general x3 -> x6, matrix products: 5.78 us -> 8 us  [the longest x2 2.84 us: pair_weights(): lax.dot_general(low, image_low, (((1,), (1,)), ((), ())), preferred_eleme...]
    unnamed x18 -> x14, local copies, waits for them, and re-layouts: 11 us -> 11.8 us
  transfers between devices with their start and end apart: 17 -> 15, of which waited for: 8 -> 7; matrix products, arithmetic and copies ran while one was open for 16% -> 16% of each run, Pallas kernels for 0% -> 0%
where the time goes in v4:
time: 162 us; the launch traced here: 160 us
  starting transfers between devices  59.4 us (37%)
  waiting for transfers between devices  34.6 us (21%)
  blocking collectives  25.3 us (16%)
  local copies, waits for them, and re-layouts  14.3 us (9%)
  other arithmetic  12.6 us (8%)
  matrix products  11.7 us (7%)
  between operations  2.32 us (1%)
    all_to_all x1, blocking collectives, sum_over_dp(): lax.all_to_all(jnp.concatenate([main, rest], axis=1), DP, 0, 0, tiled=True)  25.3 us
    ppermute x7, starting transfers between devices, ring_step(): return lax.ppermute(value, ('y', 'c'), pairs)  24 us
    ppermute x5, waiting for transfers between devices, shifted(): lax.ppermute(value, axis, [(s, (s + steps) % count) for s in range(count)])  19.8 us
    ppermute x5, starting transfers between devices, shifted(): lax.ppermute(value, axis, [(s, (s + steps) % count) for s in range(count)])  14.3 us
    unnamed x14, local copies, waits for them, and re-layouts  11.8 us
    ppermute x1, starting transfers between devices, gather(): far = lax.ppermute(own, ('a', 'b', 'zl'), [(s, 7 - s) for s in range(8)])  10.9 us
    all_to_all x2, starting transfers between devices, row_sum(): got = lax.all_to_all(slabs, ROW, 0, 0, tiled=True)  10.1 us
    all_to_all x2, waiting for transfers between devices, row_sum(): got = lax.all_to_all(slabs, ROW, 0, 0, tiled=True)  6.37 us
  transfers between devices with their start and end apart: 15, of which 7 were waited for; matrix products, arithmetic and copies ran while one was open for 16% of the time, Pallas kernels for 0%

profile of v4, /device:TPU:6, one launch (start us, length us, event | category | flops | bytes accessed | tf_op | source)
XLA Modules:
  0.0 160.3 jit_solution(1056708800675497322)
XLA Ops:
  3.2 10.9 %collective-permute-start = (bf16[64,1152]{1,0:T(8,128)(2,1)S(1)}, bf16[64,1152]{1,0:T(8,128)(2,1)S(1)}, u32[]{:S(2)}, u32[]{:S(2)}) collective-permute-start(bf16[64,1152]{1,0:T(8,128)(2,1)S(1)} %pad_maximum_fusion.4), channel_id=1, source_target_pairs={{0,56},{8,48},{16,40},{24,32},{32,24},{40,16},{48,8},{56,0},{1,57}... | collective-permute-start | bytes 442376 | tf_op jit(solution)/shard_map/ppermute | solution.py:41
  15.0 6.1 %collective-permute-done = bf16[64,1152]{1,0:T(8,128)(2,1)S(1)} collective-permute-done((bf16[64,1152]{1,0:T(8,128)(2,1)S(1)}, bf16[64,1152]{1,0:T(8,128)(2,1)S(1)}, u32[]{:S(2)}, u32[]{:S(2)}) %collective-permute-start) | collective-permute-done | bytes 147488 | tf_op jit(solution)/shard_map/ppermute | solution.py:41
  23.4 5.4 %collective-permute-start.2 = (bf16[128,1152]{1,0:T(8,128)(2,1)}, bf16[128,1152]{1,0:T(8,128)(2,1)}, u32[]{:S(2)}, u32[]{:S(2)}) collective-permute-start(bf16[128,1152]{1,0:T(8,128)(2,1)} %pad_maximum_fusion.3), channel_id=1, source_target_pairs={{0,448},{1,65},{64,0},{65,129},{128,64},{129,193},{192,128},{193,2... | collective-permute-start | bytes 884744 | tf_op jit(solution)/shard_map/ppermute | solution.py:35
  28.8 1.9 %collective-permute-start.1 = (bf16[128,1152]{1,0:T(8,128)(2,1)}, bf16[128,1152]{1,0:T(8,128)(2,1)}, u32[]{:S(2)}, u32[]{:S(2)}) collective-permute-start(bf16[128,1152]{1,0:T(8,128)(2,1)} %pad_maximum_fusion.3), channel_id=1, source_target_pairs={{0,64},{1,449},{64,128},{65,1},{128,192},{129,65},{192,256},{193,1... | collective-permute-start | bytes 884744 | tf_op jit(solution)/shard_map/ppermute | solution.py:35
  33.6 1.9 %collective-permute-start.7 = (bf16[256,1152]{0,1:T(8,128)(2,1)S(1)}, bf16[256,1152]{0,1:T(8,128)(2,1)S(1)}, u32[]{:S(2)}, u32[]{:S(2)}) collective-permute-start(bf16[256,1152]{0,1:T(8,128)(2,1)S(1)} %constant_dynamic-slice_fusion), channel_id=1, source_target_pairs={{0,16},{16,0},{1,17},{17,1},{2,18},{18,2},{3,19},{19,3},{4,20},{20... | collective-permute-start | bytes 1769480 | tf_op jit(solution)/shard_map/ppermute | solution.py:15
  35.6 5.5 %collective-permute-start.4 = (bf16[128,1152]{1,0:T(8,128)(2,1)}, bf16[128,1152]{1,0:T(8,128)(2,1)S(1)}, u32[]{:S(2)}, u32[]{:S(2)}) collective-permute-start(bf16[128,1152]{1,0:T(8,128)(2,1)} %collective-permute-done.2), channel_id=1, source_target_pairs={{0,448},{1,65},{64,0},{65,129},{128,64},{129,193},{192,128},{193,2... | collective-permute-start | bytes 884744 | tf_op jit(solution)/shard_map/ppermute | solution.py:35
  41.1 1.9 %collective-permute-start.3 = (bf16[128,1152]{1,0:T(8,128)(2,1)}, bf16[128,1152]{1,0:T(8,128)(2,1)S(1)}, u32[]{:S(2)}, u32[]{:S(2)}) collective-permute-start(bf16[128,1152]{1,0:T(8,128)(2,1)} %collective-permute-done.1), channel_id=1, source_target_pairs={{0,64},{1,449},{64,128},{65,1},{128,192},{129,65},{192,256},{193,1... | collective-permute-start | bytes 884744 | tf_op jit(solution)/shard_map/ppermute | solution.py:35
  46.3 2.3 %collective-permute-done.4 = bf16[128,1152]{1,0:T(8,128)(2,1)S(1)} collective-permute-done((bf16[128,1152]{1,0:T(8,128)(2,1)}, bf16[128,1152]{1,0:T(8,128)(2,1)S(1)}, u32[]{:S(2)}, u32[]{:S(2)}) %collective-permute-start.4) | collective-permute-done | bytes 294944 | tf_op jit(solution)/shard_map/ppermute | solution.py:35
  48.7 5.5 %collective-permute-start.6 = (bf16[128,1152]{1,0:T(8,128)(2,1)S(1)}, bf16[128,1152]{1,0:T(8,128)(2,1)S(1)}, u32[]{:S(2)}, u32[]{:S(2)}) collective-permute-start(bf16[128,1152]{1,0:T(8,128)(2,1)S(1)} %collective-permute-done.4), channel_id=1, source_target_pairs={{0,448},{1,65},{64,0},{65,129},{128,64},{129,193},{192,128},{193,2... | collective-permute-start | bytes 884744 | tf_op jit(solution)/shard_map/ppermute | solution.py:35
  54.2 1.9 %collective-permute-start.5 = (bf16[128,1152]{1,0:T(8,128)(2,1)S(1)}, bf16[128,1152]{1,0:T(8,128)(2,1)S(1)}, u32[]{:S(2)}, u32[]{:S(2)}) collective-permute-start(bf16[128,1152]{1,0:T(8,128)(2,1)S(1)} %collective-permute-done.3), channel_id=1, source_target_pairs={{0,64},{1,449},{64,128},{65,1},{128,192},{129,65},{192,256},{193,1... | collective-permute-start | bytes 884744 | tf_op jit(solution)/shard_map/ppermute | solution.py:35
  56.1 5.1 %collective-permute-done.7 = bf16[256,1152]{0,1:T(8,128)(2,1)S(1)} collective-permute-done((bf16[256,1152]{0,1:T(8,128)(2,1)S(1)}, bf16[256,1152]{0,1:T(8,128)(2,1)S(1)}, u32[]{:S(2)}, u32[]{:S(2)}) %collective-permute-start.7) | collective-permute-done | bytes 589856 | tf_op jit(solution)/shard_map/ppermute | solution.py:15
  61.2 1.9 %collective-permute-start.8 = (bf16[256,1152]{0,1:T(8,128)(2,1)S(1)}, bf16[256,1152]{0,1:T(8,128)(2,1)S(1)}, u32[]{:S(2)}, u32[]{:S(2)}) collective-permute-start(bf16[256,1152]{0,1:T(8,128)(2,1)S(1)} %collective-permute-done.7), channel_id=1, source_target_pairs={{0,1},{1,0},{2,3},{3,2},{4,5},{5,4},{6,7},{7,6},{8,9},{9,8},{10,11... | collective-permute-start | bytes 1769480 | tf_op jit(solution)/shard_map/ppermute | solution.py:15
  64.5 1.9 %collective-permute-start.9 = (bf16[128,1152]{1,0:T(8,128)(2,1)S(1)}, bf16[128,1152]{1,0:T(8,128)(2,1)S(1)}, u32[]{:S(2)}, u32[]{:S(2)}) collective-permute-start(bf16[128,1152]{1,0:T(8,128)(2,1)S(1)} %collective-permute-done.5), channel_id=1, source_target_pairs={{0,64},{1,449},{64,128},{65,1},{128,192},{129,65},{192,256},{193,1... | collective-permute-start | bytes 884744 | tf_op jit(solution)/shard_map/ppermute | solution.py:35
  69.1 2.1 %fusion.20 = bf16[448,1024]{1,0:T(8,128)(2,1)S(1)} fusion(f32[1024]{0:T(1024)S(1)} %add_rsqrt_fusion.1, f32[]{:T(128)} %bitcast.29, f32[]{:T(128)} %bitcast.27, s32[448]{0:T(512)S(1)} %iota_add_fusion, f32[]{:T(128)S(6)} %neg.12, pred[448]{0:T(512)(128)(4,1)S(1)} %iota_compare_fusion.1, bf16[448,1152]{1,0:T(8,128)(2,1)S(1)} %get-tuple-element.17, ...), kind=kOutput, calls=%fused_computation.35 | convolution fusion | flops 1073913856 | bytes 4317132 | tf_op jit(solution)/shard_map/dot_general | solution.py:105
  78.7 4.0 %collective-permute-start.10 = (bf16[8,72,1024]{2,1,0:T(8,128)(2,1)S(1)}, bf16[8,72,1024]{2,1,0:T(8,128)(2,1)S(1)}, u32[]{:S(2)}, u32[]{:S(2)}) collective-permute-start(bf16[8,72,1024]{2,1,0:T(8,128)(2,1)S(1)} %dynamic-slice_bitcast_fusion.1), channel_id=1, source_target_pairs={{0,1},{1,0},{2,3},{3,2},{4,5},{5,4},{6,7},{7,6},{8,9},{9,8},{10,11... | collective-permute-start | bytes 3538952 | tf_op jit(solution)/shard_map/ppermute | solution.py:15
  86.9 4.8 %all-to-all-start = ((bf16[8,72,1024]{2,1,0:T(8,128)(2,1)}), bf16[8,72,1024]{2,1,0:T(8,128)(2,1)S(1)}, u32[]{:S(2)}, u32[]{:S(2)}) async-start(bf16[8,72,1024]{2,1,0:T(8,128)(2,1)} %fusion.13), calls=%async_computation | async-start | bytes 2359296 | tf_op jit(solution)/shard_map/all_to_all | solution.py:70
  91.7 3.4 %convolution_convert_fusion = bf16[1152,1152]{1,0:T(8,128)(2,1)S(1)} fusion(bf16[512,1152]{1,0:T(8,128)(2,1)} %pad_maximum_fusion.1, bf16[512,1152]{1,0:T(8,128)(2,1)} %get-tuple-element.14), kind=kOutput, calls=%fused_computation | convolution fusion | flops 1360281600 | bytes 5013504 | tf_op jit(solution)/shard_map/dot_general | solution.py:142
  95.2 1.9 %collective-permute-start.12 = (bf16[8,72,1152]{2,1,0:T(8,128)(2,1)S(1)}, bf16[8,72,1152]{2,1,0:T(8,128)(2,1)S(1)}, u32[]{:S(2)}, u32[]{:S(2)}) collective-permute-start(bf16[8,72,1152]{2,1,0:T(8,128)(2,1)S(1)} %dynamic-slice_bitcast_fusion), channel_id=1, source_target_pairs={{0,1},{1,0},{2,3},{3,2},{4,5},{5,4},{6,7},{7,6},{8,9},{9,8},{10,11... | collective-permute-start | bytes 3981320 | tf_op jit(solution)/shard_map/ppermute | solution.py:15
  97.1 3.0 %collective-permute-done.12 = bf16[8,72,1152]{2,1,0:T(8,128)(2,1)S(1)} collective-permute-done((bf16[8,72,1152]{2,1,0:T(8,128)(2,1)S(1)}, bf16[8,72,1152]{2,1,0:T(8,128)(2,1)S(1)}, u32[]{:S(2)}, u32[]{:S(2)}) %collective-permute-start.12) | collective-permute-done | bytes 1327136 | tf_op jit(solution)/shard_map/ppermute | solution.py:15
  101.5 4.8 %all-to-all-done = bf16[8,72,1024]{2,1,0:T(8,128)(2,1)S(1)} async-done(((bf16[8,72,1024]{2,1,0:T(8,128)(2,1)}), bf16[8,72,1024]{2,1,0:T(8,128)(2,1)S(1)}, u32[]{:S(2)}, u32[]{:S(2)}) %all-to-all-start) | async-done | bytes 1179680 | tf_op jit(solution)/shard_map/all_to_all | solution.py:70
  107.4 5.4 %all-to-all-start.1 = ((bf16[8,72,1152]{2,1,0:T(8,128)(2,1)}), bf16[8,72,1152]{2,1,0:T(8,128)(2,1)S(1)}, u32[]{:S(2)}, u32[]{:S(2)}) async-start(bf16[8,72,1152]{2,1,0:T(8,128)(2,1)} %fusion.9), calls=%async_computation.1 | async-start | bytes 2654208 | tf_op jit(solution)/shard_map/all_to_all | solution.py:70
  114.2 4.5 %collective-permute-start.11 = (f32[72,512]{1,0:T(8,128)S(1)}, f32[72,512]{1,0:T(8,128)S(1)}, u32[]{:S(2)}, u32[]{:S(2)}) collective-permute-start(f32[72,512]{1,0:T(8,128)S(1)} %slice.119), channel_id=1, source_target_pairs={{0,16},{16,0},{1,17},{17,1},{2,18},{18,2},{3,19},{19,3},{4,20},{20... | collective-permute-start | bytes 442376 | tf_op jit(solution)/shard_map/ppermute | solution.py:15
  118.8 11.7 %collective-permute-done.11 = f32[72,512]{1,0:T(8,128)S(1)} collective-permute-done((f32[72,512]{1,0:T(8,128)S(1)}, f32[72,512]{1,0:T(8,128)S(1)}, u32[]{:S(2)}, u32[]{:S(2)}) %collective-permute-start.11) | collective-permute-done | bytes 147488 | tf_op jit(solution)/shard_map/ppermute | solution.py:15
  133.5 25.3 %all_to_all.15 = bf16[32,41,128]{2,1,0:T(8,128)(2,1)S(1)} all-to-all(bf16[32,41,128]{2,1,0:T(8,128)(2,1)S(1)} %pad_maximum_fusion.2), channel_id=1, replica_groups=mesh['y'=8,'a'=2,'b'=2,'zl'=2,'x'=4,'c'=2] {'y','a','b'}, dimensions={0} | all-to-all | bytes 671744 | tf_op jit(solution)/shard_map/all_to_all | solution.py:81
  (72 shorter events, 34.7 us)
Async XLA Ops:
  0.6 129.8 %copy-start = (bf16[512,1152]{1,0:T(8,128)(2,1)S(1)}, bf16[512,1152]{1,0:T(8,128)(2,1)}, u32[]{:S(2)}) copy-start(bf16[512,1152]{1,0:T(8,128)(2,1)} %param.8) | copy-start | bytes 3538948
  3.2 17.9 %collective-permute-start = (bf16[64,1152]{1,0:T(8,128)(2,1)S(1)}, bf16[64,1152]{1,0:T(8,128)(2,1)S(1)}, u32[]{:S(2)}, u32[]{:S(2)}) collective-permute-start(bf16[64,1152]{1,0:T(8,128)(2,1)S(1)} %pad_maximum_fusion.4), channel_id=1, source_target_pairs={{0,56},{8,48},{16,40},{24,32},{32,24},{40,16},{48,8},{56,0},{1,57}... | collective-permute-start | bytes 442376 | tf_op jit(solution)/shard_map/ppermute | solution.py:41
  23.4 12.2 %collective-permute-start.2 = (bf16[128,1152]{1,0:T(8,128)(2,1)}, bf16[128,1152]{1,0:T(8,128)(2,1)}, u32[]{:S(2)}, u32[]{:S(2)}) collective-permute-start(bf16[128,1152]{1,0:T(8,128)(2,1)} %pad_maximum_fusion.3), channel_id=1, source_target_pairs={{0,448},{1,65},{64,0},{65,129},{128,64},{129,193},{192,128},{193,2... | collective-permute-start | bytes 884744 | tf_op jit(solution)/shard_map/ppermute | solution.py:35
  28.8 12.3 %collective-permute-start.1 = (bf16[128,1152]{1,0:T(8,128)(2,1)}, bf16[128,1152]{1,0:T(8,128)(2,1)}, u32[]{:S(2)}, u32[]{:S(2)}) collective-permute-start(bf16[128,1152]{1,0:T(8,128)(2,1)} %pad_maximum_fusion.3), channel_id=1, source_target_pairs={{0,64},{1,449},{64,128},{65,1},{128,192},{129,65},{192,256},{193,1... | collective-permute-start | bytes 884744 | tf_op jit(solution)/shard_map/ppermute | solution.py:35
  33.6 27.6 %collective-permute-start.7 = (bf16[256,1152]{0,1:T(8,128)(2,1)S(1)}, bf16[256,1152]{0,1:T(8,128)(2,1)S(1)}, u32[]{:S(2)}, u32[]{:S(2)}) collective-permute-start(bf16[256,1152]{0,1:T(8,128)(2,1)S(1)} %constant_dynamic-slice_fusion), channel_id=1, source_target_pairs={{0,16},{16,0},{1,17},{17,1},{2,18},{18,2},{3,19},{19,3},{4,20},{20... | collective-permute-start | bytes 1769480 | tf_op jit(solution)/shard_map/ppermute | solution.py:15
  35.6 13.1 %collective-permute-start.4 = (bf16[128,1152]{1,0:T(8,128)(2,1)}, bf16[128,1152]{1,0:T(8,128)(2,1)S(1)}, u32[]{:S(2)}, u32[]{:S(2)}) collective-permute-start(bf16[128,1152]{1,0:T(8,128)(2,1)} %collective-permute-done.2), channel_id=1, source_target_pairs={{0,448},{1,65},{64,0},{65,129},{128,64},{129,193},{192,128},{193,2... | collective-permute-start | bytes 884744 | tf_op jit(solution)/shard_map/ppermute | solution.py:35
  41.1 13.1 %collective-permute-start.3 = (bf16[128,1152]{1,0:T(8,128)(2,1)}, bf16[128,1152]{1,0:T(8,128)(2,1)S(1)}, u32[]{:S(2)}, u32[]{:S(2)}) collective-permute-start(bf16[128,1152]{1,0:T(8,128)(2,1)} %collective-permute-done.1), channel_id=1, source_target_pairs={{0,64},{1,449},{64,128},{65,1},{128,192},{129,65},{192,256},{193,1... | collective-permute-start | bytes 884744 | tf_op jit(solution)/shard_map/ppermute | solution.py:35
  48.7 18.4 %collective-permute-start.6 = (bf16[128,1152]{1,0:T(8,128)(2,1)S(1)}, bf16[128,1152]{1,0:T(8,128)(2,1)S(1)}, u32[]{:S(2)}, u32[]{:S(2)}) collective-permute-start(bf16[128,1152]{1,0:T(8,128)(2,1)S(1)} %collective-permute-done.4), channel_id=1, source_target_pairs={{0,448},{1,65},{64,0},{65,129},{128,64},{129,193},{192,128},{193,2... | collective-permute-start | bytes 884744 | tf_op jit(solution)/shard_map/ppermute | solution.py:35
  54.2 10.3 %collective-permute-start.5 = (bf16[128,1152]{1,0:T(8,128)(2,1)S(1)}, bf16[128,1152]{1,0:T(8,128)(2,1)S(1)}, u32[]{:S(2)}, u32[]{:S(2)}) collective-permute-start(bf16[128,1152]{1,0:T(8,128)(2,1)S(1)} %collective-permute-done.3), channel_id=1, source_target_pairs={{0,64},{1,449},{64,128},{65,1},{128,192},{129,65},{192,256},{193,1... | collective-permute-start | bytes 884744 | tf_op jit(solution)/shard_map/ppermute | solution.py:35
  61.2 6.9 %collective-permute-start.8 = (bf16[256,1152]{0,1:T(8,128)(2,1)S(1)}, bf16[256,1152]{0,1:T(8,128)(2,1)S(1)}, u32[]{:S(2)}, u32[]{:S(2)}) collective-permute-start(bf16[256,1152]{0,1:T(8,128)(2,1)S(1)} %collective-permute-done.7), channel_id=1, source_target_pairs={{0,1},{1,0},{2,3},{3,2},{4,5},{5,4},{6,7},{7,6},{8,9},{9,8},{10,11... | collective-permute-start | bytes 1769480 | tf_op jit(solution)/shard_map/ppermute | solution.py:15
  64.5 10.3 %collective-permute-start.9 = (bf16[128,1152]{1,0:T(8,128)(2,1)S(1)}, bf16[128,1152]{1,0:T(8,128)(2,1)S(1)}, u32[]{:S(2)}, u32[]{:S(2)}) collective-permute-start(bf16[128,1152]{1,0:T(8,128)(2,1)S(1)} %collective-permute-done.5), channel_id=1, source_target_pairs={{0,64},{1,449},{64,128},{65,1},{128,192},{129,65},{192,256},{193,1... | collective-permute-start | bytes 884744 | tf_op jit(solution)/shard_map/ppermute | solution.py:35
  78.7 6.7 %collective-permute-start.10 = (bf16[8,72,1024]{2,1,0:T(8,128)(2,1)S(1)}, bf16[8,72,1024]{2,1,0:T(8,128)(2,1)S(1)}, u32[]{:S(2)}, u32[]{:S(2)}) collective-permute-start(bf16[8,72,1024]{2,1,0:T(8,128)(2,1)S(1)} %dynamic-slice_bitcast_fusion.1), channel_id=1, source_target_pairs={{0,1},{1,0},{2,3},{3,2},{4,5},{5,4},{6,7},{7,6},{8,9},{9,8},{10,11... | collective-permute-start | bytes 3538952 | tf_op jit(solution)/shard_map/ppermute | solution.py:15
  86.9 19.4 %all-to-all-start = ((bf16[8,72,1024]{2,1,0:T(8,128)(2,1)}), bf16[8,72,1024]{2,1,0:T(8,128)(2,1)S(1)}, u32[]{:S(2)}, u32[]{:S(2)}) async-start(bf16[8,72,1024]{2,1,0:T(8,128)(2,1)} %fusion.13), calls=%async_computation | async-start | bytes 2359296 | tf_op jit(solution)/shard_map/all_to_all | solution.py:70
  95.2 5.0 %collective-permute-start.12 = (bf16[8,72,1152]{2,1,0:T(8,128)(2,1)S(1)}, bf16[8,72,1152]{2,1,0:T(8,128)(2,1)S(1)}, u32[]{:S(2)}, u32[]{:S(2)}) collective-permute-start(bf16[8,72,1152]{2,1,0:T(8,128)(2,1)S(1)} %dynamic-slice_bitcast_fusion), channel_id=1, source_target_pairs={{0,1},{1,0},{2,3},{3,2},{4,5},{5,4},{6,7},{7,6},{8,9},{9,8},{10,11... | collective-permute-start | bytes 3981320 | tf_op jit(solution)/shard_map/ppermute | solution.py:15
  106.3 1.0 copy-start.1
  107.4 25.0 %all-to-all-start.1 = ((bf16[8,72,1152]{2,1,0:T(8,128)(2,1)}), bf16[8,72,1152]{2,1,0:T(8,128)(2,1)S(1)}, u32[]{:S(2)}, u32[]{:S(2)}) async-start(bf16[8,72,1152]{2,1,0:T(8,128)(2,1)} %fusion.9), calls=%async_computation.1 | async-start | bytes 2654208 | tf_op jit(solution)/shard_map/all_to_all | solution.py:70
  114.2 16.2 %collective-permute-start.11 = (f32[72,512]{1,0:T(8,128)S(1)}, f32[72,512]{1,0:T(8,128)S(1)}, u32[]{:S(2)}, u32[]{:S(2)}) collective-permute-start(f32[72,512]{1,0:T(8,128)S(1)} %slice.119), channel_id=1, source_target_pairs={{0,16},{16,0},{1,17},{17,1},{2,18},{18,2},{3,19},{19,3},{4,20},{20... | collective-permute-start | bytes 442376 | tf_op jit(solution)/shard_map/ppermute | solution.py:15

commit v5 on v4

--- a/solution.py
+++ b/solution.py
@@ -37,7 +37,8 @@
 
 def gather(text, feat, image_emb):
     rows = text.shape[0]
-    own = jnp.concatenate([text, feat], axis=0)
+    own = lax.optimization_barrier(jnp.concatenate([text, feat], axis=0))
+    text, feat = own[:rows], own[rows:]
     far = lax.ppermute(own, ("a", "b", "zl"), [(s, 7 - s) for s in range(8)])
     chunk = jnp.concatenate([text, far[:rows], feat, far[rows:]], axis=0)
     chunks = [chunk]
@@ -49,13 +50,14 @@
     for _ in range(3):
         up, down = ring_step(up, 1), ring_step(down, -1)
         chunks += [up, down]
+    mine = after(mine, up)
     theirs = shifted(mine, "c", 1)
     other = [jnp.where(core == 0, mine, theirs), jnp.where(core == 0, theirs, mine)]
-    last = ring_step(up, 1)
+    last = ring_step(down, -1)
     half = chunk.shape[0] // 2
     texts = jnp.concatenate([piece[:half] for piece in chunks], axis=0)
-    feats = jnp.concatenate([piece[half:] for piece in chunks + [last]], axis=0)
-    return texts, last[:half], feats, jnp.concatenate([image_emb] + other, axis=0)
+    feats = jnp.concatenate([piece[half:] for piece in chunks], axis=0)
+    return texts, feats, last, jnp.concatenate([image_emb] + other, axis=0)
 
 
 def core_sum(full):
@@ -93,7 +95,7 @@
     offset = logit_bias[0]
 
     own_feat = lax.dynamic_slice_in_dim(text_feat, column * own_rows, own_rows, 0)
-    texts, last_text, feats, images = gather(text_emb, own_feat, image_emb)
+    texts, feats, last, images = gather(text_emb, own_feat, image_emb)
     images_t = lax.optimization_barrier(images.T)
 
     image_unit, image_norm = normalize(images)
@@ -123,8 +125,9 @@
     weights = pair_weights(text_low, True)
     image_dir = image_direction(text_low, weights)
 
-    last_text = after(last_text, image_dir)
-    last_unit, last_norm = normalize(last_text)
+    last = after(last, image_dir)
+    half = last.shape[0] // 2
+    last_unit, last_norm = normalize(last[:half])
     last_low = last_unit.astype(jnp.bfloat16)
     last_weights = pair_weights(last_low, False)
     image_dir = image_dir + image_direction(last_low, last_weights)
@@ -134,12 +137,13 @@
     image_cols = image_two[:, :block] + shifted(image_two[:, block:], "b", 1)
     image_term = jnp.dot(image_cols.astype(jnp.bfloat16), image_feat, preferred_element_type=jnp.float32)
 
-    last_weights = after(last_weights, image_part)
-    text_part = jnp.concatenate(
-        [text_gradient(text_unit, text_norm, weights), text_gradient(last_unit, last_norm, last_weights)], axis=0
+    weights, last_weights = after((weights, last_weights), image_part)
+    parts = (text_gradient(text_unit, text_norm, weights), text_gradient(last_unit, last_norm, last_weights))
+    parts, last_feat = after((parts, last[half:]), image_slabs)
+    feats = jnp.concatenate([feats, last_feat], axis=0)
+    text_all = lax.dot_general(
+        jnp.concatenate(parts, axis=0), feats, (((0,), (0,)), ((), ())), preferred_element_type=jnp.float32
     )
-    text_part = after(text_part, image_slabs)
-    text_all = lax.dot_general(text_part, feats, (((0,), (0,)), ((), ())), preferred_element_type=jnp.float32)
     text_term = row_sum(core_sum(text_all.astype(jnp.bfloat16)))
 
     own = sum_over_dp(jnp.concatenate([image_term, text_term], axis=0).T)

time: 162 us -> 160 us (0.988)
    unnamed x14, local copies, waits for them, and re-layouts: 11.8 us -> 9.27 us
    ppermute x7, waiting for transfers between devices: 2.35 us -> 0.02 us  [ring_step(): return lax.ppermute(value, ('y', 'c'), pairs)]
    ppermute x7, starting transfers between devices: 24 us -> 26.3 us  [ring_step(): return lax.ppermute(value, ('y', 'c'), pairs)]
    ppermute x5, starting transfers between devices: 14.3 us -> 12.3 us  [shifted(): lax.ppermute(value, axis, [(s, (s + steps) % count) for s in range(count)])]
    ppermute x5, waiting for transfers between devices: 19.8 us -> 21.6 us  [shifted(): lax.ppermute(value, axis, [(s, (s + steps) % count) for s in range(count)])]
  transfers between devices with their start and end apart: 15 -> 15, of which waited for: 7 -> 6; matrix products, arithmetic and copies ran while one was open for 16% -> 15% of each run, Pallas kernels for 0% -> 0%
where the time goes in v5:
time: 160 us; the launch traced here: 158 us
  starting transfers between devices  59.3 us (37%)
  waiting for transfers between devices  34.5 us (22%)
  blocking collectives  25 us (16%)
  local copies, waits for them, and re-layouts  13.4 us (8%)
  other arithmetic  11.6 us (7%)
  matrix products  11.6 us (7%)
  between operations  2.32 us (1%)
    ppermute x7, starting transfers between devices, ring_step(): return lax.ppermute(value, ('y', 'c'), pairs)  26.3 us
    all_to_all x1, blocking collectives, sum_over_dp(): lax.all_to_all(jnp.concatenate([main, rest], axis=1), DP, 0, 0, tiled=True)  25 us
    ppermute x5, waiting for transfers between devices, shifted(): lax.ppermute(value, axis, [(s, (s + steps) % count) for s in range(count)])  21.6 us
    ppermute x5, starting transfers between devices, shifted(): lax.ppermute(value, axis, [(s, (s + steps) % count) for s in range(count)])  12.3 us
    ppermute x1, starting transfers between devices, gather(): far = lax.ppermute(own, ('a', 'b', 'zl'), [(s, 7 - s) for s in range(8)])  10.9 us
    all_to_all x2, starting transfers between devices, row_sum(): got = lax.all_to_all(slabs, ROW, 0, 0, tiled=True)  9.75 us
    unnamed x14, local copies, waits for them, and re-layouts  9.27 us
    all_to_all x2, waiting for transfers between devices, row_sum(): got = lax.all_to_all(slabs, ROW, 0, 0, tiled=True)  6.55 us
  transfers between devices with their start and end apart: 15, of which 6 were waited for; matrix products, arithmetic and copies ran while one was open for 15% of the time, Pallas kernels for 0%

profile of v5, /device:TPU:6, one launch (start us, length us, event | category | flops | bytes accessed | tf_op | source)
XLA Modules:
  0.0 157.8 jit_solution(17994205359206384444)
XLA Ops:
  2.5 10.9 %collective-permute-start = (bf16[64,1152]{1,0:T(8,128)(2,1)S(1)}, bf16[64,1152]{1,0:T(8,128)(2,1)S(1)}, u32[]{:S(2)}, u32[]{:S(2)}) collective-permute-start(bf16[64,1152]{1,0:T(8,128)(2,1)S(1)} %pad_maximum_fusion.3), channel_id=1, source_target_pairs={{0,56},{8,48},{16,40},{24,32},{32,24},{40,16},{48,8},{56,0},{1,57}... | collective-permute-start | bytes 442376 | tf_op jit(solution)/shard_map/ppermute | solution.py:42
  14.1 6.3 %collective-permute-done = bf16[64,1152]{1,0:T(8,128)(2,1)S(1)} collective-permute-done((bf16[64,1152]{1,0:T(8,128)(2,1)S(1)}, bf16[64,1152]{1,0:T(8,128)(2,1)S(1)}, u32[]{:S(2)}, u32[]{:S(2)}) %collective-permute-start) | collective-permute-done | bytes 147488 | tf_op jit(solution)/shard_map/ppermute | solution.py:42
  21.9 3.5 %collective-permute-start.1 = (bf16[128,1152]{1,0:T(8,128)(2,1)}, bf16[128,1152]{1,0:T(8,128)(2,1)}, u32[]{:S(2)}, u32[]{:S(2)}) collective-permute-start(bf16[128,1152]{1,0:T(8,128)(2,1)} %pad_maximum_fusion.2), channel_id=1, source_target_pairs={{0,64},{1,449},{64,128},{65,1},{128,192},{129,65},{192,256},{193,1... | collective-permute-start | bytes 884744 | tf_op jit(solution)/shard_map/ppermute | solution.py:35
  25.3 3.8 %collective-permute-start.2 = (bf16[128,1152]{1,0:T(8,128)(2,1)}, bf16[128,1152]{1,0:T(8,128)(2,1)}, u32[]{:S(2)}, u32[]{:S(2)}) collective-permute-start(bf16[128,1152]{1,0:T(8,128)(2,1)} %pad_maximum_fusion.2), channel_id=1, source_target_pairs={{0,448},{1,65},{64,0},{65,129},{128,64},{129,193},{192,128},{193,2... | collective-permute-start | bytes 884744 | tf_op jit(solution)/shard_map/ppermute | solution.py:35
  32.1 1.9 %collective-permute-start.7 = (bf16[256,1152]{0,1:T(8,128)(2,1)S(1)}, bf16[256,1152]{0,1:T(8,128)(2,1)S(1)}, u32[]{:S(2)}, u32[]{:S(2)}) collective-permute-start(bf16[256,1152]{0,1:T(8,128)(2,1)S(1)} %constant_dynamic-slice_fusion), channel_id=1, source_target_pairs={{0,16},{16,0},{1,17},{17,1},{2,18},{18,2},{3,19},{19,3},{4,20},{20... | collective-permute-start | bytes 1769480 | tf_op jit(solution)/shard_map/ppermute | solution.py:15
  34.0 2.0 %collective-permute-start.3 = (bf16[128,1152]{1,0:T(8,128)(2,1)}, bf16[128,1152]{1,0:T(8,128)(2,1)S(1)}, u32[]{:S(2)}, u32[]{:S(2)}) collective-permute-start(bf16[128,1152]{1,0:T(8,128)(2,1)} %collective-permute-done.1), channel_id=1, source_target_pairs={{0,64},{1,449},{64,128},{65,1},{128,192},{129,65},{192,256},{193,1... | collective-permute-start | bytes 884744 | tf_op jit(solution)/shard_map/ppermute | solution.py:35
  36.1 5.0 %collective-permute-start.4 = (bf16[128,1152]{1,0:T(8,128)(2,1)}, bf16[128,1152]{1,0:T(8,128)(2,1)S(1)}, u32[]{:S(2)}, u32[]{:S(2)}) collective-permute-start(bf16[128,1152]{1,0:T(8,128)(2,1)} %collective-permute-done.2), channel_id=1, source_target_pairs={{0,448},{1,65},{64,0},{65,129},{128,64},{129,193},{192,128},{193,2... | collective-permute-start | bytes 884744 | tf_op jit(solution)/shard_map/ppermute | solution.py:35
  41.1 1.7 %slice_dynamic-update-slice_fusion.11 = (bf16[448,1152]{1,0:T(8,128)(2,1)S(1)}, bf16[512,1152]{1,0:T(8,128)(2,1)}) fusion(bf16[448,1152]{1,0:T(8,128)(2,1)S(1)} %get-tuple-element.32, bf16[128,1152]{1,0:T(8,128)(2,1)} %collective-permute-done.1, bf16[512,1152]{1,0:T(8,128)(2,1)} %get-tuple-element.33), kind=kLoop, calls=%fused_computation.89 | loop fusion | bytes 589824
  44.5 2.1 %collective-permute-start.5 = (bf16[128,1152]{1,0:T(8,128)(2,1)S(1)}, bf16[128,1152]{1,0:T(8,128)(2,1)S(1)}, u32[]{:S(2)}, u32[]{:S(2)}) collective-permute-start(bf16[128,1152]{1,0:T(8,128)(2,1)S(1)} %collective-permute-done.3), channel_id=1, source_target_pairs={{0,64},{1,449},{64,128},{65,1},{128,192},{129,65},{192,256},{193,1... | collective-permute-start | bytes 884744 | tf_op jit(solution)/shard_map/ppermute | solution.py:35
  46.6 4.9 %collective-permute-start.6 = (bf16[128,1152]{1,0:T(8,128)(2,1)S(1)}, bf16[128,1152]{1,0:T(8,128)(2,1)S(1)}, u32[]{:S(2)}, u32[]{:S(2)}) collective-permute-start(bf16[128,1152]{1,0:T(8,128)(2,1)S(1)} %collective-permute-done.4), channel_id=1, source_target_pairs={{0,448},{1,65},{64,0},{65,129},{128,64},{129,193},{192,128},{193,2... | collective-permute-start | bytes 884744 | tf_op jit(solution)/shard_map/ppermute | solution.py:35
  52.9 6.8 %collective-permute-done.7 = bf16[256,1152]{0,1:T(8,128)(2,1)S(1)} collective-permute-done((bf16[256,1152]{0,1:T(8,128)(2,1)S(1)}, bf16[256,1152]{0,1:T(8,128)(2,1)S(1)}, u32[]{:S(2)}, u32[]{:S(2)}) %collective-permute-start.7) | collective-permute-done | bytes 589856 | tf_op jit(solution)/shard_map/ppermute | solution.py:15
  59.7 1.9 %collective-permute-start.8 = (bf16[256,1152]{0,1:T(8,128)(2,1)S(1)}, bf16[256,1152]{0,1:T(8,128)(2,1)S(1)}, u32[]{:S(2)}, u32[]{:S(2)}) collective-permute-start(bf16[256,1152]{0,1:T(8,128)(2,1)S(1)} %collective-permute-done.7), channel_id=1, source_target_pairs={{0,1},{1,0},{2,3},{3,2},{4,5},{5,4},{6,7},{7,6},{8,9},{9,8},{10,11... | collective-permute-start | bytes 1769480 | tf_op jit(solution)/shard_map/ppermute | solution.py:15
  61.6 4.9 %collective-permute-start.9 = (bf16[128,1152]{1,0:T(8,128)(2,1)S(1)}, bf16[128,1152]{1,0:T(8,128)(2,1)S(1)}, u32[]{:S(2)}, u32[]{:S(2)}) collective-permute-start(bf16[128,1152]{1,0:T(8,128)(2,1)S(1)} %collective-permute-done.6), channel_id=1, source_target_pairs={{0,448},{1,65},{64,0},{65,129},{128,64},{129,193},{192,128},{193,2... | collective-permute-start | bytes 884744 | tf_op jit(solution)/shard_map/ppermute | solution.py:35
  68.8 2.1 %fusion.20 = bf16[448,1024]{1,0:T(8,128)(2,1)S(1)} fusion(f32[1024]{0:T(1024)S(1)} %add_rsqrt_fusion.1, f32[]{:T(128)} %bitcast.28, f32[]{:T(128)} %bitcast.26, s32[448]{0:T(512)S(1)} %iota_add_fusion, f32[]{:T(128)S(6)} %neg.12, pred[448]{0:T(512)(128)(4,1)S(1)} %iota_compare_fusion.1, bf16[448,1152]{1,0:T(8,128)(2,1)S(1)} %get-tuple-element.20, ...), kind=kOutput, calls=%fused_computation.35 | convolution fusion | flops 1073913856 | bytes 4317132 | tf_op jit(solution)/shard_map/dot_general | solution.py:107
  77.5 2.1 %collective-permute-start.10 = (bf16[8,72,1024]{2,1,0:T(8,128)(2,1)S(1)}, bf16[8,72,1024]{2,1,0:T(8,128)(2,1)S(1)}, u32[]{:S(2)}, u32[]{:S(2)}) collective-permute-start(bf16[8,72,1024]{2,1,0:T(8,128)(2,1)S(1)} %dynamic-slice_bitcast_fusion.1), channel_id=1, source_target_pairs={{0,1},{1,0},{2,3},{3,2},{4,5},{5,4},{6,7},{7,6},{8,9},{9,8},{10,11... | collective-permute-start | bytes 3538952 | tf_op jit(solution)/shard_map/ppermute | solution.py:15
  84.2 4.8 %all-to-all-start = ((bf16[8,72,1024]{2,1,0:T(8,128)(2,1)}), bf16[8,72,1024]{2,1,0:T(8,128)(2,1)S(1)}, u32[]{:S(2)}, u32[]{:S(2)}) async-start(bf16[8,72,1024]{2,1,0:T(8,128)(2,1)} %fusion.13), calls=%async_computation | async-start | bytes 2359296 | tf_op jit(solution)/shard_map/all_to_all | solution.py:72
  89.7 3.3 %convolution_convert_fusion = bf16[1152,1152]{1,0:T(8,128)(2,1)S(1)} fusion(bf16[512,1152]{1,0:T(8,128)(2,1)} %constant_dynamic-update-slice_fusion.2, bf16[64,1152]{1,0:T(8,128)(2,1)S(1)} %fusion.70, bf16[448,1152]{1,0:T(8,128)(2,1)} %fusion.17), kind=kOutput, calls=%fused_computation | convolution fusion | flops 1362640896 | bytes 5013504 | tf_op jit(solution)/shard_map/dot_general | solution.py:144
  93.1 1.9 %collective-permute-start.12 = (bf16[8,72,1152]{2,1,0:T(8,128)(2,1)S(1)}, bf16[8,72,1152]{2,1,0:T(8,128)(2,1)S(1)}, u32[]{:S(2)}, u32[]{:S(2)}) collective-permute-start(bf16[8,72,1152]{2,1,0:T(8,128)(2,1)S(1)} %dynamic-slice_bitcast_fusion), channel_id=1, source_target_pairs={{0,1},{1,0},{2,3},{3,2},{4,5},{5,4},{6,7},{7,6},{8,9},{9,8},{10,11... | collective-permute-start | bytes 3981320 | tf_op jit(solution)/shard_map/ppermute | solution.py:15
  95.1 3.0 %collective-permute-done.12 = bf16[8,72,1152]{2,1,0:T(8,128)(2,1)S(1)} collective-permute-done((bf16[8,72,1152]{2,1,0:T(8,128)(2,1)S(1)}, bf16[8,72,1152]{2,1,0:T(8,128)(2,1)S(1)}, u32[]{:S(2)}, u32[]{:S(2)}) %collective-permute-start.12) | collective-permute-done | bytes 1327136 | tf_op jit(solution)/shard_map/ppermute | solution.py:15
  99.5 5.0 %all-to-all-done = bf16[8,72,1024]{2,1,0:T(8,128)(2,1)S(1)} async-done(((bf16[8,72,1024]{2,1,0:T(8,128)(2,1)}), bf16[8,72,1024]{2,1,0:T(8,128)(2,1)S(1)}, u32[]{:S(2)}, u32[]{:S(2)}) %all-to-all-start) | async-done | bytes 1179680 | tf_op jit(solution)/shard_map/all_to_all | solution.py:72
  105.6 5.0 %all-to-all-start.1 = ((bf16[8,72,1152]{2,1,0:T(8,128)(2,1)}), bf16[8,72,1152]{2,1,0:T(8,128)(2,1)S(1)}, u32[]{:S(2)}, u32[]{:S(2)}) async-start(bf16[8,72,1152]{2,1,0:T(8,128)(2,1)} %fusion.9), calls=%async_computation.1 | async-start | bytes 2654208 | tf_op jit(solution)/shard_map/all_to_all | solution.py:72
  112.1 4.5 %collective-permute-start.11 = (f32[72,512]{1,0:T(8,128)S(1)}, f32[72,512]{1,0:T(8,128)S(1)}, u32[]{:S(2)}, u32[]{:S(2)}) collective-permute-start(f32[72,512]{1,0:T(8,128)S(1)} %slice.128), channel_id=1, source_target_pairs={{0,16},{16,0},{1,17},{17,1},{2,18},{18,2},{3,19},{19,3},{4,20},{20... | collective-permute-start | bytes 442376 | tf_op jit(solution)/shard_map/ppermute | solution.py:15
  116.5 11.8 %collective-permute-done.11 = f32[72,512]{1,0:T(8,128)S(1)} collective-permute-done((f32[72,512]{1,0:T(8,128)S(1)}, f32[72,512]{1,0:T(8,128)S(1)}, u32[]{:S(2)}, u32[]{:S(2)}) %collective-permute-start.11) | collective-permute-done | bytes 147488 | tf_op jit(solution)/shard_map/ppermute | solution.py:15
  131.3 25.0 %all_to_all.15 = bf16[32,41,128]{2,1,0:T(8,128)(2,1)S(1)} all-to-all(bf16[32,41,128]{2,1,0:T(8,128)(2,1)S(1)} %pad_maximum_fusion.1), channel_id=1, replica_groups=mesh['y'=8,'a'=2,'b'=2,'zl'=2,'x'=4,'c'=2] {'y','a','b'}, dimensions={0} | all-to-all | bytes 671744 | tf_op jit(solution)/shard_map/all_to_all | solution.py:83
  (75 shorter events, 31.1 us)
Async XLA Ops:
  0.6 127.7 %copy-start = (bf16[512,1152]{1,0:T(8,128)(2,1)S(1)}, bf16[512,1152]{1,0:T(8,128)(2,1)}, u32[]{:S(2)}) copy-start(bf16[512,1152]{1,0:T(8,128)(2,1)} %param.8) | copy-start | bytes 3538948
  2.5 17.9 %collective-permute-start = (bf16[64,1152]{1,0:T(8,128)(2,1)S(1)}, bf16[64,1152]{1,0:T(8,128)(2,1)S(1)}, u32[]{:S(2)}, u32[]{:S(2)}) collective-permute-start(bf16[64,1152]{1,0:T(8,128)(2,1)S(1)} %pad_maximum_fusion.3), channel_id=1, source_target_pairs={{0,56},{8,48},{16,40},{24,32},{32,24},{40,16},{48,8},{56,0},{1,57}... | collective-permute-start | bytes 442376 | tf_op jit(solution)/shard_map/ppermute | solution.py:42
  21.9 12.2 %collective-permute-start.1 = (bf16[128,1152]{1,0:T(8,128)(2,1)}, bf16[128,1152]{1,0:T(8,128)(2,1)}, u32[]{:S(2)}, u32[]{:S(2)}) collective-permute-start(bf16[128,1152]{1,0:T(8,128)(2,1)} %pad_maximum_fusion.2), channel_id=1, source_target_pairs={{0,64},{1,449},{64,128},{65,1},{128,192},{129,65},{192,256},{193,1... | collective-permute-start | bytes 884744 | tf_op jit(solution)/shard_map/ppermute | solution.py:35
  25.3 10.7 %collective-permute-start.2 = (bf16[128,1152]{1,0:T(8,128)(2,1)}, bf16[128,1152]{1,0:T(8,128)(2,1)}, u32[]{:S(2)}, u32[]{:S(2)}) collective-permute-start(bf16[128,1152]{1,0:T(8,128)(2,1)} %pad_maximum_fusion.2), channel_id=1, source_target_pairs={{0,448},{1,65},{64,0},{65,129},{128,64},{129,193},{192,128},{193,2... | collective-permute-start | bytes 884744 | tf_op jit(solution)/shard_map/ppermute | solution.py:35
  32.1 27.6 %collective-permute-start.7 = (bf16[256,1152]{0,1:T(8,128)(2,1)S(1)}, bf16[256,1152]{0,1:T(8,128)(2,1)S(1)}, u32[]{:S(2)}, u32[]{:S(2)}) collective-permute-start(bf16[256,1152]{0,1:T(8,128)(2,1)S(1)} %constant_dynamic-slice_fusion), channel_id=1, source_target_pairs={{0,16},{16,0},{1,17},{17,1},{2,18},{18,2},{3,19},{19,3},{4,20},{20... | collective-permute-start | bytes 1769480 | tf_op jit(solution)/shard_map/ppermute | solution.py:15
  34.0 10.4 %collective-permute-start.3 = (bf16[128,1152]{1,0:T(8,128)(2,1)}, bf16[128,1152]{1,0:T(8,128)(2,1)S(1)}, u32[]{:S(2)}, u32[]{:S(2)}) collective-permute-start(bf16[128,1152]{1,0:T(8,128)(2,1)} %collective-permute-done.1), channel_id=1, source_target_pairs={{0,64},{1,449},{64,128},{65,1},{128,192},{129,65},{192,256},{193,1... | collective-permute-start | bytes 884744 | tf_op jit(solution)/shard_map/ppermute | solution.py:35
  36.1 10.5 %collective-permute-start.4 = (bf16[128,1152]{1,0:T(8,128)(2,1)}, bf16[128,1152]{1,0:T(8,128)(2,1)S(1)}, u32[]{:S(2)}, u32[]{:S(2)}) collective-permute-start(bf16[128,1152]{1,0:T(8,128)(2,1)} %collective-permute-done.2), channel_id=1, source_target_pairs={{0,448},{1,65},{64,0},{65,129},{128,64},{129,193},{192,128},{193,2... | collective-permute-start | bytes 884744 | tf_op jit(solution)/shard_map/ppermute | solution.py:35
  44.5 15.2 %collective-permute-start.5 = (bf16[128,1152]{1,0:T(8,128)(2,1)S(1)}, bf16[128,1152]{1,0:T(8,128)(2,1)S(1)}, u32[]{:S(2)}, u32[]{:S(2)}) collective-permute-start(bf16[128,1152]{1,0:T(8,128)(2,1)S(1)} %collective-permute-done.3), channel_id=1, source_target_pairs={{0,64},{1,449},{64,128},{65,1},{128,192},{129,65},{192,256},{193,1... | collective-permute-start | bytes 884744 | tf_op jit(solution)/shard_map/ppermute | solution.py:35
  46.6 15.0 %collective-permute-start.6 = (bf16[128,1152]{1,0:T(8,128)(2,1)S(1)}, bf16[128,1152]{1,0:T(8,128)(2,1)S(1)}, u32[]{:S(2)}, u32[]{:S(2)}) collective-permute-start(bf16[128,1152]{1,0:T(8,128)(2,1)S(1)} %collective-permute-done.4), channel_id=1, source_target_pairs={{0,448},{1,65},{64,0},{65,129},{128,64},{129,193},{192,128},{193,2... | collective-permute-start | bytes 884744 | tf_op jit(solution)/shard_map/ppermute | solution.py:35
  59.7 8.5 %collective-permute-start.8 = (bf16[256,1152]{0,1:T(8,128)(2,1)S(1)}, bf16[256,1152]{0,1:T(8,128)(2,1)S(1)}, u32[]{:S(2)}, u32[]{:S(2)}) collective-permute-start(bf16[256,1152]{0,1:T(8,128)(2,1)S(1)} %collective-permute-done.7), channel_id=1, source_target_pairs={{0,1},{1,0},{2,3},{3,2},{4,5},{5,4},{6,7},{7,6},{8,9},{9,8},{10,11... | collective-permute-start | bytes 1769480 | tf_op jit(solution)/shard_map/ppermute | solution.py:15
  61.6 11.2 %collective-permute-start.9 = (bf16[128,1152]{1,0:T(8,128)(2,1)S(1)}, bf16[128,1152]{1,0:T(8,128)(2,1)S(1)}, u32[]{:S(2)}, u32[]{:S(2)}) collective-permute-start(bf16[128,1152]{1,0:T(8,128)(2,1)S(1)} %collective-permute-done.6), channel_id=1, source_target_pairs={{0,448},{1,65},{64,0},{65,129},{128,64},{129,193},{192,128},{193,2... | collective-permute-start | bytes 884744 | tf_op jit(solution)/shard_map/ppermute | solution.py:35
  72.8 6.9 %copy-start.2 = (bf16[128,1152]{1,0:T(8,128)(2,1)}, bf16[128,1152]{1,0:T(8,128)(2,1)S(1)}, u32[]{:S(2)}) copy-start(bf16[128,1152]{1,0:T(8,128)(2,1)S(1)} %collective-permute-done.9) | copy-start | bytes 884740
  77.5 5.2 %collective-permute-start.10 = (bf16[8,72,1024]{2,1,0:T(8,128)(2,1)S(1)}, bf16[8,72,1024]{2,1,0:T(8,128)(2,1)S(1)}, u32[]{:S(2)}, u32[]{:S(2)}) collective-permute-start(bf16[8,72,1024]{2,1,0:T(8,128)(2,1)S(1)} %dynamic-slice_bitcast_fusion.1), channel_id=1, source_target_pairs={{0,1},{1,0},{2,3},{3,2},{4,5},{5,4},{6,7},{7,6},{8,9},{9,8},{10,11... | collective-permute-start | bytes 3538952 | tf_op jit(solution)/shard_map/ppermute | solution.py:15
  82.7 6.3 %slice-start = ((bf16[128,1152]{1,0:T(8,128)(2,1)}), bf16[64,1152]{1,0:T(8,128)(2,1)S(1)}, s32[]{:S(2)}) async-start(bf16[128,1152]{1,0:T(8,128)(2,1)} %copy-done.2), calls=%async_computation.3 | async-start | bytes 294912 | tf_op jit(solution)/shard_map/slice | solution.py:142
  84.2 20.3 %all-to-all-start = ((bf16[8,72,1024]{2,1,0:T(8,128)(2,1)}), bf16[8,72,1024]{2,1,0:T(8,128)(2,1)S(1)}, u32[]{:S(2)}, u32[]{:S(2)}) async-start(bf16[8,72,1024]{2,1,0:T(8,128)(2,1)} %fusion.13), calls=%async_computation | async-start | bytes 2359296 | tf_op jit(solution)/shard_map/all_to_all | solution.py:72
  93.1 5.0 %collective-permute-start.12 = (bf16[8,72,1152]{2,1,0:T(8,128)(2,1)S(1)}, bf16[8,72,1152]{2,1,0:T(8,128)(2,1)S(1)}, u32[]{:S(2)}, u32[]{:S(2)}) collective-permute-start(bf16[8,72,1152]{2,1,0:T(8,128)(2,1)S(1)} %dynamic-slice_bitcast_fusion), channel_id=1, source_target_pairs={{0,1},{1,0},{2,3},{3,2},{4,5},{5,4},{6,7},{7,6},{8,9},{9,8},{10,11... | collective-permute-start | bytes 3981320 | tf_op jit(solution)/shard_map/ppermute | solution.py:15
  104.6 1.0 copy-start.1
  105.6 24.6 %all-to-all-start.1 = ((bf16[8,72,1152]{2,1,0:T(8,128)(2,1)}), bf16[8,72,1152]{2,1,0:T(8,128)(2,1)S(1)}, u32[]{:S(2)}, u32[]{:S(2)}) async-start(bf16[8,72,1152]{2,1,0:T(8,128)(2,1)} %fusion.9), calls=%async_computation.1 | async-start | bytes 2654208 | tf_op jit(solution)/shard_map/all_to_all | solution.py:72
  112.1 16.3 %collective-permute-start.11 = (f32[72,512]{1,0:T(8,128)S(1)}, f32[72,512]{1,0:T(8,128)S(1)}, u32[]{:S(2)}, u32[]{:S(2)}) collective-permute-start(f32[72,512]{1,0:T(8,128)S(1)} %slice.128), channel_id=1, source_target_pairs={{0,16},{16,0},{1,17},{17,1},{2,18},{18,2},{3,19},{19,3},{4,20},{20... | collective-permute-start | bytes 442376 | tf_op jit(solution)/shard_map/ppermute | solution.py:15

commit v6 on v5

--- a/solution.py
+++ b/solution.py
@@ -39,13 +39,15 @@
     rows = text.shape[0]
     own = lax.optimization_barrier(jnp.concatenate([text, feat], axis=0))
     text, feat = own[:rows], own[rows:]
-    far = lax.ppermute(own, ("a", "b", "zl"), [(s, 7 - s) for s in range(8)])
-    chunk = jnp.concatenate([text, far[:rows], feat, far[rows:]], axis=0)
-    chunks = [chunk]
     core = lax.axis_index("c")
     part = image_emb.shape[0] // 2
     piece = lax.dynamic_slice_in_dim(image_emb, core * part, part, 0)
-    mine = shifted(after(piece, chunk), "b", 1)
+    far = lax.ppermute(own, ("a", "b", "zl"), [(s, 7 - s) for s in range(8)])
+    far, piece, own = lax.optimization_barrier((far, piece, own))
+    text, feat = own[:rows], own[rows:]
+    chunk = jnp.concatenate([text, far[:rows], feat, far[rows:]], axis=0)
+    chunks = [chunk]
+    mine = shifted(piece, "b", 1)
     up = down = chunk
     for _ in range(3):
         up, down = ring_step(up, 1), ring_step(down, -1)

time: 160 us -> 158 us (0.988)
    ppermute x1, waiting for transfers between devices: 6.33 us -> 4.61 us  [gather(): far = lax.ppermute(own, ('a', 'b', 'zl'), [(s, 7 - s) for s in range(8)])]
    unnamed x14 -> x12, local copies, waits for them, and re-layouts: 9.27 us -> 9.19 us
  transfers between devices with their start and end apart: 15 -> 15, of which waited for: 6 -> 7; matrix products, arithmetic and copies ran while one was open for 15% -> 15% of each run, Pallas kernels for 0% -> 0%
where the time goes in v6:
time: 158 us; the launch traced here: 156 us
  starting transfers between devices  59.2 us (37%)
  waiting for transfers between devices  33.7 us (21%)
  blocking collectives  24.5 us (16%)
  local copies, waits for them, and re-layouts  14.2 us (9%)
  matrix products  11.3 us (7%)
  other arithmetic  10.7 us (7%)
  between operations  2.33 us (1%)
    ppermute x7, starting transfers between devices, ring_step(): return lax.ppermute(value, ('y', 'c'), pairs)  26.4 us
    all_to_all x1, blocking collectives, sum_over_dp(): lax.all_to_all(jnp.concatenate([main, rest], axis=1), DP, 0, 0, tiled=True)  24.5 us
    ppermute x5, waiting for transfers between devices, shifted(): lax.ppermute(value, axis, [(s, (s + steps) % count) for s in range(count)])  22.3 us
    ppermute x5, starting transfers between devices, shifted(): lax.ppermute(value, axis, [(s, (s + steps) % count) for s in range(count)])  12.2 us
    ppermute x1, starting transfers between devices, gather(): far = lax.ppermute(own, ('a', 'b', 'zl'), [(s, 7 - s) for s in range(8)])  10.9 us
    all_to_all x2, starting transfers between devices, row_sum(): got = lax.all_to_all(slabs, ROW, 0, 0, tiled=True)  9.72 us
    unnamed x12, local copies, waits for them, and re-layouts  9.19 us
    all_to_all x2, waiting for transfers between devices, row_sum(): got = lax.all_to_all(slabs, ROW, 0, 0, tiled=True)  6.79 us
  transfers between devices with their start and end apart: 15, of which 7 were waited for; matrix products, arithmetic and copies ran while one was open for 15% of the time, Pallas kernels for 0%

profile of v6, /device:TPU:6, one launch (start us, length us, event | category | flops | bytes accessed | tf_op | source)
XLA Modules:
  0.0 155.9 jit_solution(5352706636544732401)
XLA Ops:
  2.5 10.9 %collective-permute-start = (bf16[64,1152]{1,0:T(8,128)(2,1)S(1)}, bf16[64,1152]{1,0:T(8,128)(2,1)}, u32[]{:S(2)}, u32[]{:S(2)}) collective-permute-start(bf16[64,1152]{1,0:T(8,128)(2,1)S(1)} %pad_maximum_fusion.3), channel_id=1, source_target_pairs={{0,56},{8,48},{16,40},{24,32},{32,24},{40,16},{48,8},{56,0},{1,57}... | collective-permute-start | bytes 442376 | tf_op jit(solution)/shard_map/ppermute | solution.py:45
  16.0 4.6 %collective-permute-done = bf16[64,1152]{1,0:T(8,128)(2,1)} collective-permute-done((bf16[64,1152]{1,0:T(8,128)(2,1)S(1)}, bf16[64,1152]{1,0:T(8,128)(2,1)}, u32[]{:S(2)}, u32[]{:S(2)}) %collective-permute-start) | collective-permute-done | bytes 147488 | tf_op jit(solution)/shard_map/ppermute | solution.py:45
  23.6 3.5 %collective-permute-start.1 = (bf16[128,1152]{1,0:T(8,128)(2,1)}, bf16[128,1152]{1,0:T(8,128)(2,1)}, u32[]{:S(2)}, u32[]{:S(2)}) collective-permute-start(bf16[128,1152]{1,0:T(8,128)(2,1)} %pad_maximum_fusion.2), channel_id=1, source_target_pairs={{0,64},{1,449},{64,128},{65,1},{128,192},{129,65},{192,256},{193,1... | collective-permute-start | bytes 884744 | tf_op jit(solution)/shard_map/ppermute | solution.py:35
  27.0 3.8 %collective-permute-start.2 = (bf16[128,1152]{1,0:T(8,128)(2,1)}, bf16[128,1152]{1,0:T(8,128)(2,1)}, u32[]{:S(2)}, u32[]{:S(2)}) collective-permute-start(bf16[128,1152]{1,0:T(8,128)(2,1)} %pad_maximum_fusion.2), channel_id=1, source_target_pairs={{0,448},{1,65},{64,0},{65,129},{128,64},{129,193},{192,128},{193,2... | collective-permute-start | bytes 884744 | tf_op jit(solution)/shard_map/ppermute | solution.py:35
  32.2 1.9 %collective-permute-start.7 = (bf16[256,1152]{0,1:T(8,128)(2,1)}, bf16[256,1152]{0,1:T(8,128)(2,1)S(1)}, u32[]{:S(2)}, u32[]{:S(2)}) collective-permute-start(bf16[256,1152]{0,1:T(8,128)(2,1)} %constant_dynamic-slice_fusion), channel_id=1, source_target_pairs={{0,16},{16,0},{1,17},{17,1},{2,18},{18,2},{3,19},{19,3},{4,20},{20... | collective-permute-start | bytes 1769480 | tf_op jit(solution)/shard_map/ppermute | solution.py:15
  34.1 2.9 %collective-permute-start.3 = (bf16[128,1152]{1,0:T(8,128)(2,1)}, bf16[128,1152]{1,0:T(8,128)(2,1)S(1)}, u32[]{:S(2)}, u32[]{:S(2)}) collective-permute-start(bf16[128,1152]{1,0:T(8,128)(2,1)} %collective-permute-done.1), channel_id=1, source_target_pairs={{0,64},{1,449},{64,128},{65,1},{128,192},{129,65},{192,256},{193,1... | collective-permute-start | bytes 884744 | tf_op jit(solution)/shard_map/ppermute | solution.py:35
  37.0 4.2 %collective-permute-start.4 = (bf16[128,1152]{1,0:T(8,128)(2,1)}, bf16[128,1152]{1,0:T(8,128)(2,1)S(1)}, u32[]{:S(2)}, u32[]{:S(2)}) collective-permute-start(bf16[128,1152]{1,0:T(8,128)(2,1)} %collective-permute-done.2), channel_id=1, source_target_pairs={{0,448},{1,65},{64,0},{65,129},{128,64},{129,193},{192,128},{193,2... | collective-permute-start | bytes 884744 | tf_op jit(solution)/shard_map/ppermute | solution.py:35
  41.3 1.7 %slice_dynamic-update-slice_fusion.11 = (bf16[448,1152]{1,0:T(8,128)(2,1)S(1)}, bf16[512,1152]{1,0:T(8,128)(2,1)}) fusion(bf16[448,1152]{1,0:T(8,128)(2,1)S(1)} %get-tuple-element.36, bf16[128,1152]{1,0:T(8,128)(2,1)} %collective-permute-done.1, bf16[512,1152]{1,0:T(8,128)(2,1)} %get-tuple-element.37), kind=kLoop, calls=%fused_computation.89 | loop fusion | bytes 589824
  44.6 4.2 %collective-permute-start.5 = (bf16[128,1152]{1,0:T(8,128)(2,1)S(1)}, bf16[128,1152]{1,0:T(8,128)(2,1)S(1)}, u32[]{:S(2)}, u32[]{:S(2)}) collective-permute-start(bf16[128,1152]{1,0:T(8,128)(2,1)S(1)} %collective-permute-done.3), channel_id=1, source_target_pairs={{0,64},{1,449},{64,128},{65,1},{128,192},{129,65},{192,256},{193,1... | collective-permute-start | bytes 884744 | tf_op jit(solution)/shard_map/ppermute | solution.py:35
  48.8 2.9 %collective-permute-start.6 = (bf16[128,1152]{1,0:T(8,128)(2,1)S(1)}, bf16[128,1152]{1,0:T(8,128)(2,1)S(1)}, u32[]{:S(2)}, u32[]{:S(2)}) collective-permute-start(bf16[128,1152]{1,0:T(8,128)(2,1)S(1)} %collective-permute-done.4), channel_id=1, source_target_pairs={{0,448},{1,65},{64,0},{65,129},{128,64},{129,193},{192,128},{193,2... | collective-permute-start | bytes 884744 | tf_op jit(solution)/shard_map/ppermute | solution.py:35
  53.0 6.9 %collective-permute-done.7 = bf16[256,1152]{0,1:T(8,128)(2,1)S(1)} collective-permute-done((bf16[256,1152]{0,1:T(8,128)(2,1)}, bf16[256,1152]{0,1:T(8,128)(2,1)S(1)}, u32[]{:S(2)}, u32[]{:S(2)}) %collective-permute-start.7) | collective-permute-done | bytes 589856 | tf_op jit(solution)/shard_map/ppermute | solution.py:15
  60.0 1.9 %collective-permute-start.8 = (bf16[256,1152]{0,1:T(8,128)(2,1)S(1)}, bf16[256,1152]{0,1:T(8,128)(2,1)S(1)}, u32[]{:S(2)}, u32[]{:S(2)}) collective-permute-start(bf16[256,1152]{0,1:T(8,128)(2,1)S(1)} %collective-permute-done.7), channel_id=1, source_target_pairs={{0,1},{1,0},{2,3},{3,2},{4,5},{5,4},{6,7},{7,6},{8,9},{9,8},{10,11... | collective-permute-start | bytes 1769480 | tf_op jit(solution)/shard_map/ppermute | solution.py:15
  61.9 4.9 %collective-permute-start.9 = (bf16[128,1152]{1,0:T(8,128)(2,1)S(1)}, bf16[128,1152]{1,0:T(8,128)(2,1)S(1)}, u32[]{:S(2)}, u32[]{:S(2)}) collective-permute-start(bf16[128,1152]{1,0:T(8,128)(2,1)S(1)} %collective-permute-done.6), channel_id=1, source_target_pairs={{0,448},{1,65},{64,0},{65,129},{128,64},{129,193},{192,128},{193,2... | collective-permute-start | bytes 884744 | tf_op jit(solution)/shard_map/ppermute | solution.py:35
  69.1 2.1 %fusion.20 = bf16[448,1024]{1,0:T(8,128)(2,1)S(1)} fusion(f32[1024]{0:T(1024)S(1)} %add_rsqrt_fusion.1, f32[]{:T(128)} %bitcast.28, f32[]{:T(128)} %bitcast.26, s32[448]{0:T(512)S(1)} %iota_add_fusion, f32[]{:T(128)S(6)} %neg.12, pred[448]{0:T(512)(128)(4,1)S(1)} %iota_compare_fusion.1, bf16[448,1152]{1,0:T(8,128)(2,1)S(1)} %get-tuple-element.24, ...), kind=kOutput, calls=%fused_computation.35 | convolution fusion | flops 1073913856 | bytes 4317132 | tf_op jit(solution)/shard_map/dot_general | solution.py:109
  77.8 2.1 %collective-permute-start.10 = (bf16[8,72,1024]{2,1,0:T(8,128)(2,1)S(1)}, bf16[8,72,1024]{2,1,0:T(8,128)(2,1)S(1)}, u32[]{:S(2)}, u32[]{:S(2)}) collective-permute-start(bf16[8,72,1024]{2,1,0:T(8,128)(2,1)S(1)} %dynamic-slice_bitcast_fusion.1), channel_id=1, source_target_pairs={{0,1},{1,0},{2,3},{3,2},{4,5},{5,4},{6,7},{7,6},{8,9},{9,8},{10,11... | collective-permute-start | bytes 3538952 | tf_op jit(solution)/shard_map/ppermute | solution.py:15
  84.1 4.8 %all-to-all-start = ((bf16[8,72,1024]{2,1,0:T(8,128)(2,1)}), bf16[8,72,1024]{2,1,0:T(8,128)(2,1)}, u32[]{:S(2)}, u32[]{:S(2)}) async-start(bf16[8,72,1024]{2,1,0:T(8,128)(2,1)} %fusion.13), calls=%async_computation | async-start | bytes 2359296 | tf_op jit(solution)/shard_map/all_to_all | solution.py:74
  89.5 3.0 %convolution_convert_fusion = bf16[1152,1152]{1,0:T(8,128)(2,1)S(1)} fusion(bf16[512,1152]{1,0:T(8,128)(2,1)} %constant_dynamic-update-slice_fusion.2, bf16[64,1152]{1,0:T(8,128)(2,1)S(1)} %fusion.70, bf16[448,1152]{1,0:T(8,128)(2,1)S(1)} %fusion.17), kind=kOutput, calls=%fused_computation | convolution fusion | flops 1362640896 | bytes 5013504 | tf_op jit(solution)/shard_map/dot_general | solution.py:146
  92.6 1.9 %collective-permute-start.12 = (bf16[8,72,1152]{2,1,0:T(8,128)(2,1)S(1)}, bf16[8,72,1152]{2,1,0:T(8,128)(2,1)S(1)}, u32[]{:S(2)}, u32[]{:S(2)}) collective-permute-start(bf16[8,72,1152]{2,1,0:T(8,128)(2,1)S(1)} %dynamic-slice_bitcast_fusion), channel_id=1, source_target_pairs={{0,1},{1,0},{2,3},{3,2},{4,5},{5,4},{6,7},{7,6},{8,9},{9,8},{10,11... | collective-permute-start | bytes 3981320 | tf_op jit(solution)/shard_map/ppermute | solution.py:15
  94.5 3.0 %collective-permute-done.12 = bf16[8,72,1152]{2,1,0:T(8,128)(2,1)S(1)} collective-permute-done((bf16[8,72,1152]{2,1,0:T(8,128)(2,1)S(1)}, bf16[8,72,1152]{2,1,0:T(8,128)(2,1)S(1)}, u32[]{:S(2)}, u32[]{:S(2)}) %collective-permute-start.12) | collective-permute-done | bytes 1327136 | tf_op jit(solution)/shard_map/ppermute | solution.py:15
  99.0 5.3 %all-to-all-done = bf16[8,72,1024]{2,1,0:T(8,128)(2,1)} async-done(((bf16[8,72,1024]{2,1,0:T(8,128)(2,1)}), bf16[8,72,1024]{2,1,0:T(8,128)(2,1)}, u32[]{:S(2)}, u32[]{:S(2)}) %all-to-all-start) | async-done | bytes 1179680 | tf_op jit(solution)/shard_map/all_to_all | solution.py:74
  104.3 4.9 %all-to-all-start.1 = ((bf16[8,72,1152]{2,1,0:T(8,128)(2,1)}), bf16[8,72,1152]{2,1,0:T(8,128)(2,1)S(1)}, u32[]{:S(2)}, u32[]{:S(2)}) async-start(bf16[8,72,1152]{2,1,0:T(8,128)(2,1)} %fusion.9), calls=%async_computation.1 | async-start | bytes 2654208 | tf_op jit(solution)/shard_map/all_to_all | solution.py:74
  110.7 4.3 %collective-permute-start.11 = (f32[72,512]{1,0:T(8,128)S(1)}, f32[72,512]{1,0:T(8,128)S(1)}, u32[]{:S(2)}, u32[]{:S(2)}) collective-permute-start(f32[72,512]{1,0:T(8,128)S(1)} %slice.124), channel_id=1, source_target_pairs={{0,16},{16,0},{1,17},{17,1},{2,18},{18,2},{3,19},{19,3},{4,20},{20... | collective-permute-start | bytes 442376 | tf_op jit(solution)/shard_map/ppermute | solution.py:15
  115.1 11.9 %collective-permute-done.11 = f32[72,512]{1,0:T(8,128)S(1)} collective-permute-done((f32[72,512]{1,0:T(8,128)S(1)}, f32[72,512]{1,0:T(8,128)S(1)}, u32[]{:S(2)}, u32[]{:S(2)}) %collective-permute-start.11) | collective-permute-done | bytes 147488 | tf_op jit(solution)/shard_map/ppermute | solution.py:15
  130.0 24.5 %all_to_all.15 = bf16[32,41,128]{2,1,0:T(8,128)(2,1)S(1)} all-to-all(bf16[32,41,128]{2,1,0:T(8,128)(2,1)S(1)} %pad_maximum_fusion.1), channel_id=1, replica_groups=mesh['y'=8,'a'=2,'b'=2,'zl'=2,'x'=4,'c'=2] {'y','a','b'}, dimensions={0} | all-to-all | bytes 671744 | tf_op jit(solution)/shard_map/all_to_all | solution.py:85
  (73 shorter events, 31.4 us)
Async XLA Ops:
  0.6 126.3 %copy-start = (bf16[512,1152]{1,0:T(8,128)(2,1)S(1)}, bf16[512,1152]{1,0:T(8,128)(2,1)}, u32[]{:S(2)}) copy-start(bf16[512,1152]{1,0:T(8,128)(2,1)} %param.8) | copy-start | bytes 3538948
  2.5 18.0 %collective-permute-start = (bf16[64,1152]{1,0:T(8,128)(2,1)S(1)}, bf16[64,1152]{1,0:T(8,128)(2,1)}, u32[]{:S(2)}, u32[]{:S(2)}) collective-permute-start(bf16[64,1152]{1,0:T(8,128)(2,1)S(1)} %pad_maximum_fusion.3), channel_id=1, source_target_pairs={{0,56},{8,48},{16,40},{24,32},{32,24},{40,16},{48,8},{56,0},{1,57}... | collective-permute-start | bytes 442376 | tf_op jit(solution)/shard_map/ppermute | solution.py:45
  23.6 10.6 %collective-permute-start.1 = (bf16[128,1152]{1,0:T(8,128)(2,1)}, bf16[128,1152]{1,0:T(8,128)(2,1)}, u32[]{:S(2)}, u32[]{:S(2)}) collective-permute-start(bf16[128,1152]{1,0:T(8,128)(2,1)} %pad_maximum_fusion.2), channel_id=1, source_target_pairs={{0,64},{1,449},{64,128},{65,1},{128,192},{129,65},{192,256},{193,1... | collective-permute-start | bytes 884744 | tf_op jit(solution)/shard_map/ppermute | solution.py:35
  27.0 10.0 %collective-permute-start.2 = (bf16[128,1152]{1,0:T(8,128)(2,1)}, bf16[128,1152]{1,0:T(8,128)(2,1)}, u32[]{:S(2)}, u32[]{:S(2)}) collective-permute-start(bf16[128,1152]{1,0:T(8,128)(2,1)} %pad_maximum_fusion.2), channel_id=1, source_target_pairs={{0,448},{1,65},{64,0},{65,129},{128,64},{129,193},{192,128},{193,2... | collective-permute-start | bytes 884744 | tf_op jit(solution)/shard_map/ppermute | solution.py:35
  32.2 27.8 %collective-permute-start.7 = (bf16[256,1152]{0,1:T(8,128)(2,1)}, bf16[256,1152]{0,1:T(8,128)(2,1)S(1)}, u32[]{:S(2)}, u32[]{:S(2)}) collective-permute-start(bf16[256,1152]{0,1:T(8,128)(2,1)} %constant_dynamic-slice_fusion), channel_id=1, source_target_pairs={{0,16},{16,0},{1,17},{17,1},{2,18},{18,2},{3,19},{19,3},{4,20},{20... | collective-permute-start | bytes 1769480 | tf_op jit(solution)/shard_map/ppermute | solution.py:15
  34.1 10.5 %collective-permute-start.3 = (bf16[128,1152]{1,0:T(8,128)(2,1)}, bf16[128,1152]{1,0:T(8,128)(2,1)S(1)}, u32[]{:S(2)}, u32[]{:S(2)}) collective-permute-start(bf16[128,1152]{1,0:T(8,128)(2,1)} %collective-permute-done.1), channel_id=1, source_target_pairs={{0,64},{1,449},{64,128},{65,1},{128,192},{129,65},{192,256},{193,1... | collective-permute-start | bytes 884744 | tf_op jit(solution)/shard_map/ppermute | solution.py:35
  37.0 11.8 %collective-permute-start.4 = (bf16[128,1152]{1,0:T(8,128)(2,1)}, bf16[128,1152]{1,0:T(8,128)(2,1)S(1)}, u32[]{:S(2)}, u32[]{:S(2)}) collective-permute-start(bf16[128,1152]{1,0:T(8,128)(2,1)} %collective-permute-done.2), channel_id=1, source_target_pairs={{0,448},{1,65},{64,0},{65,129},{128,64},{129,193},{192,128},{193,2... | collective-permute-start | bytes 884744 | tf_op jit(solution)/shard_map/ppermute | solution.py:35
  44.6 15.4 %collective-permute-start.5 = (bf16[128,1152]{1,0:T(8,128)(2,1)S(1)}, bf16[128,1152]{1,0:T(8,128)(2,1)S(1)}, u32[]{:S(2)}, u32[]{:S(2)}) collective-permute-start(bf16[128,1152]{1,0:T(8,128)(2,1)S(1)} %collective-permute-done.3), channel_id=1, source_target_pairs={{0,64},{1,449},{64,128},{65,1},{128,192},{129,65},{192,256},{193,1... | collective-permute-start | bytes 884744 | tf_op jit(solution)/shard_map/ppermute | solution.py:35
  48.8 13.1 %collective-permute-start.6 = (bf16[128,1152]{1,0:T(8,128)(2,1)S(1)}, bf16[128,1152]{1,0:T(8,128)(2,1)S(1)}, u32[]{:S(2)}, u32[]{:S(2)}) collective-permute-start(bf16[128,1152]{1,0:T(8,128)(2,1)S(1)} %collective-permute-done.4), channel_id=1, source_target_pairs={{0,448},{1,65},{64,0},{65,129},{128,64},{129,193},{192,128},{193,2... | collective-permute-start | bytes 884744 | tf_op jit(solution)/shard_map/ppermute | solution.py:35
  60.0 8.5 %collective-permute-start.8 = (bf16[256,1152]{0,1:T(8,128)(2,1)S(1)}, bf16[256,1152]{0,1:T(8,128)(2,1)S(1)}, u32[]{:S(2)}, u32[]{:S(2)}) collective-permute-start(bf16[256,1152]{0,1:T(8,128)(2,1)S(1)} %collective-permute-done.7), channel_id=1, source_target_pairs={{0,1},{1,0},{2,3},{3,2},{4,5},{5,4},{6,7},{7,6},{8,9},{9,8},{10,11... | collective-permute-start | bytes 1769480 | tf_op jit(solution)/shard_map/ppermute | solution.py:15
  61.9 11.2 %collective-permute-start.9 = (bf16[128,1152]{1,0:T(8,128)(2,1)S(1)}, bf16[128,1152]{1,0:T(8,128)(2,1)S(1)}, u32[]{:S(2)}, u32[]{:S(2)}) collective-permute-start(bf16[128,1152]{1,0:T(8,128)(2,1)S(1)} %collective-permute-done.6), channel_id=1, source_target_pairs={{0,448},{1,65},{64,0},{65,129},{128,64},{129,193},{192,128},{193,2... | collective-permute-start | bytes 884744 | tf_op jit(solution)/shard_map/ppermute | solution.py:35
  73.2 6.9 %copy-start.1 = (bf16[128,1152]{1,0:T(8,128)(2,1)}, bf16[128,1152]{1,0:T(8,128)(2,1)S(1)}, u32[]{:S(2)}) copy-start(bf16[128,1152]{1,0:T(8,128)(2,1)S(1)} %collective-permute-done.9) | copy-start | bytes 884740
  77.8 4.7 %collective-permute-start.10 = (bf16[8,72,1024]{2,1,0:T(8,128)(2,1)S(1)}, bf16[8,72,1024]{2,1,0:T(8,128)(2,1)S(1)}, u32[]{:S(2)}, u32[]{:S(2)}) collective-permute-start(bf16[8,72,1024]{2,1,0:T(8,128)(2,1)S(1)} %dynamic-slice_bitcast_fusion.1), channel_id=1, source_target_pairs={{0,1},{1,0},{2,3},{3,2},{4,5},{5,4},{6,7},{7,6},{8,9},{9,8},{10,11... | collective-permute-start | bytes 3538952 | tf_op jit(solution)/shard_map/ppermute | solution.py:15
  82.1 6.7 %slice-start = ((bf16[128,1152]{1,0:T(8,128)(2,1)}), bf16[64,1152]{1,0:T(8,128)(2,1)S(1)}, s32[]{:S(2)}) async-start(bf16[128,1152]{1,0:T(8,128)(2,1)} %copy-done.1), calls=%async_computation.3 | async-start | bytes 294912 | tf_op jit(solution)/shard_map/slice | solution.py:144
  84.1 20.2 %all-to-all-start = ((bf16[8,72,1024]{2,1,0:T(8,128)(2,1)}), bf16[8,72,1024]{2,1,0:T(8,128)(2,1)}, u32[]{:S(2)}, u32[]{:S(2)}) async-start(bf16[8,72,1024]{2,1,0:T(8,128)(2,1)} %fusion.13), calls=%async_computation | async-start | bytes 2359296 | tf_op jit(solution)/shard_map/all_to_all | solution.py:74
  92.6 5.0 %collective-permute-start.12 = (bf16[8,72,1152]{2,1,0:T(8,128)(2,1)S(1)}, bf16[8,72,1152]{2,1,0:T(8,128)(2,1)S(1)}, u32[]{:S(2)}, u32[]{:S(2)}) collective-permute-start(bf16[8,72,1152]{2,1,0:T(8,128)(2,1)S(1)} %dynamic-slice_bitcast_fusion), channel_id=1, source_target_pairs={{0,1},{1,0},{2,3},{3,2},{4,5},{5,4},{6,7},{7,6},{8,9},{9,8},{10,11... | collective-permute-start | bytes 3981320 | tf_op jit(solution)/shard_map/ppermute | solution.py:15
  104.3 24.6 %all-to-all-start.1 = ((bf16[8,72,1152]{2,1,0:T(8,128)(2,1)}), bf16[8,72,1152]{2,1,0:T(8,128)(2,1)S(1)}, u32[]{:S(2)}, u32[]{:S(2)}) async-start(bf16[8,72,1152]{2,1,0:T(8,128)(2,1)} %fusion.9), calls=%async_computation.1 | async-start | bytes 2654208 | tf_op jit(solution)/shard_map/all_to_all | solution.py:74
  110.7 16.2 %collective-permute-start.11 = (f32[72,512]{1,0:T(8,128)S(1)}, f32[72,512]{1,0:T(8,128)S(1)}, u32[]{:S(2)}, u32[]{:S(2)}) collective-permute-start(f32[72,512]{1,0:T(8,128)S(1)} %slice.124), channel_id=1, source_target_pairs={{0,16},{16,0},{1,17},{17,1},{2,18},{18,2},{3,19},{19,3},{4,20},{20... | collective-permute-start | bytes 442376 | tf_op jit(solution)/shard_map/ppermute | solution.py:15

commit v7 on v6

--- a/solution.py
+++ b/solution.py
@@ -136,7 +136,8 @@
     image_part = unit_back(image_dir, image_unit_t, image_norm_t, 0).astype(jnp.bfloat16)
     image_slabs = core_sum(image_part)
     image_two = row_sum(image_slabs)
-    image_cols = image_two[:, :block] + shifted(image_two[:, block:], "b", 1)
+    far_sums = shifted(image_two[:, block:].astype(jnp.bfloat16), "b", 1)
+    image_cols = image_two[:, :block] + far_sums.astype(jnp.float32)
     image_term = jnp.dot(image_cols.astype(jnp.bfloat16), image_feat, preferred_element_type=jnp.float32)
 
     weights, last_weights = after((weights, last_weights), image_part)

time: 158 us -> 157 us (level)
    ppermute x5, waiting for transfers between devices: 22.3 us -> 20.7 us  [shifted(): lax.ppermute(value, axis, [(s, (s + steps) % count) for s in range(count)])]
where the time goes in v7:
time: 157 us; the launch traced here: 154 us
  starting transfers between devices  59.2 us (38%)
  waiting for transfers between devices  32.2 us (21%)
  blocking collectives  24.5 us (16%)
  local copies, waits for them, and re-layouts  14.2 us (9%)
  matrix products  11.3 us (7%)
  other arithmetic  10.7 us (7%)
  between operations  2.34 us (1%)
    ppermute x7, starting transfers between devices, ring_step(): return lax.ppermute(value, ('y', 'c'), pairs)  26.4 us
    all_to_all x1, blocking collectives, sum_over_dp(): lax.all_to_all(jnp.concatenate([main, rest], axis=1), DP, 0, 0, tiled=True)  24.5 us
    ppermute x5, waiting for transfers between devices, shifted(): lax.ppermute(value, axis, [(s, (s + steps) % count) for s in range(count)])  20.7 us
    ppermute x5, starting transfers between devices, shifted(): lax.ppermute(value, axis, [(s, (s + steps) % count) for s in range(count)])  12.2 us
    ppermute x1, starting transfers between devices, gather(): far = lax.ppermute(own, ('a', 'b', 'zl'), [(s, 7 - s) for s in range(8)])  10.9 us
    all_to_all x2, starting transfers between devices, row_sum(): got = lax.all_to_all(slabs, ROW, 0, 0, tiled=True)  9.72 us
    unnamed x12, local copies, waits for them, and re-layouts  9.19 us
    all_to_all x2, waiting for transfers between devices, row_sum(): got = lax.all_to_all(slabs, ROW, 0, 0, tiled=True)  6.88 us
  transfers between devices with their start and end apart: 15, of which 7 were waited for; matrix products, arithmetic and copies ran while one was open for 15% of the time, Pallas kernels for 0%

profile of v7, /device:TPU:6, one launch (start us, length us, event | category | flops | bytes accessed | tf_op | source)
XLA Modules:
  0.0 154.4 jit_solution(8609500933674541041)
XLA Ops:
  2.5 10.9 %collective-permute-start = (bf16[64,1152]{1,0:T(8,128)(2,1)S(1)}, bf16[64,1152]{1,0:T(8,128)(2,1)}, u32[]{:S(2)}, u32[]{:S(2)}) collective-permute-start(bf16[64,1152]{1,0:T(8,128)(2,1)S(1)} %pad_maximum_fusion.3), channel_id=1, source_target_pairs={{0,56},{8,48},{16,40},{24,32},{32,24},{40,16},{48,8},{56,0},{1,57}... | collective-permute-start | bytes 442376 | tf_op jit(solution)/shard_map/ppermute | solution.py:45
  16.0 4.6 %collective-permute-done = bf16[64,1152]{1,0:T(8,128)(2,1)} collective-permute-done((bf16[64,1152]{1,0:T(8,128)(2,1)S(1)}, bf16[64,1152]{1,0:T(8,128)(2,1)}, u32[]{:S(2)}, u32[]{:S(2)}) %collective-permute-start) | collective-permute-done | bytes 147488 | tf_op jit(solution)/shard_map/ppermute | solution.py:45
  23.6 3.5 %collective-permute-start.1 = (bf16[128,1152]{1,0:T(8,128)(2,1)}, bf16[128,1152]{1,0:T(8,128)(2,1)}, u32[]{:S(2)}, u32[]{:S(2)}) collective-permute-start(bf16[128,1152]{1,0:T(8,128)(2,1)} %pad_maximum_fusion.2), channel_id=1, source_target_pairs={{0,64},{1,449},{64,128},{65,1},{128,192},{129,65},{192,256},{193,1... | collective-permute-start | bytes 884744 | tf_op jit(solution)/shard_map/ppermute | solution.py:35
  27.0 3.8 %collective-permute-start.2 = (bf16[128,1152]{1,0:T(8,128)(2,1)}, bf16[128,1152]{1,0:T(8,128)(2,1)}, u32[]{:S(2)}, u32[]{:S(2)}) collective-permute-start(bf16[128,1152]{1,0:T(8,128)(2,1)} %pad_maximum_fusion.2), channel_id=1, source_target_pairs={{0,448},{1,65},{64,0},{65,129},{128,64},{129,193},{192,128},{193,2... | collective-permute-start | bytes 884744 | tf_op jit(solution)/shard_map/ppermute | solution.py:35
  32.2 1.9 %collective-permute-start.7 = (bf16[256,1152]{0,1:T(8,128)(2,1)}, bf16[256,1152]{0,1:T(8,128)(2,1)S(1)}, u32[]{:S(2)}, u32[]{:S(2)}) collective-permute-start(bf16[256,1152]{0,1:T(8,128)(2,1)} %constant_dynamic-slice_fusion), channel_id=1, source_target_pairs={{0,16},{16,0},{1,17},{17,1},{2,18},{18,2},{3,19},{19,3},{4,20},{20... | collective-permute-start | bytes 1769480 | tf_op jit(solution)/shard_map/ppermute | solution.py:15
  34.1 2.9 %collective-permute-start.3 = (bf16[128,1152]{1,0:T(8,128)(2,1)}, bf16[128,1152]{1,0:T(8,128)(2,1)S(1)}, u32[]{:S(2)}, u32[]{:S(2)}) collective-permute-start(bf16[128,1152]{1,0:T(8,128)(2,1)} %collective-permute-done.1), channel_id=1, source_target_pairs={{0,64},{1,449},{64,128},{65,1},{128,192},{129,65},{192,256},{193,1... | collective-permute-start | bytes 884744 | tf_op jit(solution)/shard_map/ppermute | solution.py:35
  37.0 4.2 %collective-permute-start.4 = (bf16[128,1152]{1,0:T(8,128)(2,1)}, bf16[128,1152]{1,0:T(8,128)(2,1)S(1)}, u32[]{:S(2)}, u32[]{:S(2)}) collective-permute-start(bf16[128,1152]{1,0:T(8,128)(2,1)} %collective-permute-done.2), channel_id=1, source_target_pairs={{0,448},{1,65},{64,0},{65,129},{128,64},{129,193},{192,128},{193,2... | collective-permute-start | bytes 884744 | tf_op jit(solution)/shard_map/ppermute | solution.py:35
  41.3 1.7 %slice_dynamic-update-slice_fusion.11 = (bf16[448,1152]{1,0:T(8,128)(2,1)S(1)}, bf16[512,1152]{1,0:T(8,128)(2,1)}) fusion(bf16[448,1152]{1,0:T(8,128)(2,1)S(1)} %get-tuple-element.36, bf16[128,1152]{1,0:T(8,128)(2,1)} %collective-permute-done.1, bf16[512,1152]{1,0:T(8,128)(2,1)} %get-tuple-element.37), kind=kLoop, calls=%fused_computation.90 | loop fusion | bytes 589824
  44.6 4.2 %collective-permute-start.5 = (bf16[128,1152]{1,0:T(8,128)(2,1)S(1)}, bf16[128,1152]{1,0:T(8,128)(2,1)S(1)}, u32[]{:S(2)}, u32[]{:S(2)}) collective-permute-start(bf16[128,1152]{1,0:T(8,128)(2,1)S(1)} %collective-permute-done.3), channel_id=1, source_target_pairs={{0,64},{1,449},{64,128},{65,1},{128,192},{129,65},{192,256},{193,1... | collective-permute-start | bytes 884744 | tf_op jit(solution)/shard_map/ppermute | solution.py:35
  48.8 2.9 %collective-permute-start.6 = (bf16[128,1152]{1,0:T(8,128)(2,1)S(1)}, bf16[128,1152]{1,0:T(8,128)(2,1)S(1)}, u32[]{:S(2)}, u32[]{:S(2)}) collective-permute-start(bf16[128,1152]{1,0:T(8,128)(2,1)S(1)} %collective-permute-done.4), channel_id=1, source_target_pairs={{0,448},{1,65},{64,0},{65,129},{128,64},{129,193},{192,128},{193,2... | collective-permute-start | bytes 884744 | tf_op jit(solution)/shard_map/ppermute | solution.py:35
  53.0 6.9 %collective-permute-done.7 = bf16[256,1152]{0,1:T(8,128)(2,1)S(1)} collective-permute-done((bf16[256,1152]{0,1:T(8,128)(2,1)}, bf16[256,1152]{0,1:T(8,128)(2,1)S(1)}, u32[]{:S(2)}, u32[]{:S(2)}) %collective-permute-start.7) | collective-permute-done | bytes 589856 | tf_op jit(solution)/shard_map/ppermute | solution.py:15
  60.0 1.9 %collective-permute-start.8 = (bf16[256,1152]{0,1:T(8,128)(2,1)S(1)}, bf16[256,1152]{0,1:T(8,128)(2,1)S(1)}, u32[]{:S(2)}, u32[]{:S(2)}) collective-permute-start(bf16[256,1152]{0,1:T(8,128)(2,1)S(1)} %collective-permute-done.7), channel_id=1, source_target_pairs={{0,1},{1,0},{2,3},{3,2},{4,5},{5,4},{6,7},{7,6},{8,9},{9,8},{10,11... | collective-permute-start | bytes 1769480 | tf_op jit(solution)/shard_map/ppermute | solution.py:15
  61.9 4.9 %collective-permute-start.9 = (bf16[128,1152]{1,0:T(8,128)(2,1)S(1)}, bf16[128,1152]{1,0:T(8,128)(2,1)S(1)}, u32[]{:S(2)}, u32[]{:S(2)}) collective-permute-start(bf16[128,1152]{1,0:T(8,128)(2,1)S(1)} %collective-permute-done.6), channel_id=1, source_target_pairs={{0,448},{1,65},{64,0},{65,129},{128,64},{129,193},{192,128},{193,2... | collective-permute-start | bytes 884744 | tf_op jit(solution)/shard_map/ppermute | solution.py:35
  69.1 2.1 %fusion.20 = bf16[448,1024]{1,0:T(8,128)(2,1)S(1)} fusion(f32[1024]{0:T(1024)S(1)} %add_rsqrt_fusion.1, f32[]{:T(128)} %bitcast.28, f32[]{:T(128)} %bitcast.26, s32[448]{0:T(512)S(1)} %iota_add_fusion, f32[]{:T(128)S(6)} %neg.12, pred[448]{0:T(512)(128)(4,1)S(1)} %iota_compare_fusion.1, bf16[448,1152]{1,0:T(8,128)(2,1)S(1)} %get-tuple-element.24, ...), kind=kOutput, calls=%fused_computation.35 | convolution fusion | flops 1073913856 | bytes 4317132 | tf_op jit(solution)/shard_map/dot_general | solution.py:109
  77.8 2.1 %collective-permute-start.10 = (bf16[8,72,1024]{2,1,0:T(8,128)(2,1)S(1)}, bf16[8,72,1024]{2,1,0:T(8,128)(2,1)S(1)}, u32[]{:S(2)}, u32[]{:S(2)}) collective-permute-start(bf16[8,72,1024]{2,1,0:T(8,128)(2,1)S(1)} %dynamic-slice_bitcast_fusion.1), channel_id=1, source_target_pairs={{0,1},{1,0},{2,3},{3,2},{4,5},{5,4},{6,7},{7,6},{8,9},{9,8},{10,11... | collective-permute-start | bytes 3538952 | tf_op jit(solution)/shard_map/ppermute | solution.py:15
  84.1 4.8 %all-to-all-start = ((bf16[8,72,1024]{2,1,0:T(8,128)(2,1)}), bf16[8,72,1024]{2,1,0:T(8,128)(2,1)}, u32[]{:S(2)}, u32[]{:S(2)}) async-start(bf16[8,72,1024]{2,1,0:T(8,128)(2,1)} %fusion.13), calls=%async_computation | async-start | bytes 2359296 | tf_op jit(solution)/shard_map/all_to_all | solution.py:74
  89.5 3.0 %convolution_convert_fusion = bf16[1152,1152]{1,0:T(8,128)(2,1)S(1)} fusion(bf16[512,1152]{1,0:T(8,128)(2,1)} %constant_dynamic-update-slice_fusion.2, bf16[64,1152]{1,0:T(8,128)(2,1)S(1)} %fusion.70, bf16[448,1152]{1,0:T(8,128)(2,1)S(1)} %fusion.17), kind=kOutput, calls=%fused_computation | convolution fusion | flops 1362640896 | bytes 5013504 | tf_op jit(solution)/shard_map/dot_general | solution.py:147
  92.6 1.9 %collective-permute-start.12 = (bf16[8,72,1152]{2,1,0:T(8,128)(2,1)S(1)}, bf16[8,72,1152]{2,1,0:T(8,128)(2,1)S(1)}, u32[]{:S(2)}, u32[]{:S(2)}) collective-permute-start(bf16[8,72,1152]{2,1,0:T(8,128)(2,1)S(1)} %dynamic-slice_bitcast_fusion), channel_id=1, source_target_pairs={{0,1},{1,0},{2,3},{3,2},{4,5},{5,4},{6,7},{7,6},{8,9},{9,8},{10,11... | collective-permute-start | bytes 3981320 | tf_op jit(solution)/shard_map/ppermute | solution.py:15
  94.5 3.0 %collective-permute-done.12 = bf16[8,72,1152]{2,1,0:T(8,128)(2,1)S(1)} collective-permute-done((bf16[8,72,1152]{2,1,0:T(8,128)(2,1)S(1)}, bf16[8,72,1152]{2,1,0:T(8,128)(2,1)S(1)}, u32[]{:S(2)}, u32[]{:S(2)}) %collective-permute-start.12) | collective-permute-done | bytes 1327136 | tf_op jit(solution)/shard_map/ppermute | solution.py:15
  99.0 5.3 %all-to-all-done = bf16[8,72,1024]{2,1,0:T(8,128)(2,1)} async-done(((bf16[8,72,1024]{2,1,0:T(8,128)(2,1)}), bf16[8,72,1024]{2,1,0:T(8,128)(2,1)}, u32[]{:S(2)}, u32[]{:S(2)}) %all-to-all-start) | async-done | bytes 1179680 | tf_op jit(solution)/shard_map/all_to_all | solution.py:74
  104.3 4.9 %all-to-all-start.1 = ((bf16[8,72,1152]{2,1,0:T(8,128)(2,1)}), bf16[8,72,1152]{2,1,0:T(8,128)(2,1)S(1)}, u32[]{:S(2)}, u32[]{:S(2)}) async-start(bf16[8,72,1152]{2,1,0:T(8,128)(2,1)} %fusion.9), calls=%async_computation.1 | async-start | bytes 2654208 | tf_op jit(solution)/shard_map/all_to_all | solution.py:74
  110.7 4.3 %collective-permute-start.11 = (bf16[72,512]{1,0:T(8,128)(2,1)S(1)}, bf16[72,512]{1,0:T(8,128)(2,1)S(1)}, u32[]{:S(2)}, u32[]{:S(2)}) collective-permute-start(bf16[72,512]{1,0:T(8,128)(2,1)S(1)} %slice.165), channel_id=1, source_target_pairs={{0,16},{16,0},{1,17},{17,1},{2,18},{18,2},{3,19},{19,3},{4,20},{20... | collective-permute-start | bytes 221192 | tf_op jit(solution)/shard_map/ppermute | solution.py:15
  115.1 10.3 %collective-permute-done.11 = bf16[72,512]{1,0:T(8,128)(2,1)S(1)} collective-permute-done((bf16[72,512]{1,0:T(8,128)(2,1)S(1)}, bf16[72,512]{1,0:T(8,128)(2,1)S(1)}, u32[]{:S(2)}, u32[]{:S(2)}) %collective-permute-start.11) | collective-permute-done | bytes 73760 | tf_op jit(solution)/shard_map/ppermute | solution.py:15
  128.4 24.5 %all_to_all.15 = bf16[32,41,128]{2,1,0:T(8,128)(2,1)S(1)} all-to-all(bf16[32,41,128]{2,1,0:T(8,128)(2,1)S(1)} %pad_maximum_fusion.1), channel_id=1, replica_groups=mesh['y'=8,'a'=2,'b'=2,'zl'=2,'x'=4,'c'=2] {'y','a','b'}, dimensions={0} | all-to-all | bytes 671744 | tf_op jit(solution)/shard_map/all_to_all | solution.py:85
  (73 shorter events, 31.4 us)
Async XLA Ops:
  0.6 124.7 %copy-start = (bf16[512,1152]{1,0:T(8,128)(2,1)S(1)}, bf16[512,1152]{1,0:T(8,128)(2,1)}, u32[]{:S(2)}) copy-start(bf16[512,1152]{1,0:T(8,128)(2,1)} %param.8) | copy-start | bytes 3538948
  2.5 18.0 %collective-permute-start = (bf16[64,1152]{1,0:T(8,128)(2,1)S(1)}, bf16[64,1152]{1,0:T(8,128)(2,1)}, u32[]{:S(2)}, u32[]{:S(2)}) collective-permute-start(bf16[64,1152]{1,0:T(8,128)(2,1)S(1)} %pad_maximum_fusion.3), channel_id=1, source_target_pairs={{0,56},{8,48},{16,40},{24,32},{32,24},{40,16},{48,8},{56,0},{1,57}... | collective-permute-start | bytes 442376 | tf_op jit(solution)/shard_map/ppermute | solution.py:45
  23.6 10.6 %collective-permute-start.1 = (bf16[128,1152]{1,0:T(8,128)(2,1)}, bf16[128,1152]{1,0:T(8,128)(2,1)}, u32[]{:S(2)}, u32[]{:S(2)}) collective-permute-start(bf16[128,1152]{1,0:T(8,128)(2,1)} %pad_maximum_fusion.2), channel_id=1, source_target_pairs={{0,64},{1,449},{64,128},{65,1},{128,192},{129,65},{192,256},{193,1... | collective-permute-start | bytes 884744 | tf_op jit(solution)/shard_map/ppermute | solution.py:35
  27.0 10.0 %collective-permute-start.2 = (bf16[128,1152]{1,0:T(8,128)(2,1)}, bf16[128,1152]{1,0:T(8,128)(2,1)}, u32[]{:S(2)}, u32[]{:S(2)}) collective-permute-start(bf16[128,1152]{1,0:T(8,128)(2,1)} %pad_maximum_fusion.2), channel_id=1, source_target_pairs={{0,448},{1,65},{64,0},{65,129},{128,64},{129,193},{192,128},{193,2... | collective-permute-start | bytes 884744 | tf_op jit(solution)/shard_map/ppermute | solution.py:35
  32.2 27.8 %collective-permute-start.7 = (bf16[256,1152]{0,1:T(8,128)(2,1)}, bf16[256,1152]{0,1:T(8,128)(2,1)S(1)}, u32[]{:S(2)}, u32[]{:S(2)}) collective-permute-start(bf16[256,1152]{0,1:T(8,128)(2,1)} %constant_dynamic-slice_fusion), channel_id=1, source_target_pairs={{0,16},{16,0},{1,17},{17,1},{2,18},{18,2},{3,19},{19,3},{4,20},{20... | collective-permute-start | bytes 1769480 | tf_op jit(solution)/shard_map/ppermute | solution.py:15
  34.1 10.5 %collective-permute-start.3 = (bf16[128,1152]{1,0:T(8,128)(2,1)}, bf16[128,1152]{1,0:T(8,128)(2,1)S(1)}, u32[]{:S(2)}, u32[]{:S(2)}) collective-permute-start(bf16[128,1152]{1,0:T(8,128)(2,1)} %collective-permute-done.1), channel_id=1, source_target_pairs={{0,64},{1,449},{64,128},{65,1},{128,192},{129,65},{192,256},{193,1... | collective-permute-start | bytes 884744 | tf_op jit(solution)/shard_map/ppermute | solution.py:35
  37.0 11.8 %collective-permute-start.4 = (bf16[128,1152]{1,0:T(8,128)(2,1)}, bf16[128,1152]{1,0:T(8,128)(2,1)S(1)}, u32[]{:S(2)}, u32[]{:S(2)}) collective-permute-start(bf16[128,1152]{1,0:T(8,128)(2,1)} %collective-permute-done.2), channel_id=1, source_target_pairs={{0,448},{1,65},{64,0},{65,129},{128,64},{129,193},{192,128},{193,2... | collective-permute-start | bytes 884744 | tf_op jit(solution)/shard_map/ppermute | solution.py:35
  44.6 15.4 %collective-permute-start.5 = (bf16[128,1152]{1,0:T(8,128)(2,1)S(1)}, bf16[128,1152]{1,0:T(8,128)(2,1)S(1)}, u32[]{:S(2)}, u32[]{:S(2)}) collective-permute-start(bf16[128,1152]{1,0:T(8,128)(2,1)S(1)} %collective-permute-done.3), channel_id=1, source_target_pairs={{0,64},{1,449},{64,128},{65,1},{128,192},{129,65},{192,256},{193,1... | collective-permute-start | bytes 884744 | tf_op jit(solution)/shard_map/ppermute | solution.py:35
  48.8 13.1 %collective-permute-start.6 = (bf16[128,1152]{1,0:T(8,128)(2,1)S(1)}, bf16[128,1152]{1,0:T(8,128)(2,1)S(1)}, u32[]{:S(2)}, u32[]{:S(2)}) collective-permute-start(bf16[128,1152]{1,0:T(8,128)(2,1)S(1)} %collective-permute-done.4), channel_id=1, source_target_pairs={{0,448},{1,65},{64,0},{65,129},{128,64},{129,193},{192,128},{193,2... | collective-permute-start | bytes 884744 | tf_op jit(solution)/shard_map/ppermute | solution.py:35
  60.0 8.5 %collective-permute-start.8 = (bf16[256,1152]{0,1:T(8,128)(2,1)S(1)}, bf16[256,1152]{0,1:T(8,128)(2,1)S(1)}, u32[]{:S(2)}, u32[]{:S(2)}) collective-permute-start(bf16[256,1152]{0,1:T(8,128)(2,1)S(1)} %collective-permute-done.7), channel_id=1, source_target_pairs={{0,1},{1,0},{2,3},{3,2},{4,5},{5,4},{6,7},{7,6},{8,9},{9,8},{10,11... | collective-permute-start | bytes 1769480 | tf_op jit(solution)/shard_map/ppermute | solution.py:15
  61.9 11.2 %collective-permute-start.9 = (bf16[128,1152]{1,0:T(8,128)(2,1)S(1)}, bf16[128,1152]{1,0:T(8,128)(2,1)S(1)}, u32[]{:S(2)}, u32[]{:S(2)}) collective-permute-start(bf16[128,1152]{1,0:T(8,128)(2,1)S(1)} %collective-permute-done.6), channel_id=1, source_target_pairs={{0,448},{1,65},{64,0},{65,129},{128,64},{129,193},{192,128},{193,2... | collective-permute-start | bytes 884744 | tf_op jit(solution)/shard_map/ppermute | solution.py:35
  73.2 6.9 %copy-start.1 = (bf16[128,1152]{1,0:T(8,128)(2,1)}, bf16[128,1152]{1,0:T(8,128)(2,1)S(1)}, u32[]{:S(2)}) copy-start(bf16[128,1152]{1,0:T(8,128)(2,1)S(1)} %collective-permute-done.9) | copy-start | bytes 884740
  77.8 4.7 %collective-permute-start.10 = (bf16[8,72,1024]{2,1,0:T(8,128)(2,1)S(1)}, bf16[8,72,1024]{2,1,0:T(8,128)(2,1)S(1)}, u32[]{:S(2)}, u32[]{:S(2)}) collective-permute-start(bf16[8,72,1024]{2,1,0:T(8,128)(2,1)S(1)} %dynamic-slice_bitcast_fusion.1), channel_id=1, source_target_pairs={{0,1},{1,0},{2,3},{3,2},{4,5},{5,4},{6,7},{7,6},{8,9},{9,8},{10,11... | collective-permute-start | bytes 3538952 | tf_op jit(solution)/shard_map/ppermute | solution.py:15
  82.1 6.7 %slice-start = ((bf16[128,1152]{1,0:T(8,128)(2,1)}), bf16[64,1152]{1,0:T(8,128)(2,1)S(1)}, s32[]{:S(2)}) async-start(bf16[128,1152]{1,0:T(8,128)(2,1)} %copy-done.1), calls=%async_computation.3 | async-start | bytes 294912 | tf_op jit(solution)/shard_map/slice | solution.py:145
  84.1 20.2 %all-to-all-start = ((bf16[8,72,1024]{2,1,0:T(8,128)(2,1)}), bf16[8,72,1024]{2,1,0:T(8,128)(2,1)}, u32[]{:S(2)}, u32[]{:S(2)}) async-start(bf16[8,72,1024]{2,1,0:T(8,128)(2,1)} %fusion.13), calls=%async_computation | async-start | bytes 2359296 | tf_op jit(solution)/shard_map/all_to_all | solution.py:74
  92.6 5.0 %collective-permute-start.12 = (bf16[8,72,1152]{2,1,0:T(8,128)(2,1)S(1)}, bf16[8,72,1152]{2,1,0:T(8,128)(2,1)S(1)}, u32[]{:S(2)}, u32[]{:S(2)}) collective-permute-start(bf16[8,72,1152]{2,1,0:T(8,128)(2,1)S(1)} %dynamic-slice_bitcast_fusion), channel_id=1, source_target_pairs={{0,1},{1,0},{2,3},{3,2},{4,5},{5,4},{6,7},{7,6},{8,9},{9,8},{10,11... | collective-permute-start | bytes 3981320 | tf_op jit(solution)/shard_map/ppermute | solution.py:15
  104.3 23.1 %all-to-all-start.1 = ((bf16[8,72,1152]{2,1,0:T(8,128)(2,1)}), bf16[8,72,1152]{2,1,0:T(8,128)(2,1)S(1)}, u32[]{:S(2)}, u32[]{:S(2)}) async-start(bf16[8,72,1152]{2,1,0:T(8,128)(2,1)} %fusion.9), calls=%async_computation.1 | async-start | bytes 2654208 | tf_op jit(solution)/shard_map/all_to_all | solution.py:74
  110.7 14.6 %collective-permute-start.11 = (bf16[72,512]{1,0:T(8,128)(2,1)S(1)}, bf16[72,512]{1,0:T(8,128)(2,1)S(1)}, u32[]{:S(2)}, u32[]{:S(2)}) collective-permute-start(bf16[72,512]{1,0:T(8,128)(2,1)S(1)} %slice.165), channel_id=1, source_target_pairs={{0,16},{16,0},{1,17},{17,1},{2,18},{18,2},{3,19},{19,3},{4,20},{20... | collective-permute-start | bytes 221192 | tf_op jit(solution)/shard_map/ppermute | solution.py:15
